TPU v7x, 32 devices: a whole 2x2x4 slice. The times are simulated.
32 devices in a mesh: dp: 8 (over z, y), state: 4 (over x, core).
Axes of the slice: x: 2, y: 2, z: 4, core: 2. Of those that a mesh axis runs over, the one named last changes fastest.
Arguments:
- token_ids: int32 [8, 1024], P('dp'), may hold values from 0 to 31999
- doc_starts: int32 [8, 4], P('dp'), may hold values from 0 to 1023, as said below
- loss_positions: int32 [8, 128], P('dp'), may hold values from 0 to 1023
- loss_targets: int32 [8, 128], P('dp'), may hold values from -1 to 31999, as said below
- owners: int32 [32], replicated, may hold values from 0 to 7, as said below
- in_weight: float32 [4, 40, 64, 4352], P('state', 'dp'), may hold values from -0.125 to 0.125
- out_weight: float32 [4, 40, 64, 1920], P('state', 'dp'), may hold values from -0.125 to 0.125
- table_weight: float32 [4, 40, 64, 8000], P('state', 'dp')
- gain_weight: float32 [40, 4, 64], P('dp'), may hold values from 0.5 to 1.5
- in_first: float32 [4, 40, 64, 4352], P('state', 'dp'), may hold values from -2.670288e-05 to 2.670288e-05
- out_first: float32 [4, 40, 64, 1920], P('state', 'dp'), may hold values from -2.670288e-05 to 2.670288e-05
- table_first: float32 [4, 40, 64, 8000], P('state', 'dp'), may hold values from -2.670288e-05 to 2.670288e-05
- gain_first: float32 [40, 4, 64], P('dp'), may hold values from -0.00024414062 to 0.00024414062
- in_second: float32 [4, 40, 64, 4352], P('state', 'dp'), may hold values from 1.7105067e-12 to 2.7368108e-11
- out_second: float32 [4, 40, 64, 1920], P('state', 'dp'), may hold values from 1.7105067e-12 to 2.7368108e-11
- table_second: float32 [4, 40, 64, 8000], P('state', 'dp'), may hold values from 1.7105067e-12 to 2.7368108e-11
- gain_second: float32 [40, 4, 64], P('dp'), may hold values from 1.7105067e-10 to 2.7368108e-09
- in_average: float32 [4, 40, 64, 4352], P('state', 'dp'), may hold values from -0.125 to 0.125
- out_average: float32 [4, 40, 64, 1920], P('state', 'dp'), may hold values from -0.125 to 0.125
- table_average: float32 [4, 40, 64, 8000], P('state', 'dp'), may hold values from -0.125 to 0.125
- gain_average: float32 [40, 4, 64], P('dp'), may hold values from 0.5 to 1.5
Outputs:
- in_weight_new: float32 [4, 40, 64, 4352], P('state', 'dp')
- out_weight_new: float32 [4, 40, 64, 1920], P('state', 'dp')
- table_weight_new: float32 [4, 40, 64, 8000], P('state', 'dp')
- gain_weight_new: float32 [40, 4, 64], P('dp')
- in_first_new: float32 [4, 40, 64, 4352], P('state', 'dp')
- out_first_new: float32 [4, 40, 64, 1920], P('state', 'dp')
- table_first_new: float32 [4, 40, 64, 8000], P('state', 'dp')
- gain_first_new: float32 [40, 4, 64], P('dp')
- in_second_new: float32 [4, 40, 64, 4352], P('state', 'dp')
- out_second_new: float32 [4, 40, 64, 1920], P('state', 'dp')
- table_second_new: float32 [4, 40, 64, 8000], P('state', 'dp')
- gain_second_new: float32 [40, 4, 64], P('dp')
- in_average_new: float32 [4, 40, 64, 4352], P('state', 'dp')
- out_average_new: float32 [4, 40, 64, 1920], P('state', 'dp')
- table_average_new: float32 [4, 40, 64, 8000], P('state', 'dp')
- gain_average_new: float32 [40, 4, 64], P('dp')
- loss_sum: float32 [], replicated
- token_count: float32 [], replicated
- grad_norm: float32 [], replicated
Inputs may be any that keep to these rules, and one draw needn't show every extreme that they name: `owners`: every index of dp owns between 3 and 5 blocks, and some index owns exactly 5. `doc_starts`: each row's first start is 0 and the starts rise strictly. `loss_targets`: between one and all of a row's slots count; in the last row all count.
All inputs are finite; a program needn't handle non-finite values.
Results may differ from a plain program's by a relative error of at most 0.0173.
Values may be sent and summed in bfloat16 or wider, within the bound.
A program may use at most 640 MiB of HBM per device.

v0:
```python
import jax
import jax.numpy as jnp
from jax import lax
from jax.sharding import PartitionSpec as P

HEADS = 16
KEY_DIM = 128
GROUP = 128
STEP = 5
VAL_DIM = 128


NORM_EPS = 1e-06
LOWER_BOUND = 0.9
CLIP_NORM = 0.02
BETA_FIRST = 0.5
BETA_SECOND = 0.5
ADAM_EPS = 1e-08
LEARN_RATE = 0.02
GAIN_RATE = 0.2
WEIGHT_DECAY = 0.1
AVERAGE_DECAY = 0.9
FULL_PRECISION = lax.Precision.HIGHEST


def rms_norm(values, gain):
    return values * lax.rsqrt(jnp.mean(values * values, axis=-1, keepdims=True) + NORM_EPS) * gain


def forget_gates(query_pre, forget_pre):
    query = jax.nn.silu(query_pre)
    key_gate = (1.0 - LOWER_BOUND) * jax.nn.sigmoid(-forget_pre)
    log_forget = jnp.log(LOWER_BOUND + (1.0 - LOWER_BOUND) * jax.nn.sigmoid(forget_pre))
    return (query, key_gate, log_forget)


def mixer(query, key_gate, log_forget, values, documents, block):
    blocks = query.shape[0] // block
    heads = query.shape[1]
    key_width = query.shape[2]
    value_width = values.shape[2]

    def split(array):
        return array.reshape((blocks, block) + array.shape[1:])

    causal = jnp.arange(block)[:, None] >= jnp.arange(block)[None, :]

    def advance(carry, inputs):
        running_state, previous = carry
        query_blk, key_blk, forget_blk, value_block, doc_blk = inputs
        cumulative = jnp.cumsum(forget_blk, axis=0)
        decayed_query = query_blk * jnp.exp(cumulative)
        key_decay = key_blk * jnp.exp(-cumulative)
        allowed = causal & (doc_blk[:, None] == doc_blk[None, :])
        scores = jnp.einsum("thk,shk->hts", decayed_query, key_decay, precision=FULL_PRECISION)
        scores = jnp.where(allowed[None], scores, 0.0)
        inner = jnp.einsum("hts,shv->thv", scores, value_block, precision=FULL_PRECISION)
        carried_state = (doc_blk == previous).astype(jnp.float32)
        outer_product = (
            jnp.einsum("uwc,wcx->uwx", decayed_query, running_state, precision=FULL_PRECISION)
            * carried_state[:, None, None]
        )
        total_amount = cumulative[-1]
        last_doc = doc_blk[-1]
        keep_factor = (last_doc == previous).astype(jnp.float32)
        same_last = (doc_blk == last_doc).astype(jnp.float32)
        weight_blocks = (
            key_blk * jnp.exp(total_amount[None] - cumulative) * same_last[:, None, None]
        )
        running_state = jnp.exp(total_amount)[
            :, :, None
        ] * running_state * keep_factor + jnp.einsum(
            "ayd,aye->yde", weight_blocks, value_block, precision=FULL_PRECISION
        )
        return ((running_state, last_doc), inner + outer_product)

    start = (jnp.zeros((heads, key_width, value_width), jnp.float32), jnp.array(-1, jnp.int32))
    _, output = lax.scan(
        jax.checkpoint(advance),
        start,
        (split(query), split(key_gate), split(log_forget), split(values), split(documents)),
    )
    return output.reshape(query.shape[0], heads, value_width)


def slot_index(owners, capacity):
    order = jnp.arange(owners.shape[0])
    earlier = (owners[:, None] == owners[None, :]) & (order[None, :] < order[:, None])
    ranks = jnp.sum(earlier.astype(jnp.int32), axis=1)
    return owners * capacity + ranks


def document_ids(starts, length):
    return jnp.sum((jnp.arange(length)[:, None] >= starts[None, :]).astype(jnp.int32), axis=1) - 1


def adam_update(weight, first, second, average, grad, scale, rate, decay, occupied):
    clipped = scale * grad
    first_new = BETA_FIRST * first + (1.0 - BETA_FIRST) * clipped
    second_new = BETA_SECOND * second + (1.0 - BETA_SECOND) * clipped * clipped
    first_hat = first_new / (1.0 - BETA_FIRST**STEP)
    second_hat = second_new / (1.0 - BETA_SECOND**STEP)
    weight_new = weight - rate * (first_hat / (jnp.sqrt(second_hat) + ADAM_EPS) + decay * weight)
    average_new = AVERAGE_DECAY * average + (1.0 - AVERAGE_DECAY) * weight_new
    return (
        weight_new * occupied,
        first_new * occupied,
        second_new * occupied,
        average_new * occupied,
    )


def times_plain(left, right):
    return jnp.dot(left, right, preferred_element_type=jnp.float32)


def times_right(left, right):
    return lax.dot_general(
        left, right, (((1,), (1,)), ((), ())), preferred_element_type=jnp.float32
    )


def times_left(left, right):
    return lax.dot_general(
        left, right, (((0,), (0,)), ((), ())), preferred_element_type=jnp.float32
    )


def token_rows(values):
    return lax.all_gather(values, "state", axis=0, tiled=True)


def token_sums(values):
    return lax.psum_scatter(values, "state", scatter_dimension=0, tiled=True)


def value_cols(values):
    return lax.all_gather(values, "state", axis=1, tiled=True)


def value_sums(values):
    return lax.psum_scatter(values, "state", scatter_dimension=1, tiled=True)


def swiglu(joined):
    half_width = joined.shape[1] // 2
    return jax.nn.silu(joined[:, :half_width]) * joined[:, half_width:]


def on_device(
    token_ids,
    doc_starts,
    loss_positions,
    loss_targets,
    owners,
    in_weight,
    out_weight,
    table_weight,
    gain_weight,
    in_first,
    out_first,
    table_first,
    gain_first,
    in_second,
    out_second,
    table_second,
    gain_second,
    in_average,
    out_average,
    table_average,
    gain_average,
):
    f32 = jnp.float32
    bf16 = jnp.bfloat16
    shares = lax.axis_size("state")
    my_share = lax.axis_index("state")
    seq_len = token_ids.shape[1]
    capacity = in_weight.shape[1]
    block_rows = in_weight.shape[2]
    block_count = owners.shape[0]
    width = block_rows * block_count
    key_share = KEY_DIM // shares
    head_share = HEADS // shares
    key_cols = HEADS * key_share
    value_width = head_share * VAL_DIM
    vocab_share = table_weight.shape[3]
    mixer_cols = 2 * key_cols + value_width
    index = slot_index(owners, capacity)
    lowered = (
        in_weight[0].astype(bf16),
        out_weight[0].astype(bf16),
        table_weight[0].astype(bf16),
        gain_weight.astype(bf16),
    )
    full_in, full_out, full_table, full_gain = (
        lax.all_gather(lowered[0], "dp", axis=0, tiled=True),
        lax.all_gather(lowered[1], "dp", axis=0, tiled=True),
        lax.all_gather(lowered[2], "dp", axis=0, tiled=True),
        lax.all_gather(lowered[3], "dp", axis=0, tiled=True),
    )
    w_in = full_in[index].reshape(width, -1)
    w_out = full_out[index].reshape(width, -1)
    table = full_table[index].reshape(width, -1)
    gains = jnp.transpose(full_gain[index], (1, 0, 2)).reshape(4, width).astype(f32)
    targets = loss_targets[0]
    live = (targets >= 0).astype(f32)
    count = lax.psum(jnp.sum(live), "dp")
    ids = token_ids[0]
    vocab_local = ids - my_share * vocab_share
    inside = (vocab_local >= 0) & (vocab_local < vocab_share)
    vocab_safe = jnp.clip(vocab_local, 0, vocab_share - 1)
    looked = jnp.take(table, vocab_safe, axis=1).T.astype(f32)
    stream_zero = token_sums(jnp.where(inside[:, None], looked, 0.0))
    normed_one, back_one = jax.vjp(rms_norm, stream_zero, gains[0])
    rows_one = token_rows(normed_one.astype(bf16))
    projected = times_plain(rows_one, w_in[:, :mixer_cols])
    query_pre = projected[:, :key_cols]
    forget_pre = projected[:, key_cols : 2 * key_cols]
    value_pre = projected[:, 2 * key_cols :]
    (query, key_gate, log_forget), back_gates = jax.vjp(forget_gates, query_pre, forget_pre)
    values_all = value_cols(value_pre.astype(bf16))
    documents = document_ids(doc_starts[0], seq_len)

    def mix(query_in, key_in, forget_in, value_in):
        result = mixer(
            query_in.reshape(seq_len, HEADS, key_share),
            key_in.reshape(seq_len, HEADS, key_share),
            forget_in.reshape(seq_len, HEADS, key_share),
            value_in.reshape(seq_len, HEADS, VAL_DIM),
            documents,
            GROUP,
        )
        return result.reshape(seq_len, width)

    mixed_part, back_mix = jax.vjp(
        mix,
        query.astype(bf16).astype(f32),
        key_gate.astype(bf16).astype(f32),
        log_forget,
        values_all.astype(f32),
    )
    mixed_mine = value_sums(mixed_part)
    gain_mine = lax.dynamic_slice_in_dim(gains[1], my_share * value_width, value_width)

    def head_norm(mixed_in, gain_in):
        return rms_norm(
            mixed_in.reshape(seq_len, head_share, VAL_DIM), gain_in.reshape(head_share, VAL_DIM)
        ).reshape(seq_len, value_width)

    gated_f, back_head = jax.vjp(head_norm, mixed_mine, gain_mine)
    gated = gated_f.astype(bf16)
    stream_one = stream_zero + token_sums(times_right(gated, w_out[:, :value_width]))
    normed_two, back_two = jax.vjp(rms_norm, stream_one, gains[2])
    rows_two = token_rows(normed_two.astype(bf16))
    gate_up = times_plain(rows_two, w_in[:, mixer_cols:])
    hidden_f, back_glu = jax.vjp(swiglu, gate_up)
    hidden = hidden_f.astype(bf16)
    stream_two = stream_one + token_sums(times_right(hidden, w_out[:, value_width:]))
    normed_three, back_three = jax.vjp(rms_norm, stream_two, gains[3])
    final_rows = normed_three.astype(bf16)
    positions = loss_positions[0]
    picked_rows = token_rows(final_rows)[positions]
    logits = times_plain(picked_rows, table)
    target_local = targets - my_share * vocab_share
    target_hit = jnp.arange(vocab_share)[None, :] == target_local[:, None]
    top_local = jnp.max(logits, axis=1)
    top_all = lax.pmax(top_local, "state")
    sum_all, picked_all = lax.psum(
        (
            jnp.sum(jnp.exp(logits - top_all[:, None]), axis=1),
            jnp.sum(jnp.where(target_hit, logits, 0.0), axis=1),
        ),
        "state",
    )
    lse = top_all + jnp.log(sum_all)
    loss_part = jnp.sum((lse - picked_all) * live)
    probs = jnp.exp(logits - lse[:, None])
    dlogits = ((probs - target_hit.astype(f32)) * (live / count)[:, None]).astype(bf16)
    grad_rows = times_right(dlogits, table)
    grad_table = times_left(picked_rows, dlogits)
    grad_final = token_sums(jnp.zeros((seq_len, width), f32).at[positions].add(grad_rows))
    grad_two, grad_gain_four = back_three(grad_final)
    down_rows = token_rows(grad_two.astype(bf16))
    grad_hidden = times_plain(down_rows, w_out[:, value_width:])
    grad_down = times_left(down_rows, hidden)
    (grad_gate_up,) = back_glu(grad_hidden)
    grad_gate_up = grad_gate_up.astype(bf16)
    grad_gu_weight = times_left(rows_two, grad_gate_up)
    grad_norm_two = token_sums(times_right(grad_gate_up, w_in[:, mixer_cols:]))
    grad_stream_one, grad_gain_three = back_two(grad_norm_two)
    grad_one = grad_two + grad_stream_one
    branch_rows = token_rows(grad_one.astype(bf16))
    grad_gated = times_plain(branch_rows, w_out[:, :value_width])
    grad_output = times_left(branch_rows, gated)
    grad_mixed_mine, grad_gain_two = back_head(grad_gated)
    grad_mixed_all = value_cols(grad_mixed_mine.astype(bf16))
    grad_query, grad_key, grad_forget, grad_values_part = back_mix(grad_mixed_all.astype(f32))
    grad_value_pre = value_sums(grad_values_part)
    grad_query_pre, grad_forget_pre = back_gates((grad_query, grad_key, grad_forget))
    grad_projected = jnp.concatenate(
        [grad_query_pre, grad_forget_pre, grad_value_pre], axis=1
    ).astype(bf16)
    grad_mixer_weight = times_left(rows_one, grad_projected)
    grad_norm_one = token_sums(times_right(grad_projected, w_in[:, :mixer_cols]))
    grad_stream_zero, grad_gain_one = back_one(grad_norm_one)
    grad_zero = grad_one + grad_stream_zero
    embed_rows = token_rows(grad_zero.astype(bf16)).astype(f32)
    grad_lookup = jax.ops.segment_sum(
        jnp.where(inside[:, None], embed_rows, 0.0), vocab_safe, num_segments=vocab_share
    )
    grad_table = grad_table + grad_lookup.T
    gain_two_full = lax.dynamic_update_slice_in_dim(
        jnp.zeros((width,), f32), grad_gain_two, my_share * value_width, 0
    )
    grad_gains = lax.psum(
        jnp.stack([grad_gain_one, gain_two_full, grad_gain_three, grad_gain_four]).astype(
            jnp.bfloat16
        ),
        "state",
    ).astype(jnp.float32)
    grad_in_whole = jnp.concatenate([grad_mixer_weight, grad_gu_weight], axis=1)
    grad_out_whole = jnp.concatenate([grad_output, grad_down], axis=1)
    slot_total = lax.axis_size("dp") * capacity

    def to_slots(grad):
        blocks = grad.reshape(block_count, block_rows, grad.shape[1])
        return jnp.zeros((slot_total, block_rows, grad.shape[1]), f32).at[index].set(blocks)

    gain_slots = (
        jnp.zeros((slot_total, 4, block_rows), f32)
        .at[index]
        .set(grad_gains.reshape(4, block_count, block_rows).transpose(1, 0, 2))
    )
    own_in, own_out, own_table, own_gain = (
        lax.psum_scatter(to_slots(grad_in_whole), "dp", scatter_dimension=0, tiled=True),
        lax.psum_scatter(to_slots(grad_out_whole), "dp", scatter_dimension=0, tiled=True),
        lax.psum_scatter(to_slots(grad_table), "dp", scatter_dimension=0, tiled=True),
        lax.psum_scatter(gain_slots, "dp", scatter_dimension=0, tiled=True),
    )
    first_share = (my_share == 0).astype(f32)
    squares = (
        jnp.sum(own_in * own_in)
        + jnp.sum(own_out * own_out)
        + jnp.sum(own_table * own_table)
        + first_share * jnp.sum(own_gain * own_gain)
    )
    squares_all, loss_sum = lax.psum((squares, first_share * loss_part), ("dp", "state"))
    grad_norm = jnp.sqrt(squares_all)
    scale = jnp.minimum(1.0, CLIP_NORM / (grad_norm + 1e-06))
    held = jnp.sum((owners == lax.axis_index("dp")).astype(jnp.int32))
    occupied = (jnp.arange(capacity) < held).astype(f32)
    wide_occ = occupied[None, :, None, None]
    new_in = adam_update(
        in_weight,
        in_first,
        in_second,
        in_average,
        own_in[None],
        scale,
        LEARN_RATE,
        WEIGHT_DECAY,
        wide_occ,
    )
    new_out = adam_update(
        out_weight,
        out_first,
        out_second,
        out_average,
        own_out[None],
        scale,
        LEARN_RATE,
        WEIGHT_DECAY,
        wide_occ,
    )
    new_table = adam_update(
        table_weight,
        table_first,
        table_second,
        table_average,
        own_table[None],
        scale,
        LEARN_RATE,
        WEIGHT_DECAY,
        wide_occ,
    )
    new_gain = adam_update(
        gain_weight,
        gain_first,
        gain_second,
        gain_average,
        own_gain,
        scale,
        GAIN_RATE,
        0.0,
        occupied[:, None, None],
    )
    return (
        new_in[0],
        new_out[0],
        new_table[0],
        new_gain[0],
        new_in[1],
        new_out[1],
        new_table[1],
        new_gain[1],
        new_in[2],
        new_out[2],
        new_table[2],
        new_gain[2],
        new_in[3],
        new_out[3],
        new_table[3],
        new_gain[3],
        loss_sum,
        count,
        grad_norm,
    )


def solution(mesh):
    return jax.shard_map(
        on_device,
        mesh=mesh,
        in_specs=(
            P("dp", None),
            P("dp", None),
            P("dp", None),
            P("dp", None),
            P(),
            P("state", "dp", None, None),
            P("state", "dp", None, None),
            P("state", "dp", None, None),
            P("dp", None, None),
            P("state", "dp", None, None),
            P("state", "dp", None, None),
            P("state", "dp", None, None),
            P("dp", None, None),
            P("state", "dp", None, None),
            P("state", "dp", None, None),
            P("state", "dp", None, None),
            P("dp", None, None),
            P("state", "dp", None, None),
            P("state", "dp", None, None),
            P("state", "dp", None, None),
            P("dp", None, None),
        ),
        out_specs=(
            P("state", "dp", None, None),
            P("state", "dp", None, None),
            P("state", "dp", None, None),
            P("dp", None, None),
            P("state", "dp", None, None),
            P("state", "dp", None, None),
            P("state", "dp", None, None),
            P("dp", None, None),
            P("state", "dp", None, None),
            P("state", "dp", None, None),
            P("state", "dp", None, None),
            P("dp", None, None),
            P("state", "dp", None, None),
            P("state", "dp", None, None),
            P("state", "dp", None, None),
            P("dp", None, None),
            P(),
            P(),
            P(),
        ),
        check_vma=False,
    )
```

profile of v0, /device:TPU:0, one launch (start us, length us, event | category | flops | bytes accessed | tf_op | source)
XLA Modules:
  0.0 5916.6 jit_solution(2583918388144453457)
XLA Ops:
  16.8 783.0 %all-gather.31.cloned.1.call-done = bf16[1,40,64,8000]{3,2,0,1:T(8,128)(2,1)} async-done(((bf16[1,5,64,8000]{3,2,0,1:T(8,128)(2,1)}), bf16[1,40,64,8000]{3,2,0,1:T(8,128)(2,1)}) %all-gather.31.cloned.1.call-update) | async-done | bytes 40960016 | tf_op jit(solution)/shard_map/all_gather | solution.py:198
  822.8 42.8 copy.209
  865.6 48.2 gather_fusion.1
  956.4 35.4 reduce-scatter.16.cloned.1.call-done
  996.6 423.9 %all-gather.33.cloned.1.call-done = bf16[1,40,64,4352]{3,2,0,1:T(8,128)(2,1)} async-done(((bf16[1,5,64,4352]{3,2,0,1:T(8,128)(2,1)}), bf16[1,40,64,4352]{3,2,0,1:T(8,128)(2,1)}) %all-gather.33.cloned.1.call-update) | async-done | bytes 22282256 | tf_op jit(solution)/shard_map/all_gather | solution.py:196
  1516.8 403.7 %while.43 = (s32[]{:T(128)}, f32[16,32,128]{2,1,0:T(8,128)}, s32[]{:T(128)}, f32[8,128,16,128]{1,0,3,2:T(8,128)}, f32[8,16,32,128]{3,2,1,0:T(8,128)}, /*index=5*...) while((s32[]{:T(128)}, f32[16,32,128]{2,1,0:T(8,128)}, ...), condition=%wide.region_6.7_spmd.clone, body=%wide.region_4.6_spmd.clone.sunk | while | flops 714588672 | bytes 16040163 | solution.py:78
  1939.4 61.7 %reduce-scatter.18.cloned.1.call-done = f32[1024,512]{0,1:T(8,128)} async-done(((f32[1024,2048]{0,1:T(8,128)}), f32[1024,512]{0,1:T(8,128)}) %reduce-scatter.18.cloned.1.call-update) | async-done | bytes 2097168 | tf_op jit(solution)/shard_map/reduce_scatter | solution.py:142
  2013.3 71.8 %reduce-scatter.20.cloned.1.call-done = f32[256,2048]{1,0:T(8,128)} async-done(((f32[1024,2048]{1,0:T(8,128)}), f32[256,2048]{1,0:T(8,128)}) %reduce-scatter.20.cloned.1.call-update) | async-done | bytes 2097168 | tf_op jit(solution)/shard_map/reduce_scatter | solution.py:134
  2158.2 71.7 %reduce-scatter.22.cloned.1.call-done = f32[256,2048]{1,0:T(8,128)} async-done(((f32[1024,2048]{1,0:T(8,128)}), f32[256,2048]{1,0:T(8,128)}) %reduce-scatter.22.cloned.1.call-update) | async-done | bytes 2097168 | tf_op jit(solution)/shard_map/reduce_scatter | solution.py:134
  2355.2 68.9 %reduce-scatter.24.cloned.1.call-done = f32[256,2048]{1,0:T(8,128)} async-done(((f32[1024,2048]{1,0:T(8,128)}), f32[256,2048]{1,0:T(8,128)}) %reduce-scatter.24.cloned.1.call-update) | async-done | bytes 2097168 | tf_op jit(solution)/shard_map/reduce_scatter | solution.py:134
  2429.1 34.6 all-gather.23.cloned.1.call-done
  2499.8 71.8 %reduce-scatter.26.cloned.1.call-done = f32[256,2048]{1,0:T(8,128)} async-done(((f32[1024,2048]{1,0:T(8,128)}), f32[256,2048]{1,0:T(8,128)}) %reduce-scatter.26.cloned.1.call-update) | async-done | bytes 2097168 | tf_op jit(solution)/shard_map/reduce_scatter | solution.py:134
  2681.1 558.2 %while.44 = (s32[]{:T(128)}, f32[16,32,128]{2,1,0:T(8,128)}, f32[8,128,16,32]{3,2,1,0:T(8,128)}, f32[8,128,16,32]{3,2,1,0:T(8,128)}, f32[8,128,16,32]{3,2,1,0:T(...) while((s32[]{:T(128)}, f32[16,32,128]{2,1,0:T(8,128)}, ...), condition=%wide.region_30.31_spmd.clone, body=%wide.region_25.30_spmd.clone.sunk | while | flops 1530577408 | bytes 63295584 | solution.py:78
  3286.8 35.2 reduce-scatter.28.cloned.1.call-done
  3335.9 71.8 %reduce-scatter.32.cloned.1.call-done = f32[256,2048]{1,0:T(8,128)} async-done(((f32[1024,2048]{1,0:T(8,128)}), f32[256,2048]{1,0:T(8,128)}) %reduce-scatter.32.cloned.1.call-update) | async-done | bytes 2097168 | tf_op jit(solution)/shard_map/reduce_scatter | solution.py:134
  3558.4 62.6 %scatter_fusion = f32[40,64,4352]{2,1,0:T(8,128)} fusion(f32[40,64,4352]{2,1,0:T(8,128)} %broadcast_in_dim.210, s32[32]{0:T(128)S(1)} %copy-done.51, f32[32,64,4352]{2,1,0:T(8,128)} %bitcast.429), kind=kCustom, calls=%fused_computation.7 | custom fusion | bytes 106954880 | tf_op jit(solution)/shard_map/scatter | solution.py:327
  3631.7 60.0 %scatter_custom_fusion.3 = f32[8000,2048]{1,0:T(8,128)} fusion(s32[1024]{0:T(1024)S(1)} %get-tuple-element.657, f32[]{:T(128)} %constant.202.clone.1, f32[1024,2048]{1,0:T(8,128)} %convert_select_fusion.1, s32[1024]{0:T(1024)S(1)} %broadcast_clamp_fusion), kind=kCustom, calls=%fused_computation.118 | custom fusion | flops 2097152 | bytes 65536512 | tf_op jit(solution)/shard_map/scatter-add | solution.py:308
  3691.8 44.3 bitcast_add_fusion.1
  3736.0 64.3 %copy.235 = f32[2048,8000]{1,0:T(8,128)} copy(f32[2048,8000]{0,1:T(8,128)} %bitcast_add_fusion.1) | data formatting | bytes 131072000 | tf_op jit(solution)/shard_map/add | solution.py:311
  3826.8 120.4 %scatter_fusion.2 = f32[40,64,8000]{2,1,0:T(8,128)} fusion(f32[40,64,8000]{2,1,0:T(8,128)} %broadcast_in_dim.223, s32[32]{0:T(128)S(1)} %copy-done.51, f32[32,64,8000]{2,1,0:T(8,128)} %bitcast.428), kind=kCustom, calls=%fused_computation.10 | custom fusion | bytes 196608128 | tf_op jit(solution)/shard_map/scatter | solution.py:327
  3966.1 42.9 all-reduce.5
  4010.2 507.7 %reduce-scatter.34.cloned.1.call-done = f32[5,64,4352]{2,1,0:T(8,128)} async-done(((f32[40,64,4352]{2,1,0:T(8,128)}), f32[5,64,4352]{2,1,0:T(8,128)}) %reduce-scatter.34.cloned.1.call-update) | async-done | bytes 5570576
  4523.8 1267.1 %reduce-scatter.36.cloned.1.call-done = f32[5,64,8000]{2,1,0:T(8,128)} async-done(((f32[40,64,8000]{2,1,0:T(8,128)}), f32[5,64,8000]{2,1,0:T(8,128)}) %reduce-scatter.36.cloned.1.call-update) | async-done | bytes 10240016
  5799.4 39.7 all-reduce.6
  (935 shorter events, 1840.5 us)
Async XLA Ops:
  7.2 792.6 %all-gather.31.cloned.1.call-start = ((), (), s32[]{:S(2)}) async-start(), calls=%async_computation.28 | async-start | bytes 46448640 | tf_op jit(solution)/shard_map/all_gather | solution.py:198
  14.2 977.7 %reduce-scatter.16.cloned.1.call-start = ((), (), s32[]{:S(2)}) async-start(), calls=%async_computation.11 | async-start | bytes 10485760 | tf_op jit(solution)/shard_map/reduce_scatter | solution.py:134
  16.1 897.6 %copy-start.66 = (pred[1024]{0:T(1024)(128)(4,1)}, pred[1024]{0:T(1024)(128)(4,1)S(1)}, u32[]{:S(2)}) copy-start(pred[1024]{0:T(1024)(128)(4,1)S(1)} %and_reduce_fusion) | copy-start | bytes 3076
  919.6 500.8 %all-gather.33.cloned.1.call-start = ((), (), s32[]{:S(2)}) async-start(), calls=%async_computation.29 | async-start | bytes 25067520 | tf_op jit(solution)/shard_map/all_gather | solution.py:196
  924.1 532.9 %all-gather.15.cloned.1.call-start = ((), (), s32[]{:S(2)}) async-start(), calls=%async_computation.12 | async-start | bytes 5242880 | tf_op jit(solution)/shard_map/all_gather | solution.py:130
  956.4 479.4 %copy-start.40 = (f32[2048]{0:T(1024)}, f32[2048]{0:T(1024)S(1)}, u32[]{:S(2)}) copy-start(f32[2048]{0:T(1024)S(1)} %mul.936) | copy-start | bytes 24580
  996.5 509.0 %all-gather.17.cloned.1.call-start = ((), (), s32[]{:S(2)}) async-start(), calls=%async_computation.13 | async-start | bytes 5242880 | tf_op jit(solution)/shard_map/all_gather | solution.py:138
  1470.9 458.7 %all-gather.35.cloned.1.call-start = ((), (), s32[]{:S(2)}) async-start(), calls=%async_computation.30 | async-start | bytes 11059200 | tf_op jit(solution)/shard_map/all_gather | solution.py:197
  1472.2 529.0 %reduce-scatter.18.cloned.1.call-start = ((), (), s32[]{:S(2)}) async-start(), calls=%async_computation.14 | async-start | bytes 10485760 | tf_op jit(solution)/shard_map/reduce_scatter | solution.py:142
  1929.4 155.7 %reduce-scatter.20.cloned.1.call-start = ((), (), s32[]{:S(2)}) async-start(), calls=%async_computation.15 | async-start | bytes 10485760 | tf_op jit(solution)/shard_map/reduce_scatter | solution.py:134
  2013.2 111.0 %all-gather.19.cloned.1.call-start = ((), (), s32[]{:S(2)}) async-start(), calls=%async_computation.16 | async-start | bytes 5242880 | tf_op jit(solution)/shard_map/all_gather | solution.py:130
  2089.6 140.4 %reduce-scatter.22.cloned.1.call-start = ((), (), s32[]{:S(2)}) async-start(), calls=%async_computation.17 | async-start | bytes 10485760 | tf_op jit(solution)/shard_map/reduce_scatter | solution.py:134
  2158.1 111.0 %all-gather.21.cloned.1.call-start = ((), (), s32[]{:S(2)}) async-start(), calls=%async_computation.18 | async-start | bytes 5242880 | tf_op jit(solution)/shard_map/all_gather | solution.py:130
  2234.4 189.6 %reduce-scatter.24.cloned.1.call-start = ((), (), s32[]{:S(2)}) async-start(), calls=%async_computation.19 | async-start | bytes 10485760 | tf_op jit(solution)/shard_map/reduce_scatter | solution.py:134
  2354.7 109.0 %all-gather.23.cloned.1.call-start = ((), (), s32[]{:S(2)}) async-start(), calls=%async_computation.20 | async-start | bytes 5242880 | tf_op jit(solution)/shard_map/all_gather | solution.py:130
  2429.0 142.6 %reduce-scatter.26.cloned.1.call-start = ((), (), s32[]{:S(2)}) async-start(), calls=%async_computation.21 | async-start | bytes 10485760 | tf_op jit(solution)/shard_map/reduce_scatter | solution.py:134
  2499.8 113.7 %all-gather.25.cloned.1.call-start = ((), (), s32[]{:S(2)}) async-start(), calls=%async_computation.22 | async-start | bytes 5242880 | tf_op jit(solution)/shard_map/all_gather | solution.py:130
  2578.8 77.6 %all-gather.27.cloned.1.call-start = ((), (), s32[]{:S(2)}) async-start(), calls=%async_computation.23 | async-start | bytes 5242880 | tf_op jit(solution)/shard_map/all_gather | solution.py:138
  2621.7 700.3 %reduce-scatter.28.cloned.1.call-start = ((), (), s32[]{:S(2)}) async-start(), calls=%async_computation.24 | async-start | bytes 10485760 | tf_op jit(solution)/shard_map/reduce_scatter | solution.py:142
  3250.2 157.6 %reduce-scatter.32.cloned.1.call-start = ((), (), s32[]{:S(2)}) async-start(), calls=%async_computation.26 | async-start | bytes 10485760 | tf_op jit(solution)/shard_map/reduce_scatter | solution.py:134
  3335.9 289.5 %all-gather.29.cloned.1.call-start = ((), (), s32[]{:S(2)}) async-start(), calls=%async_computation.27 | async-start | bytes 5242880 | tf_op jit(solution)/shard_map/all_gather | solution.py:130
  3412.2 537.6 %reduce-scatter.30.cloned.1.call-start = ((), (), s32[]{:S(2)}) async-start(), calls=%async_computation.25 | async-start | bytes 22118400 | tf_op jit(solution)/shard_map/reduce_scatter | solution.py:336
  3484.3 1033.6 %reduce-scatter.34.cloned.1.call-start = ((), (), s32[]{:S(2)}) async-start(), calls=%async_computation.31 | async-start | bytes 50135040
  3621.0 2169.9 %reduce-scatter.36.cloned.1.call-start = ((), (), s32[]{:S(2)}) async-start(), calls=%async_computation.32 | async-start | bytes 92897280
  (158 other events, 2568.4 us)
Sparse Core Ops, SparseCore 0:
  14.3 785.4 all-gather.30
  919.7 72.0 reduce-scatter.15
  994.0 426.3 all-gather.32
  1422.5 34.4 all-gather.14
  1471.0 34.4 all-gather.16
  1508.4 142.8 all-gather.34
  1929.6 71.5 reduce-scatter.17
  2013.3 71.7 reduce-scatter.19
  2089.7 34.4 all-gather.18
  2158.2 71.6 reduce-scatter.21
  2234.5 34.4 all-gather.20
  2354.8 69.1 reduce-scatter.23
  2429.1 34.4 all-gather.22
  2499.9 71.6 reduce-scatter.25
  2578.9 34.4 all-gather.24
  2621.9 34.4 all-gather.26
  3250.3 71.6 reduce-scatter.27
  3336.0 71.6 reduce-scatter.31
  3412.3 34.4 all-gather.28
  3484.4 324.0 reduce-scatter.29
  3812.4 705.4 reduce-scatter.33
  4522.3 1268.5 reduce-scatter.35
where the time goes:
time: 5940 us; the launch traced here: 5920 us
  waiting for transfers between devices  3670 us (62%)
  local copies, waits for them, and re-layouts  1080 us (18%)
  matrix products  504 us (8%)
  other arithmetic  454 us (8%)
  blocking collectives  159 us (3%)
    unnamed x24, waiting for transfers between devices  1780 us
    all_gather x1, waiting for transfers between devices, on_device(): lax.all_gather(lowered[2], 'dp', axis=0, tiled=True)  783 us
    all_gather x1, waiting for transfers between devices, on_device(): lax.all_gather(lowered[0], 'dp', axis=0, tiled=True)  424 us
    reduce_scatter x6, waiting for transfers between devices, token_sums(): return lax.psum_scatter(values, 'state', scatter_dimension=0, tiled=True)  391 us
    dynamic_update_slice x32, local copies, waits for them, and re-layouts, mixer(): lax.scan(jax.checkpoint(advance), start, (split(query), split(key_gate),...  245 us
    scatter x3, local copies, waits for them, and re-layouts, to_slots(): jnp.zeros((slot_total, block_rows, grad.shape[1]), f32).at[index]  212 us
    all_gather x6, waiting for transfers between devices, token_rows(): return lax.all_gather(values, 'state', axis=0, tiled=True)  159 us
  transfers between devices with their start and end apart: 22, of which 19 were waited for; matrix products, arithmetic and copies ran while one was open for 18% of the time, Pallas kernels for 0%

commit v1 on v0

v1 whole, which is shorter than its diff:
```python
import functools

import jax
import jax.numpy as jnp
from jax import lax
from jax.experimental import pallas as pl
from jax.experimental.pallas import tpu as pltpu
from jax.sharding import PartitionSpec as P

HEADS = 16
KEY_DIM = 128
GROUP = 128
STEP = 5
VAL_DIM = 128


NORM_EPS = 1e-06
LOWER_BOUND = 0.9
CLIP_NORM = 0.02
BETA_FIRST = 0.5
BETA_SECOND = 0.5
ADAM_EPS = 1e-08
LEARN_RATE = 0.02
GAIN_RATE = 0.2
WEIGHT_DECAY = 0.1
AVERAGE_DECAY = 0.9
FULL_PRECISION = lax.Precision.HIGHEST
LANES = 128


def rms_norm(values, gain, width):
    mean = jnp.sum(values * values, axis=-1, keepdims=True) * (1.0 / width)
    return values * lax.rsqrt(mean + NORM_EPS) * gain


def forget_gates(forget_pre):
    key_gate = (1.0 - LOWER_BOUND) * jax.nn.sigmoid(-forget_pre)
    log_forget = jnp.log(LOWER_BOUND + (1.0 - LOWER_BOUND) * jax.nn.sigmoid(forget_pre))
    return key_gate, log_forget


def slot_mixer(query, key_gate, log_forget, values, pick, allowed, heads):
    slots = query.shape[0]
    tokens = key_gate.shape[0]
    blocks = tokens // GROUP
    order = jnp.arange(GROUP)
    lower = (order[:, None] >= order[None, :]).astype(jnp.float32)
    number = jnp.arange(blocks)
    before = (number[:, None] > number[None, :]).astype(jnp.float32)
    inside = jnp.einsum(
        "ts,bsk->btk", lower, log_forget.reshape(blocks, GROUP, -1), precision=FULL_PRECISION
    )
    total = inside[:, -1]
    offset = jnp.dot(before, total, precision=FULL_PRECISION)
    ends = offset + total
    along = (inside + offset[:, None]).reshape(tokens, -1)
    at_slots = jnp.dot(pick, along, precision=FULL_PRECISION)
    key_decay = key_gate * jnp.exp(total[:, None] - inside).reshape(tokens, -1)
    grown = query[None] * jnp.exp(jnp.minimum(at_slots[None] - ends[:, None], 16.0))
    grown = grown.reshape(blocks, slots, heads, KEY_DIM)
    key_decay = key_decay.reshape(blocks, GROUP, heads, KEY_DIM)
    scores = jnp.einsum("bnhk,bghk->hnbg", grown, key_decay, precision=FULL_PRECISION)
    scores = jnp.where(allowed[None], scores.reshape(heads, slots, tokens), 0.0)
    mixed = jnp.einsum(
        "hns,shv->nhv", scores, values.reshape(tokens, heads, VAL_DIM), precision=FULL_PRECISION
    )
    return mixed.reshape(slots, -1)


def document_ids(starts, length):
    return jnp.sum((jnp.arange(length)[:, None] >= starts[None, :]).astype(jnp.int32), axis=1) - 1


def slot_index(owners, capacity):
    order = jnp.arange(owners.shape[0])
    earlier = (owners[:, None] == owners[None, :]) & (order[None, :] < order[:, None])
    ranks = jnp.sum(earlier.astype(jnp.int32), axis=1)
    return owners * capacity + ranks


def adam_update(weight, first, second, average, grad, scale, rate, decay, occupied):
    clipped = scale * grad
    first_new = BETA_FIRST * first + (1.0 - BETA_FIRST) * clipped
    second_new = BETA_SECOND * second + (1.0 - BETA_SECOND) * clipped * clipped
    first_hat = first_new / (1.0 - BETA_FIRST**STEP)
    second_hat = second_new / (1.0 - BETA_SECOND**STEP)
    weight_new = weight - rate * (first_hat / (jnp.sqrt(second_hat) + ADAM_EPS) + decay * weight)
    average_new = AVERAGE_DECAY * average + (1.0 - AVERAGE_DECAY) * weight_new
    return (
        weight_new * occupied,
        first_new * occupied,
        second_new * occupied,
        average_new * occupied,
    )


def times_plain(left, right):
    return jnp.dot(left, right, preferred_element_type=jnp.float32)


def times_right(left, right):
    return lax.dot_general(
        left, right, (((1,), (1,)), ((), ())), preferred_element_type=jnp.float32
    )


def times_left(left, right):
    return lax.dot_general(
        left, right, (((0,), (0,)), ((), ())), preferred_element_type=jnp.float32
    )


def swiglu(joined):
    half_width = joined.shape[1] // 2
    return jax.nn.silu(joined[:, :half_width]) * joined[:, half_width:]


EVERY = ("dp", "state")


def gather_state(values, axis=0):
    return lax.all_gather(values, "state", axis=axis, tiled=True)


def scatter_state(values, axis=0):
    return lax.psum_scatter(values, "state", scatter_dimension=axis, tiled=True)


def swap_dp(values):
    return lax.all_to_all(values, "dp", split_axis=0, concat_axis=0, tiled=True)


def spread_columns(own, parts):
    return own.reshape(own.shape[0], parts, -1).transpose(1, 0, 2)


def join_columns(split):
    return split.transpose(1, 0, 2).reshape(split.shape[1], -1)


MESH = pl.DeviceIdType.MESH


class Links:
    def __init__(self, sends, recvs):
        self.sends, self.recvs, self.used, self.open = sends, recvs, 0, []

    def copy(self, src, dst, dp, state):
        number = self.used
        self.used += 1
        made = pltpu.make_async_remote_copy(
            src_ref=src,
            dst_ref=dst,
            send_sem=self.sends.at[number],
            recv_sem=self.recvs.at[number],
            device_id=(dp, state),
            device_id_type=MESH,
        )
        made.start()
        self.open.append(made)
        return made

    def finish(self):
        for made in self.open:
            made.wait_send()


def greet(peers):
    barrier = pltpu.get_barrier_semaphore()
    for dp, state in peers:
        pl.semaphore_signal(barrier, inc=1, device_id=(dp, state), device_id_type=MESH)
    pl.semaphore_wait(barrier, len(peers))


def places(nd, ns):
    dp, st = lax.axis_index("dp"), lax.axis_index("state")
    return dp, st, lax.div(dp, 2), lax.rem(dp, 2), lax.div(st, 2), lax.rem(st, 2)


def near_peers(nd, ns):
    dp, st, z, y, x, c = places(nd, ns)
    deep, across = nd // 2, ns // 2
    peers = [(lax.rem(z + k, deep) * 2 + y, st) for k in range(1, deep)]
    peers.append((dp + 1 - 2 * y, st))
    peers += [(dp, lax.rem(x + k, across) * 2 + c) for k in range(1, across)]
    peers.append((dp, st + 1 - 2 * c))
    return peers


def small_gather_kernel(nd, ns, everyone, count, *refs):
    sources, outs, (sends, recvs) = refs[:count], refs[count : 2 * count], refs[2 * count :]
    dp, st = lax.axis_index("dp"), lax.axis_index("state")
    peers = []
    for a in range(nd):
        for b in range(ns if everyone else 1):
            if a or b:
                peers.append((lax.rem(dp + a, nd), lax.rem(st + b, ns)))
    greet(peers)
    me = dp * ns + st if everyone else dp
    links = Links(sends, recvs)
    for source, out in zip(sources, outs):
        out[me] = source[...]
        for there, far in peers:
            links.copy(source, out.at[me], there, far)
    for made in links.open:
        made.wait_recv()
    links.finish()


def small_gather(arrays, everyone, number):
    nd, ns = lax.axis_size("dp"), lax.axis_size("state")
    members = nd * ns if everyone else nd
    copies = (members - 1) * len(arrays)
    vmem = pl.BlockSpec(memory_space=pltpu.VMEM)
    return pl.pallas_call(
        functools.partial(small_gather_kernel, nd, ns, everyone, len(arrays)),
        out_shape=[jax.ShapeDtypeStruct((members,) + a.shape, a.dtype) for a in arrays],
        in_specs=[vmem] * len(arrays),
        out_specs=[vmem] * len(arrays),
        scratch_shapes=[pltpu.SemaphoreType.DMA((copies,)), pltpu.SemaphoreType.DMA((copies,))],
        compiler_params=pltpu.CompilerParams(collective_id=number, has_side_effects=True),
    )(*arrays)


def gather_all_kernel(nd, ns, in_ref, out_ref, sends, recvs):
    dp, st, z, y, x, c = places(nd, ns)
    deep, across = nd // 2, ns // 2
    half = in_ref.shape[1] // 2
    cols = (pl.ds(0, half), pl.ds(half, half))
    greet(near_peers(nd, ns))
    links = Links(sends, recvs)
    to_y = (dp + 1 - 2 * y, st)
    to_core = (dp, st + 1 - 2 * c)
    other_y = 1 - y

    def x_at(k):
        return lax.rem(x + k, across)

    def to_x(k):
        return (dp, x_at(k) * 2 + c)

    def group(xx, yy, part):
        return out_ref.at[c, xx, yy, :, :, cols[part]]

    def send(xx, yy, part, place):
        return links.copy(group(xx, yy, part), group(xx, yy, part), *place)

    out_ref[c, x, y, z] = in_ref[...]
    first = []
    for part in range(2):
        for k in range(1, deep):
            there = (lax.rem(z + k, deep) * 2 + y, st)
            first.append(
                links.copy(
                    in_ref.at[:, cols[part]], out_ref.at[c, x, y, z, :, cols[part]], *there
                )
            )
    for made in first[: deep - 1]:
        made.wait_recv()
    a_y = send(x, y, 0, to_y)
    for made in first[deep - 1 :]:
        made.wait_recv()
    b_x = [send(x, y, 1, to_x(k)) for k in range(1, across)]
    a_x = [send(x, y, 0, to_x(k)) for k in range(1, across)]
    b_y = send(x, y, 1, to_y)
    arriving = [send(x, y, 0, to_core), send(x, y, 1, to_core)]
    a_y.wait_recv()
    a_xy = [send(x, other_y, 0, to_x(k)) for k in range(1, across)]
    arriving.append(send(x, other_y, 0, to_core))
    b_xy = []
    for k in range(1, across):
        b_x[k - 1].wait_recv()
        from_x = lax.rem(x - k + across, across)
        b_xy.append(send(from_x, y, 1, to_y))
        arriving.append(send(from_x, y, 1, to_core))
    for k in range(1, across):
        a_x[k - 1].wait_recv()
        arriving.append(send(lax.rem(x - k + across, across), y, 0, to_core))
    b_y.wait_recv()
    arriving.append(send(x, other_y, 1, to_core))
    for k in range(1, across):
        from_x = lax.rem(x - k + across, across)
        a_xy[k - 1].wait_recv()
        arriving.append(send(from_x, other_y, 0, to_core))
        b_xy[k - 1].wait_recv()
        arriving.append(send(from_x, other_y, 1, to_core))
    for made in arriving:
        made.wait_recv()
    links.finish()


def gather_all(values, number):
    nd, ns = lax.axis_size("dp"), lax.axis_size("state")
    rows, wide = values.shape
    deep, across = nd // 2, ns // 2
    copies = 2 * (deep - 1) + 2 + 4 * (across - 1) + 4 * across
    vmem = pl.BlockSpec(memory_space=pltpu.VMEM)
    out = pl.pallas_call(
        functools.partial(gather_all_kernel, nd, ns),
        out_shape=jax.ShapeDtypeStruct((2, across, 2, deep, rows, wide), values.dtype),
        in_specs=[vmem],
        out_specs=vmem,
        scratch_shapes=[pltpu.SemaphoreType.DMA((copies,)), pltpu.SemaphoreType.DMA((copies,))],
        compiler_params=pltpu.CompilerParams(
            collective_id=number, has_side_effects=True, vmem_limit_bytes=40 * 2**20
        ),
    )(values)
    return out.reshape(nd * ns * rows, wide)


def scatter_all_kernel(
    nd, ns, in_ref, out_ref, rc, acc, rx_a, ry_a, rz_a, ry_b, rx_b, rz_b, sends, recvs
):
    dp, st, z, y, x, c = places(nd, ns)
    deep, across = nd // 2, ns // 2
    half = in_ref.shape[5] // 2
    cols = (pl.ds(0, half), pl.ds(half, half))
    greet(near_peers(nd, ns))
    links = Links(sends, recvs)
    to_y = (dp + 1 - 2 * y, st)
    to_core = (dp, st + 1 - 2 * c)
    ys = (y, 1 - y)

    def x_at(k):
        return lax.rem(x + k, across)

    def to_x(k):
        return (dp, x_at(k) * 2 + c)

    core = {}
    order = [(k, ky, 0) for k in range(1, across) for ky in (1, 0)]
    order += [(k, 1, 1) for k in range(across)]
    order += [(0, 1, 0)] + [(k, 0, 1) for k in range(1, across)] + [(0, 0, 0), (0, 0, 1)]
    for k, ky, part in order:
        core[k, ky, part] = links.copy(
            in_ref.at[1 - c, x_at(k), ys[ky], :, :, cols[part]],
            rc.at[x_at(k), ys[ky], :, :, cols[part]],
            *to_core,
        )

    def total(k, ky, part, zz, others):
        found = in_ref[c, x_at(k), ys[ky], zz, :, cols[part]].astype(jnp.float32)
        found += rc[x_at(k), ys[ky], zz, :, cols[part]].astype(jnp.float32)
        for other in others:
            found += other[zz].astype(jnp.float32)
        return found

    def add(k, ky, part, others):
        core[k, ky, part].wait_recv()

        @pl.loop(0, deep)
        def _(zz):
            acc[x_at(k), ys[ky], zz, :, cols[part]] = total(k, ky, part, zz, others).astype(
                acc.dtype
            )

        return acc.at[x_at(k), ys[ky], :, :, cols[part]]

    a_x, b_y = {}, {}
    for k in range(1, across):
        for ky in (1, 0):
            a_x[k, ky] = links.copy(add(k, ky, 0, []), rx_a.at[k - 1, ky], *to_x(k))
    for k in range(across):
        b_y[k] = links.copy(add(k, 1, 1, []), ry_b.at[k], *to_y)
    for k in range(1, across):
        a_x[k, 1].wait_recv()
    a_y = links.copy(
        add(0, 1, 0, [rx_a.at[k - 1, 1] for k in range(1, across)]), ry_a, *to_y
    )
    b_x = {}
    for k in range(1, across):
        b_y[k].wait_recv()
        b_x[k] = links.copy(add(k, 0, 1, [ry_b.at[k]]), rx_b.at[k - 1], *to_x(k))
    for k in range(1, across):
        a_x[k, 0].wait_recv()
    a_y.wait_recv()
    left = [rx_a.at[k - 1, 0] for k in range(1, across)] + [ry_a]
    add(0, 0, 0, left)

    def send_z(part, land):
        return [
            links.copy(
                acc.at[x, y, lax.rem(z + k, deep), :, cols[part]],
                land.at[k - 1],
                lax.rem(z + k, deep) * 2 + y,
                st,
            )
            for k in range(1, deep)
        ]

    a_z = send_z(0, rz_a)
    b_y[0].wait_recv()
    for k in range(1, across):
        b_x[k].wait_recv()
    right = [ry_b.at[0]] + [rx_b.at[k - 1] for k in range(1, across)]
    add(0, 0, 1, right)
    b_z = send_z(1, rz_b)
    for part, made, others, land in ((0, a_z, left, rz_a), (1, b_z, right, rz_b)):
        found = total(0, 0, part, z, others)
        for k in range(1, deep):
            made[k - 1].wait_recv()
            found += land[k - 1].astype(jnp.float32)
        out_ref[:, cols[part]] = found
    links.finish()


def scatter_all(values, number):
    nd, ns = lax.axis_size("dp"), lax.axis_size("state")
    deep, across = nd // 2, ns // 2
    rows, wide = values.shape[0] // (nd * ns), values.shape[1]
    half = wide // 2
    copies = 4 * across + 2 * (across - 1) + across + 1 + (across - 1) + 2 * (deep - 1)
    vmem = pl.BlockSpec(memory_space=pltpu.VMEM)
    kind = values.dtype
    return pl.pallas_call(
        functools.partial(scatter_all_kernel, nd, ns),
        out_shape=jax.ShapeDtypeStruct((rows, wide), jnp.float32),
        in_specs=[vmem],
        out_specs=vmem,
        scratch_shapes=[
            pltpu.VMEM((across, 2, deep, rows, wide), kind),
            pltpu.VMEM((across, 2, deep, rows, wide), kind),
            pltpu.VMEM((across - 1, 2, deep, rows, half), kind),
            pltpu.VMEM((deep, rows, half), kind),
            pltpu.VMEM((deep - 1, rows, half), kind),
            pltpu.VMEM((across, deep, rows, half), kind),
            pltpu.VMEM((across - 1, deep, rows, half), kind),
            pltpu.VMEM((deep - 1, rows, half), kind),
            pltpu.SemaphoreType.DMA((copies,)),
            pltpu.SemaphoreType.DMA((copies,)),
        ],
        compiler_params=pltpu.CompilerParams(
            collective_id=number, has_side_effects=True, vmem_limit_bytes=40 * 2**20
        ),
    )(values.reshape(2, across, 2, deep, rows, wide))


def lookup_kernel(nd, ns, in_ref, out_ref, rc, acc, rx, fin, sends, recvs):
    dp, st, z, y, x, c = places(nd, ns)
    across = ns // 2
    own = in_ref.shape[0]
    tokens = in_ref.shape[1] // nd
    part = tokens // ns
    to_core = (dp, st + 1 - 2 * c)
    peers = [(lax.rem(dp + k, nd), st) for k in range(1, nd)]
    peers += [(dp, lax.rem(x + k, across) * 2 + c) for k in range(1, across)]
    peers.append(to_core)
    greet(peers)
    links = Links(sends, recvs)

    def x_at(k):
        return lax.rem(x + k, across)

    def row_at(k):
        return lax.rem(dp + k, nd)

    def block(k, kx, cc):
        start = row_at(k) * tokens + (x_at(kx) * 2 + cc) * part
        return in_ref.at[:, pl.ds(pl.multiple_of(start, part), part)]

    def place(owner, share):
        return out_ref.at[
            pl.ds(pl.multiple_of(owner * own, own), own),
            pl.ds(pl.multiple_of(share * part, part), part),
        ]

    def add(sources, target):
        @pl.loop(0, own // 32)
        def _(i):
            rows = pl.ds(pl.multiple_of(i * 32, 32), 32)
            found = sources[0][rows, :].astype(jnp.float32)
            for source in sources[1:]:
                found += source[rows, :].astype(jnp.float32)
            target[rows, :] = found.astype(target.dtype)

    turn = list(range(1, nd)) + [0]
    core, across_x, across_dp = {}, {}, {}
    for k in turn:
        for kx in list(range(1, across)) + [0]:
            core[k, kx] = links.copy(block(k, kx, 1 - c), rc.at[k, kx], *to_core)
    for k in turn:
        for kx in range(1, across):
            core[k, kx].wait_recv()
            add([block(k, kx, c), rc.at[k, kx]], acc.at[k, kx - 1])
            across_x[k, kx] = links.copy(
                acc.at[k, kx - 1], rx.at[k, kx - 1], dp, x_at(kx) * 2 + c
            )
    for k in turn:
        core[k, 0].wait_recv()
        sources = [block(k, 0, c), rc.at[k, 0]]
        for kx in range(1, across):
            across_x[k, kx].wait_recv()
            sources.append(rx.at[k, kx - 1])
        if k:
            add(sources, fin.at[k - 1])
            across_dp[k] = links.copy(fin.at[k - 1], place(dp, st), row_at(k), st)
        else:
            add(sources, place(dp, st))
    later, last = {}, []
    for k in [0] + list(range(1, nd)):
        owner = lax.rem(dp - k + nd, nd)
        if k:
            across_dp[k].wait_recv()
        for kx in range(1, across):
            later[k, kx] = links.copy(
                place(owner, st), place(owner, st), dp, x_at(kx) * 2 + c
            )
        last.append(links.copy(place(owner, st), place(owner, st), *to_core))
    for k in range(nd):
        owner = lax.rem(dp - k + nd, nd)
        for kx in range(1, across):
            later[k, kx].wait_recv()
            share = lax.rem(x - kx + across, across) * 2 + c
            last.append(links.copy(place(owner, share), place(owner, share), *to_core))
    for made in last:
        made.wait_recv()
    links.finish()


def lookup_rows(values, number):
    nd, ns = lax.axis_size("dp"), lax.axis_size("state")
    across = ns // 2
    own, total = values.shape
    tokens = total // nd
    part = tokens // ns
    copies = nd * across + nd * (across - 1) + nd - 1 + nd * across + nd * (across - 1)
    vmem = pl.BlockSpec(memory_space=pltpu.VMEM)
    kind = values.dtype
    return pl.pallas_call(
        functools.partial(lookup_kernel, nd, ns),
        out_shape=jax.ShapeDtypeStruct((nd * own, tokens), kind),
        in_specs=[vmem],
        out_specs=vmem,
        scratch_shapes=[
            pltpu.VMEM((nd, across, own, part), kind),
            pltpu.VMEM((nd, across - 1, own, part), kind),
            pltpu.VMEM((nd, across - 1, own, part), kind),
            pltpu.VMEM((nd - 1, own, part), kind),
            pltpu.SemaphoreType.DMA((copies,)),
            pltpu.SemaphoreType.DMA((copies,)),
        ],
        compiler_params=pltpu.CompilerParams(
            collective_id=number, has_side_effects=True, vmem_limit_bytes=48 * 2**20
        ),
    )(values)


def swap_parts(values):
    nd = lax.axis_size("dp")
    me = lax.axis_index("dp")
    mine = lax.dynamic_index_in_dim(values, me, 0)
    found = lax.dynamic_update_index_in_dim(jnp.zeros_like(values), mine, me, 0)
    for k in range(1, nd):
        sent = lax.dynamic_index_in_dim(values, lax.rem(me + k, nd), 0)
        got = lax.ppermute(sent, "dp", [(i, (i + k) % nd) for i in range(nd)])
        found = lax.dynamic_update_index_in_dim(found, got, lax.rem(me - k + nd, nd), 0)
    return found


def on_device(
    token_ids,
    doc_starts,
    loss_positions,
    loss_targets,
    owners,
    in_weight,
    out_weight,
    table_weight,
    gain_weight,
    in_first,
    out_first,
    table_first,
    gain_first,
    in_second,
    out_second,
    table_second,
    gain_second,
    in_average,
    out_average,
    table_average,
    gain_average,
):
    f32 = jnp.float32
    bf16 = jnp.bfloat16
    nd = lax.axis_size("dp")
    ns = lax.axis_size("state")
    me_dp = lax.axis_index("dp")
    me_state = lax.axis_index("state")
    tokens = token_ids.shape[1]
    slots = loss_positions.shape[1]
    capacity = in_weight.shape[1]
    block_rows = in_weight.shape[2]
    block_count = owners.shape[0]
    width = block_rows * block_count
    own = capacity * block_rows
    wide = nd * own
    key_share = KEY_DIM // ns
    heads = HEADS // ns
    key_cols = HEADS * key_share
    value_width = heads * VAL_DIM
    mixer_cols = 2 * key_cols + value_width
    units = out_weight.shape[3] - value_width
    unit_part = units // nd
    vocab_share = table_weight.shape[3]
    vocab_part = -(-vocab_share // (nd * LANES)) * LANES
    quarter = tokens // ns
    slot_part = slots // ns

    held_all = jnp.sum((owners[None, :] == jnp.arange(nd)[:, None]).astype(jnp.int32), axis=1)
    occupied_all = jnp.arange(capacity)[None, :] < held_all[:, None]
    held = jnp.sum((owners == me_dp).astype(jnp.int32))
    occupied_here = jnp.arange(capacity) < held
    rows_here = jnp.repeat(occupied_here, block_rows)[:, None]

    def lowered(array):
        return jnp.where(rows_here, array[0].reshape(own, -1), 0.0).astype(bf16)

    in_own = lowered(in_weight)
    out_own = lowered(out_weight)
    table_own = lowered(table_weight)

    def in_rows(flat, multiple):
        flat = jnp.pad(flat, (0, -flat.shape[0] % (multiple * LANES)))
        return flat.reshape(-1, LANES)

    small, gains_all = small_gather(
        [
            in_rows(jnp.concatenate([token_ids[0], loss_targets[0]]), 8),
            in_rows(gain_weight.astype(bf16).reshape(-1), 16),
        ],
        False,
        1,
    )
    small = small.reshape(nd, -1)
    ids_all = small[:, :tokens]
    slot_targets = small[:, tokens : tokens + slots].reshape(nd // 2, 2, ns // 2, 2, slot_part)
    targets_all = slot_targets.transpose(3, 2, 1, 0, 4).reshape(-1)
    gains_all = gains_all.reshape(nd, -1)[:, : capacity * 4 * block_rows].astype(f32)
    gains_all = gains_all.reshape(nd * capacity, 4, block_rows)
    gains = jnp.where(occupied_all.reshape(-1)[:, None, None], gains_all, 0.0)
    gains = gains.transpose(1, 0, 2).reshape(4, wide)
    index = slot_index(owners, capacity)
    head_gain = lax.dynamic_slice_in_dim(
        gains_all[index][:, 1].reshape(width), me_state * value_width, value_width
    )
    live = (targets_all >= 0).astype(f32)
    count = jnp.sum(live)

    local_ids = ids_all.reshape(-1) - me_state * vocab_share
    hit = jnp.arange(vocab_share)[:, None] == local_ids[None, :]
    looked = times_plain(table_own, hit.astype(bf16)).astype(bf16)
    stream = lookup_rows(looked, 2)
    stream_mine = lax.dynamic_slice_in_dim(stream, me_state * quarter, quarter, axis=1)

    exchanged = in_own[:, : 2 * key_cols].reshape(own, 2, ns, heads * key_share)
    exchanged = exchanged.transpose(2, 0, 1, 3).reshape(ns, own * 2, heads, key_share)
    exchanged = lax.all_to_all(exchanged, "state", split_axis=0, concat_axis=0, tiled=True)
    exchanged = exchanged.transpose(1, 2, 0, 3).reshape(own, 2 * heads * KEY_DIM)
    mixer_own = jnp.concatenate(
        [exchanged, in_own[:, 2 * key_cols : mixer_cols], out_own[:, :value_width]], axis=1
    )
    mixer_weights = lax.all_gather(mixer_own, "dp", axis=0, tiled=True)
    qcols = heads * KEY_DIM
    w_qfv = mixer_weights[:, : 2 * qcols + value_width]
    w_q = mixer_weights[:, :qcols]
    w_fv = mixer_weights[:, qcols : 2 * qcols + value_width]
    w_o = mixer_weights[:, 2 * qcols + value_width :]
    ffn_own = jnp.stack(
        [
            in_own[:, mixer_cols : mixer_cols + units].reshape(own, nd, unit_part),
            in_own[:, mixer_cols + units :].reshape(own, nd, unit_part),
            out_own[:, value_width:].reshape(own, nd, unit_part),
        ],
        axis=2,
    ).reshape(own, nd * 3 * unit_part)
    ffn = swap_parts(spread_columns(ffn_own, nd)).reshape(wide, 3 * unit_part)
    w_gu = ffn[:, : 2 * unit_part]
    w_d = ffn[:, 2 * unit_part :]
    table_padded = jnp.pad(table_own, ((0, 0), (0, nd * vocab_part - vocab_share)))
    table = swap_parts(spread_columns(table_padded, nd)).reshape(wide, vocab_part)

    positions = loss_positions[0]
    pick_hit = positions[:, None] == jnp.arange(tokens)[None, :]
    pick = pick_hit.astype(f32)
    pick_low = pick_hit.astype(bf16)
    documents = document_ids(doc_starts[0], tokens)
    doc_at = jnp.sum(jnp.where(pick_hit, documents[None, :], 0), axis=1)
    allowed = (positions[:, None] >= jnp.arange(tokens)[None, :]) & (
        doc_at[:, None] == documents[None, :]
    )

    def tall_norm(values, gain):
        mean = jnp.sum(values * values, axis=0, keepdims=True) * (1.0 / width)
        return values * lax.rsqrt(mean + NORM_EPS) * gain[:, None]

    normed_one = tall_norm(stream.astype(f32), gains[0]).astype(bf16)
    normed_at = times_right(pick_low, normed_one).astype(bf16)
    stream_at = times_right(
        lax.dynamic_slice_in_dim(pick_low, me_state * slot_part, slot_part), stream
    )
    forget_value = times_left(normed_one, w_fv)
    query_pre = times_plain(normed_at, w_q)
    query, back_query = jax.vjp(jax.nn.silu, query_pre)
    (key_gate, log_forget), back_gates = jax.vjp(forget_gates, forget_value[:, :qcols])

    def mix(query_in, key_in, forget_in, value_in):
        return slot_mixer(query_in, key_in, forget_in, value_in, pick, allowed, heads)

    mixed, back_mix = jax.vjp(
        mix,
        query.astype(bf16).astype(f32),
        key_gate.astype(bf16).astype(f32),
        log_forget,
        forget_value[:, qcols:].astype(bf16).astype(f32),
    )

    def head_norm(mixed_in, gain_in):
        return rms_norm(
            mixed_in.reshape(slots, heads, VAL_DIM), gain_in.reshape(heads, VAL_DIM), VAL_DIM
        ).reshape(slots, value_width)

    gated_f, back_head = jax.vjp(head_norm, mixed, head_gain)
    gated = gated_f.astype(bf16)
    stream_one = stream_at + scatter_state(times_right(gated, w_o))

    def wide_norm(values, gain):
        return rms_norm(values, gain, width)

    normed_two, back_two = jax.vjp(wide_norm, stream_one, gains[2])
    rows_two = gather_all(normed_two.astype(bf16), 3)
    gate_up = times_plain(rows_two, w_gu)
    hidden_f, back_glu = jax.vjp(swiglu, gate_up)
    hidden = hidden_f.astype(bf16)
    stream_two = stream_one + scatter_all(times_right(hidden, w_d).astype(bf16), 4)
    normed_three, back_three = jax.vjp(wide_norm, stream_two, gains[3])
    rows_three = gather_all(normed_three.astype(bf16), 5)

    logits = times_plain(rows_three, table)
    column = jnp.arange(vocab_part)[None, :] + me_dp * vocab_part
    target_hit = (column + me_state * vocab_share == targets_all[:, None]) & (
        column < vocab_share
    )
    logits = jnp.where(column < vocab_share, logits, -1e30)
    top_here = jnp.max(logits, axis=1)
    sum_here = jnp.sum(jnp.exp(logits - top_here[:, None]), axis=1)
    picked_here = jnp.sum(jnp.where(target_hit, logits, 0.0), axis=1)
    shares = small_gather(
        [jnp.stack([top_here, sum_here, picked_here]).reshape(-1, LANES)], True, 6
    )[0].reshape(nd * ns, 3, -1)
    top = jnp.max(shares[:, 0], axis=0)
    lse = top + jnp.log(jnp.sum(shares[:, 1] * jnp.exp(shares[:, 0] - top[None]), axis=0))
    loss_sum = jnp.sum((lse - jnp.sum(shares[:, 2], axis=0)) * live)
    probs = jnp.exp(logits - lse[:, None])
    dlogits = ((probs - target_hit.astype(f32)) * (live / count)[:, None]).astype(bf16)
    grad_three = scatter_all(times_right(dlogits, table).astype(bf16), 7)
    grad_table_part = times_left(rows_three, dlogits).astype(bf16)
    grad_table_own = join_columns(swap_parts(grad_table_part.reshape(nd, own, vocab_part)))
    grad_table_own = grad_table_own[:, :vocab_share].astype(f32)

    grad_two, grad_gain_four = back_three(grad_three)
    down_rows = gather_all(grad_two.astype(bf16), 8)
    grad_hidden = times_plain(down_rows, w_d)
    grad_down = times_left(down_rows, hidden)
    (grad_gate_up,) = back_glu(grad_hidden)
    grad_gate_up = grad_gate_up.astype(bf16)
    grad_gu = times_left(rows_two, grad_gate_up)
    grad_norm_two = scatter_all(times_right(grad_gate_up, w_gu).astype(bf16), 9)
    grad_stream_one, grad_gain_three = back_two(grad_norm_two)
    grad_one = gather_state((grad_two + grad_stream_one).astype(bf16))
    grad_ffn = jnp.concatenate([grad_gu, grad_down], axis=1).astype(bf16)
    grad_ffn = join_columns(swap_parts(grad_ffn.reshape(nd, own, 3 * unit_part)))
    grad_ffn = grad_ffn.reshape(own, nd, 3, unit_part)

    grad_gated = times_plain(grad_one, w_o)
    grad_w_o = times_left(grad_one, gated)
    grad_mixed, grad_gain_two = back_head(grad_gated)
    grad_query, grad_key, grad_forget, grad_value = back_mix(
        grad_mixed.astype(bf16).astype(f32)
    )
    (grad_query_pre,) = back_query(grad_query)
    grad_query_pre = times_left(pick, grad_query_pre)
    (grad_forget_pre,) = back_gates((grad_key, grad_forget))
    grad_qfv = jnp.concatenate([grad_query_pre, grad_forget_pre, grad_value], axis=1).astype(bf16)
    grad_w_qfv = times_plain(normed_one, grad_qfv)
    grad_norm_one = scatter_state(times_right(w_qfv, grad_qfv).astype(bf16), 1).astype(f32)
    _, back_one = jax.vjp(tall_norm, stream_mine.astype(f32), gains[0])
    grad_stream_zero, grad_gain_one = back_one(grad_norm_one)
    pick_mine = lax.dynamic_slice_in_dim(pick_low, me_state * quarter, quarter, axis=1)
    grad_zero = (grad_stream_zero + times_left(grad_one, pick_mine)).astype(bf16)
    grad_mixer_own = lax.psum_scatter(
        jnp.concatenate([grad_w_qfv, grad_w_o], axis=1).astype(bf16),
        "dp",
        scatter_dimension=0,
        tiled=True,
    )

    embed = swap_dp(grad_zero.reshape(nd, own, quarter))
    embed = gather_state(embed, 2).transpose(1, 0, 2).reshape(own, nd * tokens)
    grad_lookup = times_right(embed, hit.astype(bf16))
    own_table = grad_table_own + grad_lookup

    returned = grad_mixer_own[:, : 2 * qcols].reshape(own * 2, heads, ns, key_share)
    returned = returned.transpose(2, 0, 1, 3)
    returned = lax.all_to_all(returned, "state", split_axis=0, concat_axis=0, tiled=True)
    returned = returned.reshape(ns, own, 2, heads * key_share).transpose(1, 2, 0, 3)
    returned = returned.reshape(own, 2 * key_cols)
    own_in = jnp.concatenate(
        [
            returned,
            grad_mixer_own[:, 2 * qcols : 2 * qcols + value_width],
            grad_ffn[:, :, 0].reshape(own, units),
            grad_ffn[:, :, 1].reshape(own, units),
        ],
        axis=1,
    ).astype(f32)
    own_out = jnp.concatenate(
        [grad_mixer_own[:, 2 * qcols + value_width :], grad_ffn[:, :, 2].reshape(own, units)],
        axis=1,
    ).astype(f32)

    head_full = lax.dynamic_update_slice_in_dim(
        jnp.zeros((width,), f32), grad_gain_two, me_state * value_width, 0
    )
    gain_sums = lax.psum(
        jnp.concatenate([grad_gain_one, grad_gain_three, grad_gain_four, head_full]), EVERY
    )
    head_slots = (
        jnp.zeros((nd * capacity, block_rows), f32)
        .at[index]
        .set(gain_sums[3 * wide :].reshape(block_count, block_rows))
    )
    gain_slots = gain_sums[: 3 * wide].reshape(3, nd * capacity, block_rows)
    gain_slots = jnp.stack([gain_slots[0], head_slots, gain_slots[1], gain_slots[2]], axis=1)
    own_gain = lax.dynamic_slice_in_dim(gain_slots, me_dp * capacity, capacity)

    squares = jnp.sum(own_in * own_in) + jnp.sum(own_out * own_out) + jnp.sum(own_table * own_table)
    squares = small_gather([jnp.full((8, LANES), squares)], True, 10)[0][:, 0, 0]
    squares_all = jnp.sum(squares) + jnp.sum(gain_sums * gain_sums)
    grad_norm = jnp.sqrt(squares_all)
    scale = jnp.minimum(1.0, CLIP_NORM / (grad_norm + 1e-06))
    occupied = occupied_here.astype(f32)
    wide_occ = occupied[None, :, None, None]
    new_in = adam_update(
        in_weight,
        in_first,
        in_second,
        in_average,
        own_in.reshape(in_weight.shape),
        scale,
        LEARN_RATE,
        WEIGHT_DECAY,
        wide_occ,
    )
    new_out = adam_update(
        out_weight,
        out_first,
        out_second,
        out_average,
        own_out.reshape(out_weight.shape),
        scale,
        LEARN_RATE,
        WEIGHT_DECAY,
        wide_occ,
    )
    new_table = adam_update(
        table_weight,
        table_first,
        table_second,
        table_average,
        own_table.reshape(table_weight.shape),
        scale,
        LEARN_RATE,
        WEIGHT_DECAY,
        wide_occ,
    )
    new_gain = adam_update(
        gain_weight,
        gain_first,
        gain_second,
        gain_average,
        own_gain,
        scale,
        GAIN_RATE,
        0.0,
        occupied[:, None, None],
    )
    return (
        new_in[0],
        new_out[0],
        new_table[0],
        new_gain[0],
        new_in[1],
        new_out[1],
        new_table[1],
        new_gain[1],
        new_in[2],
        new_out[2],
        new_table[2],
        new_gain[2],
        new_in[3],
        new_out[3],
        new_table[3],
        new_gain[3],
        loss_sum,
        count,
        grad_norm,
    )


def solution(mesh):
    return jax.shard_map(
        on_device,
        mesh=mesh,
        in_specs=(
            P("dp", None),
            P("dp", None),
            P("dp", None),
            P("dp", None),
            P(),
            P("state", "dp", None, None),
            P("state", "dp", None, None),
            P("state", "dp", None, None),
            P("dp", None, None),
            P("state", "dp", None, None),
            P("state", "dp", None, None),
            P("state", "dp", None, None),
            P("dp", None, None),
            P("state", "dp", None, None),
            P("state", "dp", None, None),
            P("state", "dp", None, None),
            P("dp", None, None),
            P("state", "dp", None, None),
            P("state", "dp", None, None),
            P("state", "dp", None, None),
            P("dp", None, None),
        ),
        out_specs=(
            P("state", "dp", None, None),
            P("state", "dp", None, None),
            P("state", "dp", None, None),
            P("dp", None, None),
            P("state", "dp", None, None),
            P("state", "dp", None, None),
            P("state", "dp", None, None),
            P("dp", None, None),
            P("state", "dp", None, None),
            P("state", "dp", None, None),
            P("state", "dp", None, None),
            P("dp", None, None),
            P("state", "dp", None, None),
            P("state", "dp", None, None),
            P("state", "dp", None, None),
            P("dp", None, None),
            P(),
            P(),
            P(),
        ),
        check_vma=False,
    )
```

time: 5940 us -> 1600 us (0.27)
  waiting for transfers between devices: 3670 us -> 175 us
  local copies, waits for them, and re-layouts: 1080 us -> 274 us
  Pallas kernels: 0 us -> 472 us
  other arithmetic: 454 us -> 136 us
  matrix products: 504 us -> 242 us
  starting transfers between devices: 1.93 us -> 165 us
    unnamed x24 -> x6, waiting for transfers between devices: 1780 us -> 0.08 us
    all_gather x11 -> x2, waiting for transfers between devices: 1410 us -> 0.01 us  [the longest x1 0.01 us: on_device(): mixer_weights = lax.all_gather(mixer_own, 'dp', axis=0, tiled=True)]
    pallas_call x0 -> x10, Pallas kernels: none -> 472 us  [the longest x3 141 us: gather_all(): pl.pallas_call(functools.partial(gather_all_kernel, nd, ns), out_shape=ja...]
    reduce_scatter x9 -> x2, waiting for transfers between devices: 488 us -> 50.3 us  [scatter_state(): return lax.psum_scatter(values, 'state', scatter_dimension=axis, tiled=True)]
    dot_general x104 -> x12, matrix products: 279 us -> 33.1 us  [the longest x3 18.6 us: slot_mixer(): jnp.einsum('bnhk,bghk->hnbg', grown, key_decay, precision=FULL_PRECISION)]
    scatter x4 -> x1, local copies, waits for them, and re-layouts: 214 us -> 1.35 us  [on_device(): head_slots = jnp.zeros((nd * capacity, block_rows), f32).at[index].set(ga...]
    dynamic_update_slice x32, local copies, waits for them, and re-layouts: 245 us -> 46.7 us  [the longest x29 44.6 us: swap_parts(): lax.dynamic_update_index_in_dim(found, got, lax.rem(me - k + nd, nd), 0)]
    ppermute x0 -> x28, starting transfers between devices: none -> 157 us  [swap_parts(): got = lax.ppermute(sent, 'dp', [(i, (i + k) % nd) for i in range(nd)])]
  transfers between devices with their start and end apart: 22 -> 35, of which waited for: 19 -> 13; matrix products, arithmetic and copies ran while one was open for 18% -> 26% of each run, Pallas kernels for 0% -> 10%
where the time goes in v1:
time: 1600 us; the launch traced here: 1590 us
  Pallas kernels  472 us (30%)
  local copies, waits for them, and re-layouts  274 us (17%)
  matrix products  242 us (15%)
  waiting for transfers between devices  175 us (11%)
  starting transfers between devices  165 us (10%)
  other arithmetic  136 us (8%)
  blocking collectives  104 us (6%)
  between operations  21.2 us (1%)
    ppermute x28, starting transfers between devices, swap_parts(): got = lax.ppermute(sent, 'dp', [(i, (i + k) % nd) for i in range(nd)])  157 us
    pallas_call x3, Pallas kernels, gather_all(): pl.pallas_call(functools.partial(gather_all_kernel, nd, ns), out_shape=ja...  141 us
    pallas_call x3, Pallas kernels, scatter_all(): pl.pallas_call(functools.partial(scatter_all_kernel, nd, ns), out_shape=j...  137 us
    pallas_call x3, Pallas kernels, small_gather(): pl.pallas_call(functools.partial(small_gather_kernel, nd, ns, everyone, l...  126 us
    ppermute x28, waiting for transfers between devices, swap_parts(): got = lax.ppermute(sent, 'dp', [(i, (i + k) % nd) for i in range(nd)])  118 us
    dot_general x7, matrix products, times_right(): lax.dot_general(left, right, (((1,), (1,)), ((), ())), preferred_element_...  96.2 us
    dot_general x7, matrix products, times_plain(): return jnp.dot(left, right, preferred_element_type=jnp.float32)  78.2 us
    pallas_call x1, Pallas kernels, lookup_rows(): pl.pallas_call(functools.partial(lookup_kernel, nd, ns), out_shape=jax.Sh...  67.8 us
  transfers between devices with their start and end apart: 35, of which 13 were waited for; matrix products, arithmetic and copies ran while one was open for 26% of the time, Pallas kernels for 10%

profile of v1, /device:TPU:0, one launch (start us, length us, event | category | flops | bytes accessed | tf_op | source)
XLA Modules:
  0.0 1589.5 jit_solution(16090408216633346432)
XLA Ops:
  74.7 98.1 %shard_map.348 = (s32[8,16,128]{2,1,0:T(8,128)}, bf16[8,16,128]{2,1,0:T(8,128)(2,1)}) custom-call(s32[16,128]{1,0:T(8,128)} %pad_bitcast_fusion.refs_0_, bf16[16,128]{1,0:T(8,128)(2,1)} %pad_bitcast_fusion.1.refs_1_), custom_call_target="tpu_custom_call" | custom-call | tf_op jit(solution)/shard_map/pallas_call | solution.py:215
  181.1 48.4 %fusion.5.in_ref = bf16[320,8192]{1,0:T(8,128)(2,1)} fusion(bf16[320,8000]{1,0:T(8,128)(2,1)S(1)} %fusion.10, s32[8192]{0:T(1024)S(1)} %bitcast.374), kind=kOutput, calls=%fused_computation.13 | convolution fusion | flops 42011197440 | bytes 10395648 | tf_op jit(solution)/shard_map/dot_general | solution.py:98
  229.5 67.8 %shard_map.349 = bf16[2560,1024]{1,0:T(8,128)(2,1)S(1)} custom-call(bf16[320,8192]{1,0:T(8,128)(2,1)} %fusion.5.in_ref), custom_call_target="tpu_custom_call" | custom-call | tf_op jit(solution)/shard_map/pallas_call | solution.py:529
  368.4 27.3 %constant_dynamic-slice_fusion.7 = (bf16[320,1,1024]{2,1,0:T(2,128)(2,1)S(1)}, bf16[320,1,1024]{2,1,0:T(2,128)(2,1)}, bf16[320,1,1024]{2,1,0:T(2,128)(2,1)}, bf1...) fusion(bf16[320,8,1024]{2,1,0:T(8,128)(2,1)} %bitcast.315, ...), kind=kLoop, calls=%fused_computation.323 | loop fusion | bytes 10485792 | tf_op jit(solution)/shard_map/dynamic-slice.15
  439.7 19.8 %collective-permute-done.6 = bf16[1,320,528]{1,2,0:T(8,128)(2,1)S(1)} collective-permute-done((bf16[1,320,528]{1,2,0:T(8,128)(2,1)}, bf16[1,320,528]{1,2,0:T(8,128)(2,1)S(1)}, u32[]{:S(2)}, u32[]{:S(2)}) %collective-permute-start.6) | collective-permute-done | bytes 337952 | tf_op jit(solution)/shard_map/ppermute | solution.py:555
  478.5 26.5 %collective-permute-done.9 = bf16[1,320,1024]{2,1,0:T(8,128)(2,1)} collective-permute-done((bf16[1,320,1024]{2,1,0:T(8,128)(2,1)}, bf16[1,320,1024]{2,1,0:T(8,128)(2,1)}, u32[]{:S(2)}, u32[]{:S(2)}) %collective-permute-start.9) | collective-permute-done | bytes 655392 | tf_op jit(solution)/shard_map/ppermute | solution.py:555
  534.3 61.7 %shard_map.350 = bf16[2,2,2,4,32,2560]{5,4,3,2,1,0:T(8,128)(2,1)S(1)} custom-call(bf16[32,2560]{1,0:T(8,128)(2,1)S(1)} %multiply_convert_fusion.4.in_ref), custom_call_target="tpu_custom_call" | custom-call | tf_op jit(solution)/shard_map/pallas_call | solution.py:298
  601.3 48.5 %shard_map.351 = f32[32,2560]{1,0:T(8,128)S(1)} custom-call(bf16[2,2,2,4,32,2560]{5,4,3,2,1,0:T(8,128)(2,1)S(1)} %bitcast.304), custom_call_target="tpu_custom_call" | custom-call | tf_op jit(solution)/shard_map/pallas_call | solution.py:415
  650.1 37.7 %shard_map.352 = bf16[2,2,2,4,32,2560]{5,4,3,2,1,0:T(8,128)(2,1)S(1)} custom-call(bf16[32,2560]{1,0:T(8,128)(2,1)S(1)} %multiply_convert_fusion.3.in_ref), custom_call_target="tpu_custom_call" | custom-call | tf_op jit(solution)/shard_map/pallas_call | solution.py:298
  698.2 15.8 shard_map.353
  730.2 45.4 %shard_map.354 = f32[32,2560]{1,0:T(8,128)S(1)} custom-call(bf16[2,2,2,4,32,2560]{5,4,3,2,1,0:T(8,128)(2,1)S(1)} %bitcast.313), custom_call_target="tpu_custom_call" | custom-call | tf_op jit(solution)/shard_map/pallas_call | solution.py:415
  776.5 41.4 %shard_map.355 = bf16[2,2,2,4,32,2560]{5,4,3,2,1,0:T(8,128)(2,1)S(1)} custom-call(bf16[32,2560]{1,0:T(8,128)(2,1)S(1)} %fusion.145.in_ref), custom_call_target="tpu_custom_call" | custom-call | tf_op jit(solution)/shard_map/pallas_call | solution.py:298
  823.5 43.5 %shard_map.356 = f32[32,2560]{1,0:T(8,128)S(1)} custom-call(bf16[2,2,2,4,32,2560]{5,4,3,2,1,0:T(8,128)(2,1)S(1)} %bitcast.314), custom_call_target="tpu_custom_call" | custom-call | tf_op jit(solution)/shard_map/pallas_call | solution.py:415
  925.9 50.3 %reduce-scatter.8.cloned.1.call-done = bf16[2560,256]{1,0:T(8,128)(2,1)} async-done(((bf16[2560,1024]{1,0:T(8,128)(2,1)}), bf16[2560,256]{1,0:T(8,128)(2,1)}) %reduce-scatter.8.cloned.1.call-update) | async-done | bytes 1310736 | tf_op jit(solution)/shard_map/reduce_scatter | solution.py:126
  982.2 36.9 %all_to_all.15 = bf16[8,320,256]{2,1,0:T(8,128)(2,1)} all-to-all(bf16[8,320,256]{2,1,0:T(8,128)(2,1)S(1)} %bitcast.356), channel_id=1, replica_groups=mesh['dp'=8,'state'=4] {'dp'}, dimensions={0} | all-to-all | bytes 2621440 | tf_op jit(solution)/shard_map/all_to_all | solution.py:130
  1127.3 21.9 %collective-permute-start.20 = (bf16[1,320,528]{2,1,0:T(8,128)(2,1)}, bf16[1,320,528]{2,1,0:T(8,128)(2,1)}, u32[]{:S(2)}, u32[]{:S(2)}) collective-permute-start(bf16[1,320,528]{2,1,0:T(8,128)(2,1)} %get-tuple-element.194), channel_id=1, source_target_pairs={{0,28},{4,0},{8,4},{12,8},{16,12},{20,16},{24,20},{28,24},{1,29},{... | collective-permute-start | bytes 1013768 | tf_op jit(solution)/shard_map/ppermute | solution.py:555
  1161.9 18.8 %collective-permute-done.16 = bf16[1,320,528]{2,1,0:T(8,128)(2,1)} collective-permute-done((bf16[1,320,528]{2,1,0:T(8,128)(2,1)}, bf16[1,320,528]{2,1,0:T(8,128)(2,1)}, u32[]{:S(2)}, u32[]{:S(2)}) %collective-permute-start.16) | collective-permute-done | bytes 337952 | tf_op jit(solution)/shard_map/ppermute | solution.py:555
  1180.7 21.5 %collective-permute-start.22 = (bf16[1,320,1024]{2,1,0:T(8,128)(2,1)}, bf16[1,320,1024]{2,1,0:T(8,128)(2,1)}, u32[]{:S(2)}, u32[]{:S(2)}) collective-permute-start(bf16[1,320,1024]{2,1,0:T(8,128)(2,1)} %get-tuple-element.181), channel_id=1, source_target_pairs={{0,8},{4,12},{8,16},{12,20},{16,24},{20,28},{24,0},{28,4},{1,9},{5... | collective-permute-start | bytes 1966088 | tf_op jit(solution)/shard_map/ppermute | solution.py:555
  1204.2 18.9 %collective-permute-start.23 = (bf16[1,320,1024]{2,1,0:T(8,128)(2,1)}, bf16[1,320,1024]{2,1,0:T(8,128)(2,1)}, u32[]{:S(2)}, u32[]{:S(2)}) collective-permute-start(bf16[1,320,1024]{2,1,0:T(8,128)(2,1)} %get-tuple-element.180), channel_id=1, source_target_pairs={{0,12},{4,16},{8,20},{12,24},{16,28},{20,0},{24,4},{28,8},{1,13},{... | collective-permute-start | bytes 1966088 | tf_op jit(solution)/shard_map/ppermute | solution.py:555
  1230.5 41.1 %collective-permute-start.25 = (bf16[1,320,1024]{2,1,0:T(8,128)(2,1)}, bf16[1,320,1024]{2,1,0:T(8,128)(2,1)}, u32[]{:S(2)}, u32[]{:S(2)}) collective-permute-start(bf16[1,320,1024]{2,1,0:T(8,128)(2,1)} %get-tuple-element.178), channel_id=1, source_target_pairs={{0,20},{4,24},{8,28},{12,0},{16,4},{20,8},{24,12},{28,16},{1,21},{... | collective-permute-start | bytes 1966088 | tf_op jit(solution)/shard_map/ppermute | solution.py:555
  1333.6 59.8 %psum.7 = f32[9728]{0:T(1024)S(1)} all-reduce(f32[9728]{0:T(1024)S(1)} %pad_maximum_fusion.8), channel_id=1, replica_groups=mesh['dp'=8,'state'=4] {'dp','state'}, use_global_device_ids=true, to_apply=%region_36.37 | all-reduce | flops 9728 | bytes 77824 | tf_op jit(solution)/shard_map/psum | solution.py:824
  1412.7 59.6 %multiply_reduce_fusion = (f32[]{:T(128)}, f32[320,8000]{1,0:T(8,128)}) fusion(bf16[320,8192]{1,0:T(8,128)(2,1)} %bitcast.339, s32[8192]{0:T(1024)S(1)} %bitcast.375, bf16[320,8192]{1,0:T(8,128)(2,1)} %bitcast.337), kind=kOutput, calls=%fused_computation.23 | convolution fusion | flops 42018816000 | bytes 20635652 | tf_op jit(solution)/shard_map/dot_general | solution.py:102
  1514.7 29.6 %add_multiply_fusion = (f32[1,5,64,8000]{3,2,1,0:T(8,128)}, f32[1,5,64,8000]{3,2,1,0:T(8,128)}, f32[1,5,64,8000]{3,2,1,0:T(8,128)}, f32[1,5,64,8000]{3,2,1,0:T(8,128)}) fusion(f32[1,5,64,8000]{3,2,1,0:T(8,128)} %param.40, f32[5]{0:T(128)S(1)} %copy-done.92, f32[1,5,64,8000]{3,2,1,0:T(8,128)} %param.28, f32[1,5,64,8000]{3,2,1,0:T(8,128)} %bitcast.316, ...), kind=kLoop, calls=%fused_computation.21 | loop fusion | flops 51200000 | bytes 92160016 | tf_op jit(solution)/shard_map/mul | solution.py:93
  1561.4 14.7 add_multiply_fusion.1
  (570 shorter events, 613.1 us)
Async XLA Ops:
  31.2 287.1 %all-gather.3.cloned.1.call-start = ((), (), s32[]{:S(2)}) async-start(), calls=%async_computation.6 | async-start | bytes 11796480 | tf_op jit(solution)/shard_map/all_gather | solution.py:662
  51.6 478.2 %reduce-scatter.6.cloned.1.call-start = ((), (), s32[]{:S(2)}) async-start(), calls=%async_computation.7 | async-start | bytes 1638400 | tf_op jit(solution)/shard_map/reduce_scatter | solution.py:126
  63.0 352.3 %collective-permute-start = (bf16[1,320,528]{1,2,0:T(8,128)(2,1)}, bf16[1,320,528]{1,2,0:T(8,128)(2,1)}, u32[]{:S(2)}, u32[]{:S(2)}) collective-permute-start(bf16[1,320,528]{1,2,0:T(8,128)(2,1)} %get-tuple-element.211), channel_id=1, source_target_pairs={{0,4},{4,8},{8,12},{12,16},{16,20},{20,24},{24,28},{28,0},{1,5},{5... | collective-permute-start | bytes 1013768 | tf_op jit(solution)/shard_map/ppermute | solution.py:555
  65.2 353.0 %collective-permute-start.1 = (bf16[1,320,528]{1,2,0:T(8,128)(2,1)}, bf16[1,320,528]{1,2,0:T(8,128)(2,1)}, u32[]{:S(2)}, u32[]{:S(2)}) collective-permute-start(bf16[1,320,528]{1,2,0:T(8,128)(2,1)} %get-tuple-element.210), channel_id=1, source_target_pairs={{0,8},{4,12},{8,16},{12,20},{16,24},{20,28},{24,0},{28,4},{1,9},{5... | collective-permute-start | bytes 1013768 | tf_op jit(solution)/shard_map/ppermute | solution.py:555
  66.8 359.9 %collective-permute-start.2 = (bf16[1,320,528]{1,2,0:T(8,128)(2,1)}, bf16[1,320,528]{1,2,0:T(8,128)(2,1)}, u32[]{:S(2)}, u32[]{:S(2)}) collective-permute-start(bf16[1,320,528]{1,2,0:T(8,128)(2,1)} %get-tuple-element.209), channel_id=1, source_target_pairs={{0,12},{4,16},{8,20},{12,24},{16,28},{20,0},{24,4},{28,8},{1,13},{... | collective-permute-start | bytes 1013768 | tf_op jit(solution)/shard_map/ppermute | solution.py:555
  69.3 359.1 %collective-permute-start.3 = (bf16[1,320,528]{1,2,0:T(8,128)(2,1)}, bf16[1,320,528]{1,2,0:T(8,128)(2,1)}, u32[]{:S(2)}, u32[]{:S(2)}) collective-permute-start(bf16[1,320,528]{1,2,0:T(8,128)(2,1)} %get-tuple-element.208), channel_id=1, source_target_pairs={{0,16},{4,20},{8,24},{12,28},{16,0},{20,4},{24,8},{28,12},{1,17},{... | collective-permute-start | bytes 1013768 | tf_op jit(solution)/shard_map/ppermute | solution.py:555
  70.5 363.0 %collective-permute-start.4 = (bf16[1,320,528]{1,2,0:T(8,128)(2,1)}, bf16[1,320,528]{1,2,0:T(8,128)(2,1)}, u32[]{:S(2)}, u32[]{:S(2)}) collective-permute-start(bf16[1,320,528]{1,2,0:T(8,128)(2,1)} %get-tuple-element.207), channel_id=1, source_target_pairs={{0,20},{4,24},{8,28},{12,0},{16,4},{20,8},{24,12},{28,16},{1,21},{... | collective-permute-start | bytes 1013768 | tf_op jit(solution)/shard_map/ppermute | solution.py:555
  368.3 607.9 %reduce-scatter.8.cloned.1.call-start = ((), (), s32[]{:S(2)}) async-start(), calls=%async_computation.8 | async-start | bytes 6553600 | tf_op jit(solution)/shard_map/reduce_scatter | solution.py:126
  433.5 71.5 %collective-permute-start.9 = (bf16[1,320,1024]{2,1,0:T(8,128)(2,1)}, bf16[1,320,1024]{2,1,0:T(8,128)(2,1)}, u32[]{:S(2)}, u32[]{:S(2)}) collective-permute-start(bf16[1,320,1024]{2,1,0:T(8,128)(2,1)} %bitcast.364), channel_id=1, source_target_pairs={{0,12},{4,16},{8,20},{12,24},{16,28},{20,0},{24,4},{28,8},{1,13},{... | collective-permute-start | bytes 1966088 | tf_op jit(solution)/shard_map/ppermute | solution.py:555
  436.7 75.4 %collective-permute-start.10 = (bf16[1,320,1024]{2,1,0:T(8,128)(2,1)}, bf16[1,320,1024]{2,1,0:T(8,128)(2,1)}, u32[]{:S(2)}, u32[]{:S(2)}) collective-permute-start(bf16[1,320,1024]{2,1,0:T(8,128)(2,1)} %bitcast.363), channel_id=1, source_target_pairs={{0,16},{4,20},{8,24},{12,28},{16,0},{20,4},{24,8},{28,12},{1,17},{... | collective-permute-start | bytes 1966088 | tf_op jit(solution)/shard_map/ppermute | solution.py:555
  459.5 54.6 %collective-permute-start.11 = (bf16[1,320,1024]{2,1,0:T(8,128)(2,1)}, bf16[1,320,1024]{2,1,0:T(8,128)(2,1)}, u32[]{:S(2)}, u32[]{:S(2)}) collective-permute-start(bf16[1,320,1024]{2,1,0:T(8,128)(2,1)} %bitcast.362), channel_id=1, source_target_pairs={{0,20},{4,24},{8,28},{12,0},{16,4},{20,8},{24,12},{28,16},{1,21},{... | collective-permute-start | bytes 1966088 | tf_op jit(solution)/shard_map/ppermute | solution.py:555
  924.1 473.3 %all-gather.5.cloned.1.call-start = ((), (), s32[]{:S(2)}) async-start(), calls=%async_computation.9 | async-start | bytes 6553600 | tf_op jit(solution)/shard_map/all_gather | solution.py:122
  1019.1 384.0 %reduce-scatter.10.cloned.1.call-start = ((), (), s32[]{:S(2)}) async-start(), calls=%async_computation.10 | async-start | bytes 11796480
  1082.7 71.9 %collective-permute-start.18 = (bf16[1,320,528]{2,1,0:T(8,128)(2,1)}, bf16[1,320,528]{2,1,0:T(8,128)(2,1)}, u32[]{:S(2)}, u32[]{:S(2)}) collective-permute-start(bf16[1,320,528]{2,1,0:T(8,128)(2,1)} %get-tuple-element.201), channel_id=1, source_target_pairs={{0,20},{4,24},{8,28},{12,0},{16,4},{20,8},{24,12},{28,16},{1,21},{... | collective-permute-start | bytes 1013768 | tf_op jit(solution)/shard_map/ppermute | solution.py:555
  1098.3 82.5 %collective-permute-start.16 = (bf16[1,320,528]{2,1,0:T(8,128)(2,1)}, bf16[1,320,528]{2,1,0:T(8,128)(2,1)}, u32[]{:S(2)}, u32[]{:S(2)}) collective-permute-start(bf16[1,320,528]{2,1,0:T(8,128)(2,1)} %get-tuple-element.198), channel_id=1, source_target_pairs={{0,12},{4,16},{8,20},{12,24},{16,28},{20,0},{24,4},{28,8},{1,13},{... | collective-permute-start | bytes 1013768 | tf_op jit(solution)/shard_map/ppermute | solution.py:555
  1100.1 104.1 %collective-permute-start.17 = (bf16[1,320,528]{2,1,0:T(8,128)(2,1)}, bf16[1,320,528]{2,1,0:T(8,128)(2,1)}, u32[]{:S(2)}, u32[]{:S(2)}) collective-permute-start(bf16[1,320,528]{2,1,0:T(8,128)(2,1)} %get-tuple-element.199), channel_id=1, source_target_pairs={{0,16},{4,20},{8,24},{12,28},{16,0},{20,4},{24,8},{28,12},{1,17},{... | collective-permute-start | bytes 1013768 | tf_op jit(solution)/shard_map/ppermute | solution.py:555
  1122.6 102.5 %collective-permute-start.19 = (bf16[1,320,528]{2,1,0:T(8,128)(2,1)}, bf16[1,320,528]{2,1,0:T(8,128)(2,1)}, u32[]{:S(2)}, u32[]{:S(2)}) collective-permute-start(bf16[1,320,528]{2,1,0:T(8,128)(2,1)} %get-tuple-element.200), channel_id=1, source_target_pairs={{0,24},{4,28},{8,0},{12,4},{16,8},{20,12},{24,16},{28,20},{1,25},{... | collective-permute-start | bytes 1013768 | tf_op jit(solution)/shard_map/ppermute | solution.py:555
  1127.3 103.2 %collective-permute-start.20 = (bf16[1,320,528]{2,1,0:T(8,128)(2,1)}, bf16[1,320,528]{2,1,0:T(8,128)(2,1)}, u32[]{:S(2)}, u32[]{:S(2)}) collective-permute-start(bf16[1,320,528]{2,1,0:T(8,128)(2,1)} %get-tuple-element.194), channel_id=1, source_target_pairs={{0,28},{4,0},{8,4},{12,8},{16,12},{20,16},{24,20},{28,24},{1,29},{... | collective-permute-start | bytes 1013768 | tf_op jit(solution)/shard_map/ppermute | solution.py:555
  1154.6 123.3 %collective-permute-start.21 = (bf16[1,320,1024]{2,1,0:T(8,128)(2,1)}, bf16[1,320,1024]{2,1,0:T(8,128)(2,1)}, u32[]{:S(2)}, u32[]{:S(2)}) collective-permute-start(bf16[1,320,1024]{2,1,0:T(8,128)(2,1)} %get-tuple-element.182), channel_id=1, source_target_pairs={{0,4},{4,8},{8,12},{12,16},{16,20},{20,24},{24,28},{28,0},{1,5},{5... | collective-permute-start | bytes 1966088 | tf_op jit(solution)/shard_map/ppermute | solution.py:555
  1180.7 113.4 %collective-permute-start.22 = (bf16[1,320,1024]{2,1,0:T(8,128)(2,1)}, bf16[1,320,1024]{2,1,0:T(8,128)(2,1)}, u32[]{:S(2)}, u32[]{:S(2)}) collective-permute-start(bf16[1,320,1024]{2,1,0:T(8,128)(2,1)} %get-tuple-element.181), channel_id=1, source_target_pairs={{0,8},{4,12},{8,16},{12,20},{16,24},{20,28},{24,0},{28,4},{1,9},{5... | collective-permute-start | bytes 1966088 | tf_op jit(solution)/shard_map/ppermute | solution.py:555
  1204.2 94.2 %collective-permute-start.23 = (bf16[1,320,1024]{2,1,0:T(8,128)(2,1)}, bf16[1,320,1024]{2,1,0:T(8,128)(2,1)}, u32[]{:S(2)}, u32[]{:S(2)}) collective-permute-start(bf16[1,320,1024]{2,1,0:T(8,128)(2,1)} %get-tuple-element.180), channel_id=1, source_target_pairs={{0,12},{4,16},{8,20},{12,24},{16,28},{20,0},{24,4},{28,8},{1,13},{... | collective-permute-start | bytes 1966088 | tf_op jit(solution)/shard_map/ppermute | solution.py:555
  1225.0 75.3 %collective-permute-start.24 = (bf16[1,320,1024]{2,1,0:T(8,128)(2,1)}, bf16[1,320,1024]{2,1,0:T(8,128)(2,1)}, u32[]{:S(2)}, u32[]{:S(2)}) collective-permute-start(bf16[1,320,1024]{2,1,0:T(8,128)(2,1)} %get-tuple-element.179), channel_id=1, source_target_pairs={{0,16},{4,20},{8,24},{12,28},{16,0},{20,4},{24,8},{28,12},{1,17},{... | collective-permute-start | bytes 1966088 | tf_op jit(solution)/shard_map/ppermute | solution.py:555
  1230.5 83.3 %collective-permute-start.25 = (bf16[1,320,1024]{2,1,0:T(8,128)(2,1)}, bf16[1,320,1024]{2,1,0:T(8,128)(2,1)}, u32[]{:S(2)}, u32[]{:S(2)}) collective-permute-start(bf16[1,320,1024]{2,1,0:T(8,128)(2,1)} %get-tuple-element.178), channel_id=1, source_target_pairs={{0,20},{4,24},{8,28},{12,0},{16,4},{20,8},{24,12},{28,16},{1,21},{... | collective-permute-start | bytes 1966088 | tf_op jit(solution)/shard_map/ppermute | solution.py:555
  1409.2 66.0 %all-to-all-start.1 = ((bf16[4,640,4,32]{1,3,2,0:T(8,128)(2,1)}), bf16[4,640,4,32]{1,3,2,0:T(8,128)(2,1)S(1)}, u32[]{:S(2)}, u32[]{:S(2)}) async-start(bf16[4,640,4,32]{1,3,2,0:T(8,128)(2,1)} %copy.408), calls=%async_computation.2 | async-start | bytes 1310720 | tf_op jit(solution)/shard_map/all_to_all | solution.py:804
  (136 other events, 2621.4 us)
Sparse Core Ops, SparseCore 0:
  51.8 225.9 all-gather.2
  368.4 31.4 reduce-scatter.5
  924.2 51.9 reduce-scatter.7
  1019.2 39.1 all-gather.4
  1061.9 335.5 reduce-scatter.9

commit v2 on v1

--- a/solution.py
+++ b/solution.py
@@ -39,7 +39,7 @@
     return key_gate, log_forget
 
 
-def slot_mixer(query, key_gate, log_forget, values, pick, allowed, heads):
+def slot_mixer(query, key_gate, log_forget, values, pick, allowed, heads, key_part):
     slots = query.shape[0]
     tokens = key_gate.shape[0]
     blocks = tokens // GROUP
@@ -57,9 +57,11 @@
     at_slots = jnp.dot(pick, along, precision=FULL_PRECISION)
     key_decay = key_gate * jnp.exp(total[:, None] - inside).reshape(tokens, -1)
     grown = query[None] * jnp.exp(jnp.minimum(at_slots[None] - ends[:, None], 16.0))
-    grown = grown.reshape(blocks, slots, heads, KEY_DIM)
-    key_decay = key_decay.reshape(blocks, GROUP, heads, KEY_DIM)
-    scores = jnp.einsum("bnhk,bghk->hnbg", grown, key_decay, precision=FULL_PRECISION)
+    key_decay = key_decay.reshape(blocks, GROUP, heads * KEY_DIM)
+    column = jnp.arange(heads * KEY_DIM)
+    of_head = (column % key_part) // (key_part // heads) == jnp.arange(heads)[:, None]
+    grown = jnp.where(of_head[:, None, None], grown[None], 0.0)
+    scores = jnp.einsum("hbnk,bgk->hnbg", grown, key_decay, precision=FULL_PRECISION)
     scores = jnp.where(allowed[None], scores.reshape(heads, slots, tokens), 0.0)
     mixed = jnp.einsum(
         "hns,shv->nhv", scores, values.reshape(tokens, heads, VAL_DIM), precision=FULL_PRECISION
@@ -110,9 +112,10 @@
     )
 
 
-def swiglu(joined):
-    half_width = joined.shape[1] // 2
-    return jax.nn.silu(joined[:, :half_width]) * joined[:, half_width:]
+def swiglu(joined, units, cols):
+    gate = joined[:, :units]
+    up = joined[:, units : 2 * units]
+    return jnp.pad(jax.nn.silu(gate) * up, ((0, 0), (0, cols - units)))
 
 
 EVERY = ("dp", "state")
@@ -159,6 +162,11 @@
         made.start()
         self.open.append(made)
         return made
+
+    def settle(self, copies):
+        for made in copies:
+            made.wait_send()
+        self.open = [made for made in self.open if not any(made is one for one in copies)]
 
     def finish(self):
         for made in self.open:
@@ -223,12 +231,17 @@
 
 
 def gather_all_kernel(nd, ns, in_ref, out_ref, sends, recvs):
+    greet(near_peers(nd, ns))
+    links = Links(sends, recvs)
+    gather_body(nd, ns, links, in_ref, out_ref)
+    links.finish()
+
+
+def gather_body(nd, ns, links, in_ref, out_ref):
     dp, st, z, y, x, c = places(nd, ns)
     deep, across = nd // 2, ns // 2
     half = in_ref.shape[1] // 2
     cols = (pl.ds(0, half), pl.ds(half, half))
-    greet(near_peers(nd, ns))
-    links = Links(sends, recvs)
     to_y = (dp + 1 - 2 * y, st)
     to_core = (dp, st + 1 - 2 * c)
     other_y = 1 - y
@@ -286,14 +299,19 @@
         arriving.append(send(from_x, other_y, 1, to_core))
     for made in arriving:
         made.wait_recv()
-    links.finish()
+    links.settle(first + [a_y, b_y] + b_x + a_x + a_xy + b_xy + arriving)
+
+
+def gather_copies(nd, ns):
+    deep, across = nd // 2, ns // 2
+    return 2 * (deep - 1) + 2 + 4 * (across - 1) + 4 * across
 
 
 def gather_all(values, number):
     nd, ns = lax.axis_size("dp"), lax.axis_size("state")
     rows, wide = values.shape
     deep, across = nd // 2, ns // 2
-    copies = 2 * (deep - 1) + 2 + 4 * (across - 1) + 4 * across
+    copies = gather_copies(nd, ns)
     vmem = pl.BlockSpec(memory_space=pltpu.VMEM)
     out = pl.pallas_call(
         functools.partial(gather_all_kernel, nd, ns),
@@ -308,15 +326,20 @@
     return out.reshape(nd * ns * rows, wide)
 
 
-def scatter_all_kernel(
-    nd, ns, in_ref, out_ref, rc, acc, rx_a, ry_a, rz_a, ry_b, rx_b, rz_b, sends, recvs
-):
+def scatter_all_kernel(nd, ns, in_ref, out_ref, *scratch):
+    sends, recvs = scratch[-2:]
+    greet(near_peers(nd, ns))
+    links = Links(sends, recvs)
+    scatter_body(nd, ns, links, in_ref, out_ref, scratch[:-2])
+    links.finish()
+
+
+def scatter_body(nd, ns, links, in_ref, out_ref, scratch, meanwhile=None):
+    rc, acc, rx_a, ry_a, rz_a, ry_b, rx_b, rz_b = scratch
     dp, st, z, y, x, c = places(nd, ns)
     deep, across = nd // 2, ns // 2
     half = in_ref.shape[5] // 2
     cols = (pl.ds(0, half), pl.ds(half, half))
-    greet(near_peers(nd, ns))
-    links = Links(sends, recvs)
     to_y = (dp + 1 - 2 * y, st)
     to_core = (dp, st + 1 - 2 * c)
     ys = (y, 1 - y)
@@ -356,6 +379,8 @@
 
         return acc.at[x_at(k), ys[ky], :, :, cols[part]]
 
+    if meanwhile is not None:
+        meanwhile()
     a_x, b_y = {}, {}
     for k in range(1, across):
         for ky in (1, 0):
@@ -401,15 +426,37 @@
             made[k - 1].wait_recv()
             found += land[k - 1].astype(jnp.float32)
         out_ref[:, cols[part]] = found
-    links.finish()
+    links.settle(
+        list(core.values()) + list(a_x.values()) + list(b_y.values()) + list(b_x.values())
+        + [a_y] + a_z + b_z
+    )
+
+
+def scatter_copies(nd, ns):
+    deep, across = nd // 2, ns // 2
+    return 4 * across + 2 * (across - 1) + across + 1 + (across - 1) + 2 * (deep - 1)
+
+
+def scatter_scratch(nd, ns, rows, wide, kind):
+    deep, across = nd // 2, ns // 2
+    half = wide // 2
+    return [
+        pltpu.VMEM((across, 2, deep, rows, wide), kind),
+        pltpu.VMEM((across, 2, deep, rows, wide), kind),
+        pltpu.VMEM((across - 1, 2, deep, rows, half), kind),
+        pltpu.VMEM((deep, rows, half), kind),
+        pltpu.VMEM((deep - 1, rows, half), kind),
+        pltpu.VMEM((across, deep, rows, half), kind),
+        pltpu.VMEM((across - 1, deep, rows, half), kind),
+        pltpu.VMEM((deep - 1, rows, half), kind),
+    ]
 
 
 def scatter_all(values, number):
     nd, ns = lax.axis_size("dp"), lax.axis_size("state")
     deep, across = nd // 2, ns // 2
     rows, wide = values.shape[0] // (nd * ns), values.shape[1]
-    half = wide // 2
-    copies = 4 * across + 2 * (across - 1) + across + 1 + (across - 1) + 2 * (deep - 1)
+    copies = scatter_copies(nd, ns)
     vmem = pl.BlockSpec(memory_space=pltpu.VMEM)
     kind = values.dtype
     return pl.pallas_call(
@@ -417,36 +464,145 @@
         out_shape=jax.ShapeDtypeStruct((rows, wide), jnp.float32),
         in_specs=[vmem],
         out_specs=vmem,
-        scratch_shapes=[
-            pltpu.VMEM((across, 2, deep, rows, wide), kind),
-            pltpu.VMEM((across, 2, deep, rows, wide), kind),
-            pltpu.VMEM((across - 1, 2, deep, rows, half), kind),
-            pltpu.VMEM((deep, rows, half), kind),
-            pltpu.VMEM((deep - 1, rows, half), kind),
-            pltpu.VMEM((across, deep, rows, half), kind),
-            pltpu.VMEM((across - 1, deep, rows, half), kind),
-            pltpu.VMEM((deep - 1, rows, half), kind),
-            pltpu.SemaphoreType.DMA((copies,)),
-            pltpu.SemaphoreType.DMA((copies,)),
-        ],
+        scratch_shapes=scatter_scratch(nd, ns, rows, wide, kind)
+        + [pltpu.SemaphoreType.DMA((copies,)), pltpu.SemaphoreType.DMA((copies,))],
         compiler_params=pltpu.CompilerParams(
             collective_id=number, has_side_effects=True, vmem_limit_bytes=40 * 2**20
         ),
     )(values.reshape(2, across, 2, deep, rows, wide))
 
 
-def lookup_kernel(nd, ns, in_ref, out_ref, rc, acc, rx, fin, sends, recvs):
+def front_kernel(
+    nd,
+    ns,
+    depth_used,
+    small_ref,
+    gain_ref,
+    table_ref,
+    keys_ref,
+    rest_ref,
+    parts_ref,
+    small_out,
+    gain_out,
+    rows_out,
+    keys_out,
+    rest_out,
+    parts_out,
+    looked,
+    rc,
+    acc,
+    rx,
+    fin,
+    sums,
+    sends,
+    recvs,
+    local,
+):
     dp, st, z, y, x, c = places(nd, ns)
-    across = ns // 2
-    own = in_ref.shape[0]
-    tokens = in_ref.shape[1] // nd
+    deep, across = nd // 2, ns // 2
+    own = table_ref.shape[0]
+    tokens = rows_out.shape[1]
     part = tokens // ns
     to_core = (dp, st + 1 - 2 * c)
-    peers = [(lax.rem(dp + k, nd), st) for k in range(1, nd)]
-    peers += [(dp, lax.rem(x + k, across) * 2 + c) for k in range(1, across)]
-    peers.append(to_core)
-    greet(peers)
+    to_y = (dp + 1 - 2 * y, st)
+    other_y = dp + 1 - 2 * y
+    dp_peers = [(lax.rem(dp + k, nd), st) for k in range(1, nd)]
+    state_peers = [(dp, lax.rem(st + k, ns)) for k in range(1, ns)]
+    greet(dp_peers + state_peers)
     links = Links(sends, recvs)
+
+    ids_made = {}
+    small_out[dp] = small_ref[...]
+    gain_out[dp] = gain_ref[...]
+    for k in range(1, nd):
+        ids_made[k] = links.copy(small_ref, small_out.at[dp], *dp_peers[k - 1])
+    gain_made = [links.copy(gain_ref, gain_out.at[dp], *peer) for peer in dp_peers]
+
+    here = [
+        pltpu.make_async_copy(keys_ref.at[st], keys_out.at[st, dp], local.at[0]),
+        pltpu.make_async_copy(rest_ref, rest_out.at[dp], local.at[1]),
+        pltpu.make_async_copy(parts_ref.at[dp], parts_out.at[dp], local.at[2]),
+    ]
+    for made in here:
+        made.start()
+    key_made = [
+        links.copy(keys_ref.at[peer[1]], keys_out.at[st, dp], *peer) for peer in state_peers
+    ]
+
+    class Gather:
+        def __init__(self, view):
+            self.view = view
+            self.base = links.used
+            links.used += 2 * (deep - 1) + 1 + 2 * (deep - 1)
+
+        def copy(self, number, owner, place):
+            return pltpu.make_async_remote_copy(
+                src_ref=self.view(owner),
+                dst_ref=self.view(owner),
+                send_sem=sends.at[self.base + number],
+                recv_sem=recvs.at[self.base + number],
+                device_id=place,
+                device_id_type=MESH,
+            )
+
+        def pass_on(self, way, step):
+            behind = z - way * step
+            ahead = z + way
+            number = step if way > 0 else deep - 1 + step
+
+            def go(made):
+                @pl.when((behind >= 0) & (behind < deep) & (ahead >= 0) & (ahead < deep))
+                def _():
+                    made(self.copy(number, behind * 2 + y, (ahead * 2 + y, st)))
+
+            return go
+
+        def begin(self):
+            self.copy(2 * (deep - 1), dp, to_y).start()
+            for way in (1, -1):
+                self.pass_on(way, 0)(lambda made: made.start())
+
+        def arrive(self, way, step):
+            began = z - way * (step + 1)
+            number = step if way > 0 else deep - 1 + step
+
+            @pl.when((began >= 0) & (began < deep))
+            def _():
+                self.copy(number, began * 2 + y, to_y).wait_recv()
+                self.copy(2 * (deep - 1) + 1 + number, began * 2 + y, to_y).start()
+
+            if step + 1 < deep - 1:
+                self.pass_on(way, step + 1)(lambda made: made.start())
+
+        def finish(self):
+            self.copy(2 * (deep - 1), other_y, to_y).wait_recv()
+            self.copy(2 * (deep - 1), dp, to_y).wait_send()
+            for way in (1, -1):
+                for step in range(deep - 1):
+                    began = z - way * (step + 1)
+                    number = step if way > 0 else deep - 1 + step
+                    self.pass_on(way, step)(lambda made: made.wait_send())
+
+                    @pl.when((began >= 0) & (began < deep))
+                    def _():
+                        made = self.copy(2 * (deep - 1) + 1 + number, began * 2 + y, to_y)
+                        made.wait_send()
+                        made.wait_recv()
+
+    rest = Gather(lambda owner: rest_out.at[owner])
+    keys = Gather(lambda owner: keys_out.at[:, owner])
+    here[1].wait()
+    rest.begin()
+
+    def swap(k):
+        there = lax.rem(dp + k, nd)
+        return links.copy(parts_ref.at[there], parts_out.at[dp], there, st)
+
+    swapped = [swap(k) for k in range(1, nd // 2)]
+    here[0].wait()
+    for made in key_made:
+        made.wait_recv()
+    keys.begin()
 
     def x_at(k):
         return lax.rem(x + k, across)
@@ -455,11 +611,11 @@
         return lax.rem(dp + k, nd)
 
     def block(k, kx, cc):
-        start = row_at(k) * tokens + (x_at(kx) * 2 + cc) * part
-        return in_ref.at[:, pl.ds(pl.multiple_of(start, part), part)]
+        start = (x_at(kx) * 2 + cc) * part
+        return looked.at[k, :, pl.ds(pl.multiple_of(start, part), part)]
 
     def place(owner, share):
-        return out_ref.at[
+        return rows_out.at[
             pl.ds(pl.multiple_of(owner * own, own), own),
             pl.ds(pl.multiple_of(share * part, part), part),
         ]
@@ -473,19 +629,50 @@
                 found += source[rows, :].astype(jnp.float32)
             target[rows, :] = found.astype(target.dtype)
 
+    depth = table_ref.shape[1]
+    piece = min(1024, depth)
+    span = 2 * LANES
+
+    def look(k):
+        row = row_at(k)
+
+        @pl.loop(0, tokens // span)
+        def _(i):
+            ids = jnp.concatenate(
+                [small_out[row, pl.ds(2 * i, 1), :], small_out[row, pl.ds(2 * i + 1, 1), :]],
+                axis=1,
+            )
+            ids = ids - st * depth_used
+            sums[...] = jnp.zeros_like(sums)
+
+            @pl.loop(0, depth // piece)
+            def _(j):
+                number = lax.broadcasted_iota(jnp.int32, (piece, span), 0)
+                hit = jnp.where(number == ids - j * piece, 1.0, 0.0).astype(jnp.bfloat16)
+                cols = pl.ds(pl.multiple_of(j * piece, piece), piece)
+                sums[...] += jnp.dot(
+                    table_ref[:, cols], hit, preferred_element_type=jnp.float32
+                )
+
+            cols = pl.ds(pl.multiple_of(i * span, span), span)
+            looked[k, :, cols] = sums[...].astype(looked.dtype)
+
     turn = list(range(1, nd)) + [0]
     core, across_x, across_dp = {}, {}, {}
-    for k in turn:
+
+    def start_core(k):
         for kx in list(range(1, across)) + [0]:
             core[k, kx] = links.copy(block(k, kx, 1 - c), rc.at[k, kx], *to_core)
-    for k in turn:
+
+    def start_x(k):
         for kx in range(1, across):
             core[k, kx].wait_recv()
             add([block(k, kx, c), rc.at[k, kx]], acc.at[k, kx - 1])
             across_x[k, kx] = links.copy(
                 acc.at[k, kx - 1], rx.at[k, kx - 1], dp, x_at(kx) * 2 + c
             )
-    for k in turn:
+
+    def start_dp(k):
         core[k, 0].wait_recv()
         sources = [block(k, 0, c), rc.at[k, 0]]
         for kx in range(1, across):
@@ -496,8 +683,33 @@
             across_dp[k] = links.copy(fin.at[k - 1], place(dp, st), row_at(k), st)
         else:
             add(sources, place(dp, st))
+
+    chores = []
+    for step in range(deep - 1):
+        for way in (1, -1):
+            chores.append(functools.partial(rest.arrive, way, step))
+    for step in range(deep - 1):
+        for way in (1, -1):
+            chores.append(functools.partial(keys.arrive, way, step))
+    each = -(-len(chores) // nd)
+    for number, k in enumerate(turn):
+        if k:
+            ids_made[nd - k].wait_recv()
+        look(k)
+        start_core(k)
+        if number >= 1:
+            start_x(turn[number - 1])
+        if number >= 2:
+            start_dp(turn[number - 2])
+        for _ in range(each):
+            if number >= 2 and chores:
+                chores.pop(0)()
+    start_x(turn[-1])
+    start_dp(turn[-2])
+    start_dp(turn[-1])
+    swapped += [swap(k) for k in range(nd // 2, nd)]
     later, last = {}, []
-    for k in [0] + list(range(1, nd)):
+    for number, k in enumerate([0] + list(range(1, nd))):
         owner = lax.rem(dp - k + nd, nd)
         if k:
             across_dp[k].wait_recv()
@@ -506,55 +718,274 @@
                 place(owner, st), place(owner, st), dp, x_at(kx) * 2 + c
             )
         last.append(links.copy(place(owner, st), place(owner, st), *to_core))
+        if chores:
+            chores.pop(0)()
     for k in range(nd):
         owner = lax.rem(dp - k + nd, nd)
         for kx in range(1, across):
             later[k, kx].wait_recv()
             share = lax.rem(x - kx + across, across) * 2 + c
             last.append(links.copy(place(owner, share), place(owner, share), *to_core))
-    for made in last:
+    while chores:
+        chores.pop(0)()
+    for made in last + swapped + gain_made:
         made.wait_recv()
+    here[2].wait()
     links.finish()
-
-
-def lookup_rows(values, number):
+    rest.finish()
+    keys.finish()
+
+
+def front(small, gain, table, keys, rest, parts, tokens, vocab, number):
     nd, ns = lax.axis_size("dp"), lax.axis_size("state")
-    across = ns // 2
-    own, total = values.shape
-    tokens = total // nd
+    deep, across = nd // 2, ns // 2
+    own = table.shape[0]
     part = tokens // ns
-    copies = nd * across + nd * (across - 1) + nd - 1 + nd * across + nd * (across - 1)
+    kind = table.dtype
+    copies = 2 * (nd - 1) + ns - 1 + 2 * (4 * (deep - 1) + 1) + nd - 1
+    copies += nd * across + nd * (across - 1) + nd - 1 + nd * across + nd * (across - 1)
     vmem = pl.BlockSpec(memory_space=pltpu.VMEM)
-    kind = values.dtype
+    hbm = pl.BlockSpec(memory_space=pl.ANY)
     return pl.pallas_call(
-        functools.partial(lookup_kernel, nd, ns),
-        out_shape=jax.ShapeDtypeStruct((nd * own, tokens), kind),
-        in_specs=[vmem],
-        out_specs=vmem,
+        functools.partial(front_kernel, nd, ns, vocab),
+        out_shape=[
+            jax.ShapeDtypeStruct((nd,) + small.shape, small.dtype),
+            jax.ShapeDtypeStruct((nd,) + gain.shape, gain.dtype),
+            jax.ShapeDtypeStruct((nd * own, tokens), kind),
+            jax.ShapeDtypeStruct((ns, nd) + keys.shape[1:], kind),
+            jax.ShapeDtypeStruct((nd,) + rest.shape, kind),
+            jax.ShapeDtypeStruct(parts.shape, kind),
+        ],
+        in_specs=[vmem, vmem, vmem, hbm, hbm, hbm],
+        out_specs=[vmem, vmem, vmem, hbm, hbm, hbm],
         scratch_shapes=[
+            pltpu.VMEM((nd, own, tokens), kind),
             pltpu.VMEM((nd, across, own, part), kind),
             pltpu.VMEM((nd, across - 1, own, part), kind),
             pltpu.VMEM((nd, across - 1, own, part), kind),
             pltpu.VMEM((nd - 1, own, part), kind),
+            pltpu.VMEM((own, 2 * LANES), jnp.float32),
             pltpu.SemaphoreType.DMA((copies,)),
             pltpu.SemaphoreType.DMA((copies,)),
+            pltpu.SemaphoreType.DMA((3,)),
         ],
         compiler_params=pltpu.CompilerParams(
-            collective_id=number, has_side_effects=True, vmem_limit_bytes=48 * 2**20
+            collective_id=number, has_side_effects=True, vmem_limit_bytes=52 * 2**20
         ),
-    )(values)
-
-
-def swap_parts(values):
-    nd = lax.axis_size("dp")
-    me = lax.axis_index("dp")
-    mine = lax.dynamic_index_in_dim(values, me, 0)
-    found = lax.dynamic_update_index_in_dim(jnp.zeros_like(values), mine, me, 0)
-    for k in range(1, nd):
-        sent = lax.dynamic_index_in_dim(values, lax.rem(me + k, nd), 0)
-        got = lax.ppermute(sent, "dp", [(i, (i + k) % nd) for i in range(nd)])
-        found = lax.dynamic_update_index_in_dim(found, got, lax.rem(me - k + nd, nd), 0)
-    return found
+        cost_estimate=pl.CostEstimate(
+            flops=2 * table.size * nd * tokens, bytes_accessed=4 * parts.size, transcendentals=0
+        ),
+    )(small, gain, table, keys, rest, parts)
+
+
+def slots_back_kernel(
+    nd,
+    ns,
+    width,
+    units,
+    part_hbm,
+    table_ref,
+    two_ref,
+    one_ref,
+    gain_ref,
+    wd_ref,
+    wgu_ref,
+    gu_ref,
+    hidden_ref,
+    rows_ref,
+    one_out,
+    table_out,
+    ffn_out,
+    gains_out,
+    part_ref,
+    summed,
+    low,
+    down,
+    dgu,
+    dffn,
+    local,
+    *scratch,
+):
+    sends, recvs = scratch[-2:]
+    dp, st, z, y, x, c = places(nd, ns)
+    deep, across = nd // 2, ns // 2
+    count, wide = two_ref.shape
+    every = nd * ns * count
+    dp_peers = [(lax.rem(dp + k, nd), st) for k in range(1, nd)]
+    state_peers = [(dp, lax.rem(st + k, ns)) for k in range(1, ns)]
+    fill = pltpu.make_async_copy(part_hbm, part_ref, local.at[2])
+    fill.start()
+    greet(dp_peers + state_peers)
+    links = Links(sends, recvs)
+    own_copy = pltpu.make_async_copy(table_ref.at[dp], table_out.at[dp], local.at[0])
+    own_copy.start()
+    local_copies = [own_copy]
+    swapped = [
+        links.copy(table_ref.at[peer[0]], table_out.at[dp], *peer) for peer in dp_peers
+    ]
+
+    def norm_back(grad, values, gain, row):
+        mean = jnp.sum(values * values, axis=1, keepdims=True) * (1.0 / width)
+        root = lax.rsqrt(mean + NORM_EPS)
+        scaled = grad * gain
+        inner = jnp.sum(scaled * values, axis=1, keepdims=True) * (1.0 / width)
+        gains_out[pl.ds(row, 1), :] = jnp.sum(grad * values * root, axis=0, keepdims=True)
+        return scaled * root - values * (root * root * root * inner)
+
+    fill.wait()
+    scatter_body(nd, ns, links, part_ref, summed, scratch[:-2])
+    summed[...] = norm_back(summed[...], two_ref[...], gain_ref[pl.ds(1, 1), :], 1)
+    low[...] = summed[...].astype(low.dtype)
+    gather_body(nd, ns, links, low, down)
+
+    inner_cols = gu_ref.shape[1]
+    step = deep * count
+    flat_down = down
+
+    @pl.loop(0, 2 * across * 2)
+    def _(i):
+        cc, rest = lax.div(i, 2 * across), lax.rem(i, 2 * across)
+        xx, yy = lax.div(rest, 2), lax.rem(rest, 2)
+        rows = pl.ds(pl.multiple_of(i * step, step), step)
+        grad = jnp.dot(
+            flat_down[cc, xx, yy].reshape(step, wide),
+            wd_ref[...],
+            preferred_element_type=jnp.float32,
+        )
+        grad = jnp.concatenate(
+            [grad, jnp.zeros((step, inner_cols - grad.shape[1]), jnp.float32)], axis=1
+        ) if inner_cols > grad.shape[1] else grad[:, :inner_cols]
+        gate = gu_ref[rows, :]
+        up = pltpu.roll(gate, inner_cols - units, 1)
+        gated = 1.0 / (1.0 + jnp.exp(-gate))
+        grad_gate = grad * up * (gated * (1.0 + gate * (1.0 - gated)))
+        grad_up = pltpu.roll(grad * gate * gated, units, 1)
+        lanes = lax.broadcasted_iota(jnp.int32, grad_gate.shape, 1)
+        joined = jnp.where(lanes < units, grad_gate, grad_up).astype(dgu.dtype)
+        dgu[rows, :] = joined
+        part_ref[cc, xx, yy] = (
+            lax.dot_general(
+                joined, wgu_ref[...], (((1,), (1,)), ((), ())), preferred_element_type=jnp.float32
+            )
+            .astype(part_ref.dtype)
+            .reshape(deep, count, wide)
+        )
+
+    def weight_grads():
+        span = 2 * LANES
+
+        @pl.loop(0, wide // span)
+        def _(i):
+            cols = pl.ds(pl.multiple_of(i * span, span), span)
+            dffn[cols, :inner_cols] = lax.dot_general(
+                rows_ref[:, cols], dgu[...], (((0,), (0,)), ((), ())),
+                preferred_element_type=jnp.float32,
+            ).astype(dffn.dtype)
+            dffn[cols, inner_cols:] = lax.dot_general(
+                flat_down[:, :, :, :, :, cols].reshape(every, span), hidden_ref[...],
+                (((0,), (0,)), ((), ())),
+                preferred_element_type=jnp.float32,
+            ).astype(dffn.dtype)
+
+        own = ffn_out.shape[1]
+
+        def block(owner):
+            return dffn.at[pl.ds(pl.multiple_of(owner * own, own), own), :]
+
+        mine = pltpu.make_async_copy(block(dp), ffn_out.at[dp], local.at[1])
+        mine.start()
+        swapped.extend(links.copy(block(peer[0]), ffn_out.at[dp], *peer) for peer in dp_peers)
+        local_copies.append(mine)
+
+    grad_two = summed[...]
+    scatter_body(nd, ns, links, part_ref, summed, scratch[:-2], weight_grads)
+    grad_one = grad_two + norm_back(summed[...], one_ref[...], gain_ref[pl.ds(0, 1), :], 0)
+    one_out[st] = grad_one.astype(one_out.dtype)
+    low[...] = grad_one.astype(low.dtype)
+    made = [links.copy(low, one_out.at[st], *peer) for peer in state_peers]
+    for copy in made:
+        copy.wait_recv()
+    for copy in swapped:
+        copy.wait_recv()
+    for copy in local_copies:
+        copy.wait()
+    links.finish()
+
+
+def slots_back(part, table, two, one, gain, wd, wgu, gu, hidden, rows, width, units, number):
+    nd, ns = lax.axis_size("dp"), lax.axis_size("state")
+    deep, across = nd // 2, ns // 2
+    count, wide = two.shape
+    kind = part.dtype
+    own = wide // nd
+    cols = wgu.shape[1] + wd.shape[1]
+    copies = 2 * scatter_copies(nd, ns) + gather_copies(nd, ns) + 2 * (nd - 1) + ns - 1
+    vmem = pl.BlockSpec(memory_space=pltpu.VMEM)
+    hbm = pl.BlockSpec(memory_space=pl.ANY)
+    six = (2, across, 2, deep, count, wide)
+    out = pl.pallas_call(
+        functools.partial(slots_back_kernel, nd, ns, width, units),
+        out_shape=[
+            jax.ShapeDtypeStruct((ns, count, wide), kind),
+            jax.ShapeDtypeStruct(table.shape, kind),
+            jax.ShapeDtypeStruct((nd, own, cols), kind),
+            jax.ShapeDtypeStruct((2, wide), jnp.float32),
+        ],
+        in_specs=[hbm, hbm] + [vmem] * 8,
+        out_specs=[vmem, hbm, hbm, vmem],
+        scratch_shapes=[
+            pltpu.VMEM(six, kind),
+            pltpu.VMEM((count, wide), jnp.float32),
+            pltpu.VMEM((count, wide), kind),
+            pltpu.VMEM(six, kind),
+            pltpu.VMEM((nd * ns * count, wgu.shape[1]), kind),
+            pltpu.VMEM((wide, cols), kind),
+            pltpu.SemaphoreType.DMA((3,)),
+        ]
+        + scatter_scratch(nd, ns, count, wide, kind)
+        + [pltpu.SemaphoreType.DMA((copies,)), pltpu.SemaphoreType.DMA((copies,))],
+        compiler_params=pltpu.CompilerParams(
+            collective_id=number, has_side_effects=True, vmem_limit_bytes=58 * 2**20
+        ),
+        cost_estimate=pl.CostEstimate(
+            flops=8 * rows.size * cols, bytes_accessed=100 * part.size, transcendentals=0
+        ),
+    )(part.reshape(six), table, two, one, gain, wd, wgu, gu, hidden, rows)
+    return (out[0].reshape(ns * count, wide),) + tuple(out[1:])
+
+
+def state_sum_kernel(nd, ns, in_ref, out_ref, land, sends, recvs):
+    dp, st = lax.axis_index("dp"), lax.axis_index("state")
+    peers = [(dp, lax.rem(st + k, ns)) for k in range(1, ns)]
+    greet(peers)
+    links = Links(sends, recvs)
+    made = [
+        links.copy(in_ref.at[there[1]], land.at[k], *there) for k, there in enumerate(peers)
+    ]
+    found = in_ref[st].astype(jnp.float32)
+    for k in range(ns - 1):
+        made[k].wait_recv()
+        found += land[k].astype(jnp.float32)
+    out_ref[...] = found
+    links.finish()
+
+
+def state_sum(values, number):
+    nd, ns = lax.axis_size("dp"), lax.axis_size("state")
+    rows, wide = values.shape[0] // ns, values.shape[1]
+    vmem = pl.BlockSpec(memory_space=pltpu.VMEM)
+    return pl.pallas_call(
+        functools.partial(state_sum_kernel, nd, ns),
+        out_shape=jax.ShapeDtypeStruct((rows, wide), jnp.float32),
+        in_specs=[vmem],
+        out_specs=vmem,
+        scratch_shapes=[
+            pltpu.VMEM((ns - 1, rows, wide), values.dtype),
+            pltpu.SemaphoreType.DMA((ns - 1,)),
+            pltpu.SemaphoreType.DMA((ns - 1,)),
+        ],
+        compiler_params=pltpu.CompilerParams(collective_id=number, has_side_effects=True),
+    )(values.reshape(ns, rows, wide))
 
 
 def on_device(
@@ -619,16 +1050,46 @@
     out_own = lowered(out_weight)
     table_own = lowered(table_weight)
 
-    def in_rows(flat, multiple):
-        flat = jnp.pad(flat, (0, -flat.shape[0] % (multiple * LANES)))
+    def in_rows(flat):
+        flat = jnp.pad(flat, (0, -flat.shape[0] % (16 * LANES)))
         return flat.reshape(-1, LANES)
 
-    small, gains_all = small_gather(
+    key_part = heads * key_share
+    keys_sent = in_own[:, : 2 * key_cols].reshape(own, 2, ns, key_part)
+    keys_sent = keys_sent.transpose(2, 0, 1, 3).reshape(ns, own, 2 * key_part)
+    rest_sent = jnp.concatenate(
+        [in_own[:, 2 * key_cols : mixer_cols], out_own[:, :value_width]], axis=1
+    )
+    table_padded = jnp.pad(table_own, ((0, 0), (0, nd * vocab_part - vocab_share)))
+
+    def by_part(columns, parts):
+        return columns.reshape(own, nd, parts)
+
+    def zeros(parts):
+        return jnp.zeros((own, nd, parts), bf16)
+
+    gu_cols = -(-2 * unit_part // LANES) * LANES
+    down_cols = -(-unit_part // LANES) * LANES
+    parts_sent = jnp.concatenate(
         [
-            in_rows(jnp.concatenate([token_ids[0], loss_targets[0]]), 8),
-            in_rows(gain_weight.astype(bf16).reshape(-1), 16),
+            by_part(table_padded, vocab_part),
+            by_part(in_own[:, mixer_cols : mixer_cols + units], unit_part),
+            by_part(in_own[:, mixer_cols + units :], unit_part),
+            zeros(gu_cols - 2 * unit_part),
+            by_part(out_own[:, value_width:], unit_part),
+            zeros(down_cols - unit_part),
         ],
-        False,
+        axis=2,
+    ).transpose(1, 0, 2)
+    small, gains_all, stream, keys_all, rest_all, parts_all = front(
+        in_rows(jnp.concatenate([token_ids[0], loss_targets[0]])),
+        in_rows(gain_weight.astype(bf16).reshape(-1)),
+        table_padded,
+        keys_sent,
+        rest_sent,
+        parts_sent,
+        tokens,
+        vocab_share,
         1,
     )
     small = small.reshape(nd, -1)
@@ -645,39 +1106,23 @@
     )
     live = (targets_all >= 0).astype(f32)
     count = jnp.sum(live)
-
     local_ids = ids_all.reshape(-1) - me_state * vocab_share
     hit = jnp.arange(vocab_share)[:, None] == local_ids[None, :]
-    looked = times_plain(table_own, hit.astype(bf16)).astype(bf16)
-    stream = lookup_rows(looked, 2)
     stream_mine = lax.dynamic_slice_in_dim(stream, me_state * quarter, quarter, axis=1)
 
-    exchanged = in_own[:, : 2 * key_cols].reshape(own, 2, ns, heads * key_share)
-    exchanged = exchanged.transpose(2, 0, 1, 3).reshape(ns, own * 2, heads, key_share)
-    exchanged = lax.all_to_all(exchanged, "state", split_axis=0, concat_axis=0, tiled=True)
-    exchanged = exchanged.transpose(1, 2, 0, 3).reshape(own, 2 * heads * KEY_DIM)
-    mixer_own = jnp.concatenate(
-        [exchanged, in_own[:, 2 * key_cols : mixer_cols], out_own[:, :value_width]], axis=1
-    )
-    mixer_weights = lax.all_gather(mixer_own, "dp", axis=0, tiled=True)
     qcols = heads * KEY_DIM
-    w_qfv = mixer_weights[:, : 2 * qcols + value_width]
-    w_q = mixer_weights[:, :qcols]
-    w_fv = mixer_weights[:, qcols : 2 * qcols + value_width]
-    w_o = mixer_weights[:, 2 * qcols + value_width :]
-    ffn_own = jnp.stack(
-        [
-            in_own[:, mixer_cols : mixer_cols + units].reshape(own, nd, unit_part),
-            in_own[:, mixer_cols + units :].reshape(own, nd, unit_part),
-            out_own[:, value_width:].reshape(own, nd, unit_part),
-        ],
-        axis=2,
-    ).reshape(own, nd * 3 * unit_part)
-    ffn = swap_parts(spread_columns(ffn_own, nd)).reshape(wide, 3 * unit_part)
-    w_gu = ffn[:, : 2 * unit_part]
-    w_d = ffn[:, 2 * unit_part :]
-    table_padded = jnp.pad(table_own, ((0, 0), (0, nd * vocab_part - vocab_share)))
-    table = swap_parts(spread_columns(table_padded, nd)).reshape(wide, vocab_part)
+    keys_all = keys_all.reshape(ns, wide, 2 * key_part)
+    w_q = keys_all[:, :, :key_part].transpose(1, 0, 2).reshape(wide, qcols)
+    w_f = keys_all[:, :, key_part:].transpose(1, 0, 2).reshape(wide, qcols)
+    rest_all = rest_all.reshape(wide, 2 * value_width)
+    w_v = rest_all[:, :value_width]
+    w_o = rest_all[:, value_width:]
+    w_fv = jnp.concatenate([w_f, w_v], axis=1)
+    w_qfv = jnp.concatenate([w_q, w_fv], axis=1)
+    parts_all = parts_all.reshape(wide, -1)
+    table = parts_all[:, :vocab_part]
+    w_gu = parts_all[:, vocab_part : vocab_part + gu_cols]
+    w_d = parts_all[:, vocab_part + gu_cols :]
 
     positions = loss_positions[0]
     pick_hit = positions[:, None] == jnp.arange(tokens)[None, :]
@@ -704,7 +1149,7 @@
     (key_gate, log_forget), back_gates = jax.vjp(forget_gates, forget_value[:, :qcols])
 
     def mix(query_in, key_in, forget_in, value_in):
-        return slot_mixer(query_in, key_in, forget_in, value_in, pick, allowed, heads)
+        return slot_mixer(query_in, key_in, forget_in, value_in, pick, allowed, heads, key_part)
 
     mixed, back_mix = jax.vjp(
         mix,
@@ -721,18 +1166,17 @@
 
     gated_f, back_head = jax.vjp(head_norm, mixed, head_gain)
     gated = gated_f.astype(bf16)
-    stream_one = stream_at + scatter_state(times_right(gated, w_o))
+    stream_one = stream_at + state_sum(times_right(gated, w_o).astype(bf16), 2)
 
     def wide_norm(values, gain):
         return rms_norm(values, gain, width)
 
-    normed_two, back_two = jax.vjp(wide_norm, stream_one, gains[2])
+    normed_two = wide_norm(stream_one, gains[2])
     rows_two = gather_all(normed_two.astype(bf16), 3)
     gate_up = times_plain(rows_two, w_gu)
-    hidden_f, back_glu = jax.vjp(swiglu, gate_up)
-    hidden = hidden_f.astype(bf16)
+    hidden = swiglu(gate_up, unit_part, down_cols).astype(bf16)
     stream_two = stream_one + scatter_all(times_right(hidden, w_d).astype(bf16), 4)
-    normed_three, back_three = jax.vjp(wide_norm, stream_two, gains[3])
+    normed_three = wide_norm(stream_two, gains[3])
     rows_three = gather_all(normed_three.astype(bf16), 5)
 
     logits = times_plain(rows_three, table)
@@ -752,24 +1196,24 @@
     loss_sum = jnp.sum((lse - jnp.sum(shares[:, 2], axis=0)) * live)
     probs = jnp.exp(logits - lse[:, None])
     dlogits = ((probs - target_hit.astype(f32)) * (live / count)[:, None]).astype(bf16)
-    grad_three = scatter_all(times_right(dlogits, table).astype(bf16), 7)
     grad_table_part = times_left(rows_three, dlogits).astype(bf16)
-    grad_table_own = join_columns(swap_parts(grad_table_part.reshape(nd, own, vocab_part)))
-    grad_table_own = grad_table_own[:, :vocab_share].astype(f32)
-
-    grad_two, grad_gain_four = back_three(grad_three)
-    down_rows = gather_all(grad_two.astype(bf16), 8)
-    grad_hidden = times_plain(down_rows, w_d)
-    grad_down = times_left(down_rows, hidden)
-    (grad_gate_up,) = back_glu(grad_hidden)
-    grad_gate_up = grad_gate_up.astype(bf16)
-    grad_gu = times_left(rows_two, grad_gate_up)
-    grad_norm_two = scatter_all(times_right(grad_gate_up, w_gu).astype(bf16), 9)
-    grad_stream_one, grad_gain_three = back_two(grad_norm_two)
-    grad_one = gather_state((grad_two + grad_stream_one).astype(bf16))
-    grad_ffn = jnp.concatenate([grad_gu, grad_down], axis=1).astype(bf16)
-    grad_ffn = join_columns(swap_parts(grad_ffn.reshape(nd, own, 3 * unit_part)))
-    grad_ffn = grad_ffn.reshape(own, nd, 3, unit_part)
+    grad_one, grad_table_back, grad_ffn, gain_pair = slots_back(
+        times_right(dlogits, table).astype(bf16),
+        grad_table_part.reshape(nd, own, vocab_part),
+        stream_two,
+        stream_one,
+        gains[2:],
+        w_d,
+        w_gu,
+        gate_up,
+        hidden,
+        rows_two,
+        width,
+        unit_part,
+        7,
+    )
+    grad_gain_three, grad_gain_four = gain_pair
+    grad_table_own = join_columns(grad_table_back)[:, :vocab_share].astype(f32)
 
     grad_gated = times_plain(grad_one, w_o)
     grad_w_o = times_left(grad_one, gated)
@@ -797,33 +1241,36 @@
     embed = swap_dp(grad_zero.reshape(nd, own, quarter))
     embed = gather_state(embed, 2).transpose(1, 0, 2).reshape(own, nd * tokens)
     grad_lookup = times_right(embed, hit.astype(bf16))
+    grad_mixer_own, grad_lookup = lax.optimization_barrier((grad_mixer_own, grad_lookup))
     own_table = grad_table_own + grad_lookup
 
-    returned = grad_mixer_own[:, : 2 * qcols].reshape(own * 2, heads, ns, key_share)
-    returned = returned.transpose(2, 0, 1, 3)
-    returned = lax.all_to_all(returned, "state", split_axis=0, concat_axis=0, tiled=True)
-    returned = returned.reshape(ns, own, 2, heads * key_share).transpose(1, 2, 0, 3)
-    returned = returned.reshape(own, 2 * key_cols)
+    grad_keys = grad_mixer_own[:, : 2 * qcols].reshape(own, 2, ns, key_part)
+    grad_keys = grad_keys.transpose(2, 0, 1, 3).reshape(ns, own, 2 * key_part)
+    grad_keys = lax.all_to_all(grad_keys, "state", split_axis=0, concat_axis=0, tiled=True)
+    grad_keys = grad_keys.reshape(ns, own, 2, key_part).transpose(1, 2, 0, 3)
+    grad_gate = grad_ffn[:, :, :unit_part]
+    grad_up = grad_ffn[:, :, unit_part : 2 * unit_part]
+    grad_down = grad_ffn[:, :, gu_cols : gu_cols + unit_part]
     own_in = jnp.concatenate(
         [
-            returned,
+            grad_keys.reshape(own, 2 * key_cols),
             grad_mixer_own[:, 2 * qcols : 2 * qcols + value_width],
-            grad_ffn[:, :, 0].reshape(own, units),
-            grad_ffn[:, :, 1].reshape(own, units),
+            join_columns(grad_gate),
+            join_columns(grad_up),
         ],
         axis=1,
     ).astype(f32)
     own_out = jnp.concatenate(
-        [grad_mixer_own[:, 2 * qcols + value_width :], grad_ffn[:, :, 2].reshape(own, units)],
+        [grad_mixer_own[:, 2 * qcols + value_width :], join_columns(grad_down)],
         axis=1,
     ).astype(f32)
 
     head_full = lax.dynamic_update_slice_in_dim(
         jnp.zeros((width,), f32), grad_gain_two, me_state * value_width, 0
     )
-    gain_sums = lax.psum(
-        jnp.concatenate([grad_gain_one, grad_gain_three, grad_gain_four, head_full]), EVERY
-    )
+    gain_parts = jnp.concatenate([grad_gain_one, grad_gain_three, grad_gain_four, head_full])
+    gain_parts = small_gather([in_rows(gain_parts.astype(bf16))], True, 11)[0]
+    gain_sums = jnp.sum(gain_parts.reshape(nd * ns, -1)[:, : 3 * wide + width].astype(f32), axis=0)
     head_slots = (
         jnp.zeros((nd * capacity, block_rows), f32)
         .at[index]

time: 1600 us -> 1470 us (0.919)
  Pallas kernels: 472 us -> 796 us
  starting transfers between devices: 165 us -> 4.98 us
  local copies, waits for them, and re-layouts: 274 us -> 147 us
  blocking collectives: 104 us -> 37 us
  matrix products: 242 us -> 183 us
  waiting for transfers between devices: 175 us -> 127 us
    pallas_call x1 -> x3, Pallas kernels: 67.8 us -> 588 us  [the longest x1 290 us: front(): pl.pallas_call(functools.partial(front_kernel, nd, ns, vocab), out_shape=...]
    ppermute x28 -> x0, starting transfers between devices: 157 us -> none  [swap_parts(): got = lax.ppermute(sent, 'dp', [(i, (i + k) % nd) for i in range(nd)])]
    ppermute x28 -> x0, waiting for transfers between devices: 118 us -> none  [swap_parts(): got = lax.ppermute(sent, 'dp', [(i, (i + k) % nd) for i in range(nd)])]
    pallas_call x3 -> x1, Pallas kernels: 137 us -> 49.2 us  [scatter_all(): pl.pallas_call(functools.partial(scatter_all_kernel, nd, ns), out_shape=j...]
    unnamed x6 -> x4, waiting for transfers between devices: 0.08 us -> 75.6 us
    pallas_call x3, Pallas kernels: 126 us -> 51.7 us  [small_gather(): pl.pallas_call(functools.partial(small_gather_kernel, nd, ns, everyone, l...]
    psum x1 -> x0, blocking collectives: 59.8 us -> none  [on_device(): lax.psum(jnp.concatenate([grad_gain_one, grad_gain_three, grad_gain_four,...]
    dynamic_update_slice x32 -> x0, local copies, waits for them, and re-layouts: 46.7 us -> none  [the longest x29 44.6 us: swap_parts(): lax.dynamic_update_index_in_dim(found, got, lax.rem(me - k + nd, nd), 0)]
  transfers between devices with their start and end apart: 35 -> 4, of which waited for: 13 -> 3; matrix products, arithmetic and copies ran while one was open for 26% -> 9% of each run, Pallas kernels for 10% -> 2%
where the time goes in v2:
time: 1470 us; the launch traced here: 1460 us
  Pallas kernels  796 us (54%)
  matrix products  183 us (12%)
  local copies, waits for them, and re-layouts  147 us (10%)
  other arithmetic  144 us (10%)
  waiting for transfers between devices  127 us (9%)
  blocking collectives  37 us (3%)
  between operations  22.7 us (2%)
    pallas_call x1, Pallas kernels, front(): pl.pallas_call(functools.partial(front_kernel, nd, ns, vocab), out_shape=...  290 us
    pallas_call x1, Pallas kernels, slots_back(): pl.pallas_call(functools.partial(slots_back_kernel, nd, ns, width, units)...  288 us
    pallas_call x2, Pallas kernels, gather_all(): pl.pallas_call(functools.partial(gather_all_kernel, nd, ns), out_shape=ja...  107 us
    dot_general x6, matrix products, times_right(): lax.dot_general(left, right, (((1,), (1,)), ((), ())), preferred_element_...  90.6 us
    unnamed x4, waiting for transfers between devices  75.6 us
    pallas_call x3, Pallas kernels, small_gather(): pl.pallas_call(functools.partial(small_gather_kernel, nd, ns, everyone, l...  51.7 us
    reduce_scatter x1, waiting for transfers between devices, scatter_state(): return lax.psum_scatter(values, 'state', scatter_dimension=axis, tiled=True)  50.8 us
    pallas_call x1, Pallas kernels, scatter_all(): pl.pallas_call(functools.partial(scatter_all_kernel, nd, ns), out_shape=j...  49.2 us
  transfers between devices with their start and end apart: 4, of which 3 were waited for; matrix products, arithmetic and copies ran while one was open for 9% of the time, Pallas kernels for 2%

profile of v2, /device:TPU:0, one launch (start us, length us, event | category | flops | bytes accessed | tf_op | source)
XLA Modules:
  0.0 1462.0 jit_solution(3523731307615826482)
XLA Ops:
  42.0 14.1 concatenate.76
  56.1 290.2 %shard_map.348 = (s32[8,16,128]{2,1,0:T(8,128)S(1)}, bf16[8,16,128]{2,1,0:T(8,128)(2,1)S(1)}, bf16[2560,1024]{1,0:T(8,128)(2,1)}, bf16[4,8,320,256]{3,2,1,0:T(8,...) custom-call(s32[16,128]{1,0:T(8,128)S(1)} %pad_bitcast_fusion.small_ref, ...), custom_call_target="tpu_custom_call" | custom-call | flops 42949672960 | bytes 17039360 | tf_op jit(solution)/shard_map/pallas_call | solution.py:749
  401.0 9.8 shard_map.349
  415.3 68.0 %shard_map.350 = bf16[2,2,2,4,32,2560]{5,4,3,2,1,0:T(8,128)(2,1)S(1)} custom-call(bf16[32,2560]{1,0:T(8,128)(2,1)S(1)} %multiply_convert_fusion.3.in_ref), custom_call_target="tpu_custom_call" | custom-call | tf_op jit(solution)/shard_map/pallas_call | solution.py:316
  492.7 49.2 %shard_map.351 = f32[32,2560]{1,0:T(8,128)S(1)} custom-call(bf16[2,2,2,4,32,2560]{5,4,3,2,1,0:T(8,128)(2,1)S(1)} %bitcast.257), custom_call_target="tpu_custom_call" | custom-call | tf_op jit(solution)/shard_map/pallas_call | solution.py:462
  544.8 38.9 %shard_map.352 = bf16[2,2,2,4,32,2560]{5,4,3,2,1,0:T(8,128)(2,1)S(1)} custom-call(bf16[32,2560]{1,0:T(8,128)(2,1)S(1)} %multiply_convert_fusion.2.in_ref), custom_call_target="tpu_custom_call" | custom-call | tf_op jit(solution)/shard_map/pallas_call | solution.py:316
  600.4 15.3 %shard_map.353 = f32[32,24,128]{2,1,0:T(8,128)} custom-call(f32[24,128]{1,0:T(8,128)} %reshape.760.refs_0_), custom_call_target="tpu_custom_call" | custom-call | tf_op jit(solution)/shard_map/pallas_call | solution.py:223
  621.0 11.7 convolution_convert_fusion.2
  632.7 11.8 convolution_convert_fusion.3
  656.7 288.1 %shard_map.354 = (bf16[4,32,2560]{2,1,0:T(8,128)(2,1)}, bf16[8,320,1024]{2,1,0:T(8,128)(2,1)}, bf16[8,320,640]{2,1,0:T(8,128)(2,1)}, f32[2,2560]{1,0:T(2,128)}) custom-call(bf16[2,2,2,4,32,2560]{5,4,3,2,1,0:T(8,128)(2,1)} %bitcast.341, bf16[8,320,1024]{2,1,0:T(8,128)(2,1)} %bitcast.340, f32[32,2560]{1,0:T(8,128)} %get-tuple-element.151.two_ref, ...), custom_call_target="tpu_custom_call" | custom-call | flops 13421772800 | bytes 262144000 | tf_op jit(solution)/shard_map/pallas_call | solution.py:926
  984.1 12.8 fusion.18
  999.2 50.8 %reduce-scatter.5.cloned.1.call-done = bf16[2560,256]{1,0:T(8,128)(2,1)} async-done(((bf16[2560,1024]{1,0:T(8,128)(2,1)}), bf16[2560,256]{1,0:T(8,128)(2,1)}) %reduce-scatter.5.cloned.1.call-update) | async-done | bytes 1310736 | tf_op jit(solution)/shard_map/reduce_scatter | solution.py:129
  1055.9 37.0 %all_to_all.10 = bf16[8,320,256]{2,1,0:T(8,128)(2,1)} all-to-all(bf16[8,320,256]{2,1,0:T(8,128)(2,1)S(1)} %bitcast.316), channel_id=1, replica_groups=mesh['dp'=8,'state'=4] {'dp'}, dimensions={0} | all-to-all | bytes 2621440 | tf_op jit(solution)/shard_map/all_to_all | solution.py:133
  1094.4 11.2 convolution_convert_fusion
  1110.3 14.0 copy.288
  1153.5 26.9 %shard_map.356 = bf16[32,80,128]{2,1,0:T(8,128)(2,1)} custom-call(bf16[80,128]{1,0:T(8,128)(2,1)} %fusion.130.refs_0_), custom_call_target="tpu_custom_call" | custom-call | tf_op jit(solution)/shard_map/pallas_call | solution.py:223
  1186.6 55.0 %fusion = f32[320,8000]{1,0:T(8,128)} fusion(bf16[320,8192]{1,0:T(8,128)(2,1)S(1)} %bitcast.289, s32[8192]{0:T(1024)S(1)} %bitcast.327), kind=kOutput, calls=%fused_computation.3 | convolution fusion | flops 42008576000 | bytes 15515648 | tf_op jit(solution)/shard_map/dot_general | solution.py:104
  1241.6 75.6 %reduce-scatter.7.cloned.1.call-done = bf16[320,2048]{1,0:T(8,128)(2,1)} async-done(((bf16[2560,2048]{1,0:T(8,128)(2,1)}), bf16[320,2048]{1,0:T(8,128)(2,1)}) %reduce-scatter.7.cloned.1.call-update) | async-done | bytes 1310736
  1346.0 11.8 multiply_reduce_fusion.1
  1360.4 9.5 shard_map.355
  1372.9 10.5 fusion.17
  1386.0 29.9 %add_multiply_fusion = (f32[1,5,64,8000]{3,2,1,0:T(8,128)}, f32[1,5,64,8000]{3,2,1,0:T(8,128)}, f32[1,5,64,8000]{3,2,1,0:T(8,128)}, f32[1,5,64,8000]{3,2,1,0:T(8,128)}) fusion(f32[1,5,64,8000]{3,2,1,0:T(8,128)} %param.40, f32[5]{0:T(128)S(1)} %copy-done.64, f32[1,5,64,8000]{3,2,1,0:T(8,128)} %param.28, f32[1,5,64,8000]{3,2,1,0:T(8,128)} %bitcast.266, ...), kind=kLoop, calls=%fused_computation.21 | loop fusion | flops 51200000 | bytes 92160016 | tf_op jit(solution)/shard_map/mul | solution.py:95
  1415.9 9.8 broadcast_multiply_fusion.2
  1432.7 14.7 %add_multiply_fusion.1 = (f32[1,5,64,4352]{3,2,1,0:T(8,128)}, f32[1,5,64,4352]{3,2,1,0:T(8,128)}, f32[1,5,64,4352]{3,2,1,0:T(8,128)}, f32[1,5,64,4352]{3,2,1,0:T(8,128)}) fusion(f32[1,5,64,4352]{3,2,1,0:T(8,128)} %param.38, f32[5]{0:T(128)S(1)} %copy-done.64, f32[1,5,64,4352]{3,2,1,0:T(8,128)} %param.26, f32[1,5,64,4352]{3,2,1,0:T(8,128)} %param.34, ...), kind=kLoop, calls=%fused_computation.43 | loop fusion | flops 40386560 | bytes 47349784 | tf_op jit(solution)/shard_map/mul | solution.py:95
  (383 shorter events, 272.8 us)
Async XLA Ops:
  8.0 1042.0 %reduce-scatter.5.cloned.1.call-start = ((), (), s32[]{:S(2)}) async-start(), calls=%async_computation.4 | async-start | bytes 6553600 | tf_op jit(solution)/shard_map/reduce_scatter | solution.py:129
  10.3 386.1 %copy-start.80 = (s32[32]{0:T(128)}, s32[32]{0:T(128)S(1)}, u32[]{:S(2)}) copy-start(s32[32]{0:T(128)S(1)} %get-tuple-element.183) | copy-start | bytes 388
  349.9 19.9 %copy-start.78 = (f32[1024]{0:T(1024)}, f32[1024]{0:T(1024)S(1)}, u32[]{:S(2)}) copy-start(f32[1024]{0:T(1024)S(1)} %add_rsqrt_fusion) | copy-start | bytes 12292
  351.1 18.7 %copy-start.56 = (f32[2560]{0:T(1024)}, f32[2560]{0:T(1024)S(1)}, u32[]{:S(2)}) copy-start(f32[2560]{0:T(1024)S(1)} %mul.750) | copy-start | bytes 30724
  392.5 18.3 %copy-start.53 = (pred[128,1024]{1,0:T(32,128)(4,1)}, pred[128,1024]{1,0:T(32,128)(4,1)S(1)}, u32[]{:S(2)}) copy-start(pred[128,1024]{1,0:T(32,128)(4,1)S(1)} %get-tuple-element.181) | copy-start | bytes 393220
  396.4 14.5 copy-start.70
  396.4 14.4 copy-start.68
  397.2 13.6 copy-start.62
  397.4 13.5 copy-start.48
  415.1 126.9 %copy-start.30 = (f32[32,2560]{1,0:T(8,128)}, f32[32,2560]{1,0:T(8,128)S(1)}, u32[]{:S(2)}) copy-start(f32[32,2560]{1,0:T(8,128)S(1)} %get-tuple-element.192.one_ref) | copy-start | bytes 983044
  621.0 11.7 copy-start.25
  656.7 288.1 %copy-start.11 = (bf16[512,2560]{1,0:T(8,128)(2,1)S(1)}, bf16[512,2560]{1,0:T(8,128)(2,1)}, u32[]{:S(2)}) copy-start(bf16[512,2560]{1,0:T(8,128)(2,1)} %copy.240) | copy-start | bytes 7864324
  656.7 288.1 %copy-start.63 = (f32[4,128]{1,0:T(4,128)S(1)}, f32[4,128]{1,0:T(4,128)}, u32[]{:S(2)}) copy-start(f32[4,128]{1,0:T(4,128)} %copy-done.62) | copy-start | bytes 6148
  656.7 288.1 %copy-start.69 = (f32[128,4]{0,1:T(4,128)S(1)}, f32[128,4]{0,1:T(4,128)}, u32[]{:S(2)}) copy-start(f32[128,4]{0,1:T(4,128)} %copy-done.68) | copy-start | bytes 6148
  656.7 290.9 %copy-start.71 = (f32[128,4]{0,1:T(4,128)S(1)}, f32[128,4]{0,1:T(4,128)}, u32[]{:S(2)}) copy-start(f32[128,4]{0,1:T(4,128)} %copy-done.70) | copy-start | bytes 6148
  984.1 12.9 copy-start.84
  997.0 53.0 %copy-start.57 = (f32[2560]{0:T(1024)S(1)}, f32[2560]{0:T(1024)}, u32[]{:S(2)}) copy-start(f32[2560]{0:T(1024)} %copy-done.56) | copy-start | bytes 30724
  997.0 56.1 %copy-start.35 = (bf16[4,32,2560]{2,1,0:T(8,128)(2,1)S(1)}, bf16[4,32,2560]{2,1,0:T(8,128)(2,1)}, u32[]{:S(2)}) copy-start(bf16[4,32,2560]{2,1,0:T(8,128)(2,1)} %get-tuple-element.37) | copy-start | bytes 1966084
  997.0 186.5 %all-gather.2.cloned.1.call-start = ((), (), s32[]{:S(2)}) async-start(), calls=%async_computation.5 | async-start | bytes 6553600 | tf_op jit(solution)/shard_map/all_gather | solution.py:125
  1055.9 37.0 %copy-start.49 = (bf16[128,4,128]{0,2,1:T(8,128)(2,1)S(1)}, bf16[128,4,128]{0,2,1:T(8,128)(2,1)}, u32[]{:S(2)}) copy-start(bf16[128,4,128]{0,2,1:T(8,128)(2,1)} %copy-done.48) | copy-start | bytes 393220
  1092.9 224.3 %reduce-scatter.7.cloned.1.call-start = ((), (), s32[]{:S(2)}) async-start(), calls=%async_computation.6 | async-start | bytes 11796480
  1241.6 79.4 %copy-start.21 = (bf16[320,8,176]{0,2,1:T(8,128)(2,1)S(1)}, bf16[320,8,176]{0,2,1:T(8,128)(2,1)}, u32[]{:S(2)}) copy-start(bf16[320,8,176]{0,2,1:T(8,128)(2,1)} %copy.255) | copy-start | bytes 2703364
  1325.9 14.7 %all-to-all-start.1 = ((bf16[4,320,256]{2,1,0:T(8,128)(2,1)}), bf16[4,320,256]{2,1,0:T(8,128)(2,1)}, u32[]{:S(2)}, u32[]{:S(2)}) async-start(bf16[4,320,256]{2,1,0:T(8,128)(2,1)} %reshape.773), calls=%async_computation.2 | async-start | bytes 1310720 | tf_op jit(solution)/shard_map/all_to_all | solution.py:1249
  1372.8 10.5 copy-start.58
  (72 other events, 335.4 us)
Sparse Core Ops, SparseCore 0:
  997.1 52.8 reduce-scatter.4
  1093.0 39.1 all-gather.1
Sparse Core Ops, SparseCore 1:
  1124.4 192.7 reduce-scatter.6

commit v3 on v2

--- a/solution.py
+++ b/solution.py
@@ -26,6 +26,8 @@
 AVERAGE_DECAY = 0.9
 FULL_PRECISION = lax.Precision.HIGHEST
 LANES = 128
+CHUNKS = 5
+FEED = ((2, 3, 3), (6, 4), 6, (5, 6, 0))
 
 
 def rms_norm(values, gain, width):
@@ -96,6 +98,41 @@
     )
 
 
+def adam_kernel(
+    rate, decay, scale_ref, held_ref, weight, first, second, average, grad,
+    weight_out, first_out, second_out, average_out
+):
+    occupied = held_ref[pl.program_id(0)]
+    found = adam_update(
+        weight[...],
+        first[...],
+        second[...],
+        average[...],
+        grad[...],
+        scale_ref[0],
+        rate,
+        decay,
+        occupied,
+    )
+    for out, value in zip((weight_out, first_out, second_out, average_out), found):
+        out[...] = value
+
+
+def adam_blocks(weight, first, second, average, grad, scale, rate, decay, occupied):
+    capacity, block_rows, cols = weight.shape[1:]
+    rows = 16
+    block = pl.BlockSpec((1, 1, rows, cols), lambda i, j: (0, i, j, 0))
+    scalar = pl.BlockSpec(memory_space=pltpu.SMEM)
+    return pl.pallas_call(
+        functools.partial(adam_kernel, rate, decay),
+        grid=(capacity, block_rows // rows),
+        out_shape=[jax.ShapeDtypeStruct(weight.shape, weight.dtype)] * 4,
+        in_specs=[scalar, scalar] + [block] * 5,
+        out_specs=[block] * 4,
+        compiler_params=pltpu.CompilerParams(vmem_limit_bytes=40 * 2**20),
+    )(scale.reshape(1), occupied, weight, first, second, average, grad)
+
+
 def times_plain(left, right):
     return jnp.dot(left, right, preferred_element_type=jnp.float32)
 
@@ -171,6 +208,10 @@
     def finish(self):
         for made in self.open:
             made.wait_send()
+
+
+def nothing(place):
+    del place
 
 
 def greet(peers):
@@ -237,7 +278,7 @@
     links.finish()
 
 
-def gather_body(nd, ns, links, in_ref, out_ref):
+def gather_body(nd, ns, links, in_ref, out_ref, meanwhile=nothing):
     dp, st, z, y, x, c = places(nd, ns)
     deep, across = nd // 2, ns // 2
     half = in_ref.shape[1] // 2
@@ -277,6 +318,7 @@
     a_x = [send(x, y, 0, to_x(k)) for k in range(1, across)]
     b_y = send(x, y, 1, to_y)
     arriving = [send(x, y, 0, to_core), send(x, y, 1, to_core)]
+    meanwhile(0)
     a_y.wait_recv()
     a_xy = [send(x, other_y, 0, to_x(k)) for k in range(1, across)]
     arriving.append(send(x, other_y, 0, to_core))
@@ -286,6 +328,7 @@
         from_x = lax.rem(x - k + across, across)
         b_xy.append(send(from_x, y, 1, to_y))
         arriving.append(send(from_x, y, 1, to_core))
+    meanwhile(1)
     for k in range(1, across):
         a_x[k - 1].wait_recv()
         arriving.append(send(lax.rem(x - k + across, across), y, 0, to_core))
@@ -334,7 +377,7 @@
     links.finish()
 
 
-def scatter_body(nd, ns, links, in_ref, out_ref, scratch, meanwhile=None):
+def scatter_body(nd, ns, links, in_ref, out_ref, scratch, meanwhile=nothing):
     rc, acc, rx_a, ry_a, rz_a, ry_b, rx_b, rz_b = scratch
     dp, st, z, y, x, c = places(nd, ns)
     deep, across = nd // 2, ns // 2
@@ -379,14 +422,14 @@
 
         return acc.at[x_at(k), ys[ky], :, :, cols[part]]
 
-    if meanwhile is not None:
-        meanwhile()
+    meanwhile(0)
     a_x, b_y = {}, {}
     for k in range(1, across):
         for ky in (1, 0):
             a_x[k, ky] = links.copy(add(k, ky, 0, []), rx_a.at[k - 1, ky], *to_x(k))
     for k in range(across):
         b_y[k] = links.copy(add(k, 1, 1, []), ry_b.at[k], *to_y)
+    meanwhile(1)
     for k in range(1, across):
         a_x[k, 1].wait_recv()
     a_y = links.copy(
@@ -396,6 +439,7 @@
     for k in range(1, across):
         b_y[k].wait_recv()
         b_x[k] = links.copy(add(k, 0, 1, [ry_b.at[k]]), rx_b.at[k - 1], *to_x(k))
+    meanwhile(2)
     for k in range(1, across):
         a_x[k, 0].wait_recv()
     a_y.wait_recv()
@@ -820,9 +864,21 @@
     own_copy = pltpu.make_async_copy(table_ref.at[dp], table_out.at[dp], local.at[0])
     own_copy.start()
     local_copies = [own_copy]
-    swapped = [
-        links.copy(table_ref.at[peer[0]], table_out.at[dp], *peer) for peer in dp_peers
-    ]
+    own = table_ref.shape[1]
+    chunk = own // CHUNKS
+    queue = [(peer, i) for i in range(CHUNKS) for peer in dp_peers]
+    swapped = []
+
+    def feed(amount):
+        for _ in range(min(amount, len(queue))):
+            peer, i = queue.pop(0)
+            rows = pl.ds(i * chunk, chunk)
+            swapped.append(
+                links.copy(table_ref.at[peer[0], rows], table_out.at[dp, rows], *peer)
+            )
+
+    def feeding(amounts):
+        return lambda place: feed(amounts[place])
 
     def norm_back(grad, values, gain, row):
         mean = jnp.sum(values * values, axis=1, keepdims=True) * (1.0 / width)
@@ -833,10 +889,11 @@
         return scaled * root - values * (root * root * root * inner)
 
     fill.wait()
-    scatter_body(nd, ns, links, part_ref, summed, scratch[:-2])
+    scatter_body(nd, ns, links, part_ref, summed, scratch[:-2], feeding(FEED[0]))
     summed[...] = norm_back(summed[...], two_ref[...], gain_ref[pl.ds(1, 1), :], 1)
     low[...] = summed[...].astype(low.dtype)
-    gather_body(nd, ns, links, low, down)
+    gather_body(nd, ns, links, low, down, feeding(FEED[1]))
+    feed(FEED[2])
 
     inner_cols = gu_ref.shape[1]
     step = deep * count
@@ -871,7 +928,10 @@
             .reshape(deep, count, wide)
         )
 
-    def weight_grads():
+    def weight_grads(place):
+        feed(FEED[3][place])
+        if place:
+            return
         span = 2 * LANES
 
         @pl.loop(0, wide // span)
@@ -887,15 +947,9 @@
                 preferred_element_type=jnp.float32,
             ).astype(dffn.dtype)
 
-        own = ffn_out.shape[1]
-
-        def block(owner):
-            return dffn.at[pl.ds(pl.multiple_of(owner * own, own), own), :]
-
-        mine = pltpu.make_async_copy(block(dp), ffn_out.at[dp], local.at[1])
-        mine.start()
-        swapped.extend(links.copy(block(peer[0]), ffn_out.at[dp], *peer) for peer in dp_peers)
-        local_copies.append(mine)
+        home = pltpu.make_async_copy(dffn, ffn_out, local.at[1])
+        home.start()
+        local_copies.append(home)
 
     grad_two = summed[...]
     scatter_body(nd, ns, links, part_ref, summed, scratch[:-2], weight_grads)
@@ -905,6 +959,7 @@
     made = [links.copy(low, one_out.at[st], *peer) for peer in state_peers]
     for copy in made:
         copy.wait_recv()
+    feed(len(queue))
     for copy in swapped:
         copy.wait_recv()
     for copy in local_copies:
@@ -917,9 +972,8 @@
     deep, across = nd // 2, ns // 2
     count, wide = two.shape
     kind = part.dtype
-    own = wide // nd
     cols = wgu.shape[1] + wd.shape[1]
-    copies = 2 * scatter_copies(nd, ns) + gather_copies(nd, ns) + 2 * (nd - 1) + ns - 1
+    copies = 2 * scatter_copies(nd, ns) + gather_copies(nd, ns) + (nd - 1) * CHUNKS + ns - 1
     vmem = pl.BlockSpec(memory_space=pltpu.VMEM)
     hbm = pl.BlockSpec(memory_space=pl.ANY)
     six = (2, across, 2, deep, count, wide)
@@ -928,7 +982,7 @@
         out_shape=[
             jax.ShapeDtypeStruct((ns, count, wide), kind),
             jax.ShapeDtypeStruct(table.shape, kind),
-            jax.ShapeDtypeStruct((nd, own, cols), kind),
+            jax.ShapeDtypeStruct((wide, cols), kind),
             jax.ShapeDtypeStruct((2, wide), jnp.float32),
         ],
         in_specs=[hbm, hbm] + [vmem] * 8,
@@ -952,6 +1006,143 @@
         ),
     )(part.reshape(six), table, two, one, gain, wd, wgu, gu, hidden, rows)
     return (out[0].reshape(ns * count, wide),) + tuple(out[1:])
+
+
+def rows_back_kernel(
+    nd, ns, width, in_ref, stream_ref, gain_ref, more_ref, out_ref, gain_out, rc, acc, rx, fin, low,
+    sends, recvs
+):
+    dp, st, z, y, x, c = places(nd, ns)
+    across = ns // 2
+    tokens = in_ref.shape[1]
+    own = in_ref.shape[0] // nd
+    part = tokens // ns
+    to_core = (dp, st + 1 - 2 * c)
+    dp_peers = [(lax.rem(dp + k, nd), st) for k in range(1, nd)]
+    peers = dp_peers + [(dp, lax.rem(x + k, across) * 2 + c) for k in range(1, across)]
+    greet(peers + [to_core])
+    links = Links(sends, recvs)
+
+    def x_at(k):
+        return lax.rem(x + k, across)
+
+    def rows_of(owner):
+        return pl.ds(pl.multiple_of(owner * own, own), own)
+
+    def block(k, kx, cc):
+        start = (x_at(kx) * 2 + cc) * part
+        return in_ref.at[pl.ds(k * own, own), pl.ds(pl.multiple_of(start, part), part)]
+
+    def place(row, share):
+        return out_ref.at[:, pl.ds(pl.multiple_of(row * tokens + share * part, part), part)]
+
+    def add(sources, target):
+        @pl.loop(0, own // 32)
+        def _(i):
+            rows = pl.ds(pl.multiple_of(i * 32, 32), 32)
+            found = sources[0][rows, :].astype(jnp.float32)
+            for source in sources[1:]:
+                found += source[rows, :].astype(jnp.float32)
+            target[rows, :] = found.astype(target.dtype)
+
+    core, across_x = {}, {}
+    for kx in list(range(1, across)) + [0]:
+        for k in range(nd):
+            core[k, kx] = links.copy(block(k, kx, 1 - c), rc.at[k, kx], *to_core)
+    for kx in range(1, across):
+        for k in range(nd):
+            core[k, kx].wait_recv()
+            add([block(k, kx, c), rc.at[k, kx]], acc.at[k, kx - 1])
+            across_x[k, kx] = links.copy(
+                acc.at[k, kx - 1], rx.at[k, kx - 1], dp, x_at(kx) * 2 + c
+            )
+    for k in range(nd):
+        core[k, 0].wait_recv()
+        sources = [block(k, 0, c), rc.at[k, 0]]
+        for kx in range(1, across):
+            across_x[k, kx].wait_recv()
+            sources.append(rx.at[k, kx - 1])
+        add(sources, fin.at[pl.ds(k * own, own), :])
+
+    step = 32
+    pieces = in_ref.shape[0] // step
+
+    def at(i):
+        return pl.ds(pl.multiple_of(i * step, step), step)
+
+    def gather_sums(i, carry):
+        square, inner = carry
+        values = stream_ref[at(i), :].astype(jnp.float32)
+        scaled = fin[at(i), :] * gain_ref[at(i), :] * values
+        square = square + jnp.sum(values * values, axis=0, keepdims=True)
+        return square, inner + jnp.sum(scaled, axis=0, keepdims=True)
+
+    none = jnp.zeros((1, part), jnp.float32)
+    square, inner = lax.fori_loop(0, pieces, gather_sums, (none, none))
+    root = lax.rsqrt(square * (1.0 / width) + NORM_EPS)
+    inner = inner * (1.0 / width) * root * root * root
+
+    @pl.loop(0, pieces)
+    def _(i):
+        values = stream_ref[at(i), :].astype(jnp.float32)
+        grad = fin[at(i), :]
+        gain_out[at(i), :] = jnp.sum(grad * values * root, axis=1, keepdims=True)
+        found = grad * gain_ref[at(i), :] * root - values * inner + more_ref[at(i), :]
+        low[at(i), :] = found.astype(low.dtype)
+
+    swapped = [links.copy(low.at[rows_of(p[0]), :], place(dp, st), *p) for p in dp_peers]
+    place(dp, st)[...] = low[rows_of(dp), :]
+    later, last = {}, []
+    for k in range(nd):
+        row = lax.rem(dp - k + nd, nd)
+        if k:
+            swapped[k - 1].wait_recv()
+        for kx in range(1, across):
+            later[k, kx] = links.copy(place(row, st), place(row, st), dp, x_at(kx) * 2 + c)
+        last.append(links.copy(place(row, st), place(row, st), *to_core))
+    for k in range(nd):
+        row = lax.rem(dp - k + nd, nd)
+        for kx in range(1, across):
+            later[k, kx].wait_recv()
+            share = lax.rem(x - kx + across, across) * 2 + c
+            last.append(links.copy(place(row, share), place(row, share), *to_core))
+    for made in last:
+        made.wait_recv()
+    links.finish()
+
+
+def rows_back(values, stream, gain, more, width, number):
+    nd, ns = lax.axis_size("dp"), lax.axis_size("state")
+    across = ns // 2
+    wide, tokens = values.shape
+    own, part = wide // nd, tokens // ns
+    copies = nd * across + nd * (across - 1) + nd - 1 + nd * across + nd * (across - 1)
+    vmem = pl.BlockSpec(memory_space=pltpu.VMEM)
+    kind = values.dtype
+    return pl.pallas_call(
+        functools.partial(rows_back_kernel, nd, ns, width),
+        out_shape=[
+            jax.ShapeDtypeStruct((own, nd * tokens), kind),
+            jax.ShapeDtypeStruct((wide, 1), jnp.float32),
+        ],
+        in_specs=[vmem] * 4,
+        out_specs=[vmem] * 2,
+        scratch_shapes=[
+            pltpu.VMEM((nd, across, own, part), kind),
+            pltpu.VMEM((nd, across - 1, own, part), kind),
+            pltpu.VMEM((nd, across - 1, own, part), kind),
+            pltpu.VMEM((wide, part), jnp.float32),
+            pltpu.VMEM((wide, part), kind),
+            pltpu.SemaphoreType.DMA((copies,)),
+            pltpu.SemaphoreType.DMA((copies,)),
+        ],
+        compiler_params=pltpu.CompilerParams(
+            collective_id=number, has_side_effects=True, vmem_limit_bytes=48 * 2**20
+        ),
+        cost_estimate=pl.CostEstimate(
+            flops=0, bytes_accessed=60 * values.size, transcendentals=0
+        ),
+    )(values, stream, gain, more)
 
 
 def state_sum_kernel(nd, ns, in_ref, out_ref, land, sends, recvs):
@@ -1072,7 +1263,6 @@
     down_cols = -(-unit_part // LANES) * LANES
     parts_sent = jnp.concatenate(
         [
-            by_part(table_padded, vocab_part),
             by_part(in_own[:, mixer_cols : mixer_cols + units], unit_part),
             by_part(in_own[:, mixer_cols + units :], unit_part),
             zeros(gu_cols - 2 * unit_part),
@@ -1120,9 +1310,10 @@
     w_fv = jnp.concatenate([w_f, w_v], axis=1)
     w_qfv = jnp.concatenate([w_q, w_fv], axis=1)
     parts_all = parts_all.reshape(wide, -1)
-    table = parts_all[:, :vocab_part]
-    w_gu = parts_all[:, vocab_part : vocab_part + gu_cols]
-    w_d = parts_all[:, vocab_part + gu_cols :]
+    w_gu = parts_all[:, :gu_cols]
+    w_d = parts_all[:, gu_cols:]
+    table_padded, stream = lax.optimization_barrier((table_padded, stream))
+    table = swap_dp(spread_columns(table_padded, nd)).reshape(wide, vocab_part)
 
     positions = loss_positions[0]
     pick_hit = positions[:, None] == jnp.arange(tokens)[None, :]
@@ -1214,9 +1405,12 @@
     )
     grad_gain_three, grad_gain_four = gain_pair
     grad_table_own = join_columns(grad_table_back)[:, :vocab_share].astype(f32)
+    grad_ffn = swap_dp(grad_ffn.reshape(nd, own, gu_cols + down_cols))
 
     grad_gated = times_plain(grad_one, w_o)
-    grad_w_o = times_left(grad_one, gated)
+    grad_o_own = lax.psum_scatter(
+        times_left(grad_one, gated).astype(bf16), "dp", scatter_dimension=0, tiled=True
+    )
     grad_mixed, grad_gain_two = back_head(grad_gated)
     grad_query, grad_key, grad_forget, grad_value = back_mix(
         grad_mixed.astype(bf16).astype(f32)
@@ -1225,26 +1419,28 @@
     grad_query_pre = times_left(pick, grad_query_pre)
     (grad_forget_pre,) = back_gates((grad_key, grad_forget))
     grad_qfv = jnp.concatenate([grad_query_pre, grad_forget_pre, grad_value], axis=1).astype(bf16)
-    grad_w_qfv = times_plain(normed_one, grad_qfv)
-    grad_norm_one = scatter_state(times_right(w_qfv, grad_qfv).astype(bf16), 1).astype(f32)
-    _, back_one = jax.vjp(tall_norm, stream_mine.astype(f32), gains[0])
-    grad_stream_zero, grad_gain_one = back_one(grad_norm_one)
+    grad_qfv, grad_ffn = lax.optimization_barrier((grad_qfv, grad_ffn))
     pick_mine = lax.dynamic_slice_in_dim(pick_low, me_state * quarter, quarter, axis=1)
-    grad_zero = (grad_stream_zero + times_left(grad_one, pick_mine)).astype(bf16)
-    grad_mixer_own = lax.psum_scatter(
-        jnp.concatenate([grad_w_qfv, grad_w_o], axis=1).astype(bf16),
-        "dp",
-        scatter_dimension=0,
-        tiled=True,
-    )
-
-    embed = swap_dp(grad_zero.reshape(nd, own, quarter))
-    embed = gather_state(embed, 2).transpose(1, 0, 2).reshape(own, nd * tokens)
+    embed, grad_gain_one = rows_back(
+        times_right(w_qfv, grad_qfv).astype(bf16),
+        stream_mine,
+        gains[0][:, None],
+        times_left(grad_one, pick_mine),
+        width,
+        8,
+    )
+    grad_gain_one = grad_gain_one[:, 0]
+    grad_w_qfv = times_plain(normed_one, grad_qfv).astype(bf16)
+
+    def sum_dp(values):
+        return lax.psum_scatter(values, "dp", scatter_dimension=0, tiled=True)
+
+    grad_qfv_own = sum_dp(grad_w_qfv)
     grad_lookup = times_right(embed, hit.astype(bf16))
-    grad_mixer_own, grad_lookup = lax.optimization_barrier((grad_mixer_own, grad_lookup))
+    grad_qfv_own, grad_lookup = lax.optimization_barrier((grad_qfv_own, grad_lookup))
     own_table = grad_table_own + grad_lookup
 
-    grad_keys = grad_mixer_own[:, : 2 * qcols].reshape(own, 2, ns, key_part)
+    grad_keys = grad_qfv_own[:, : 2 * qcols].reshape(own, 2, ns, key_part)
     grad_keys = grad_keys.transpose(2, 0, 1, 3).reshape(ns, own, 2 * key_part)
     grad_keys = lax.all_to_all(grad_keys, "state", split_axis=0, concat_axis=0, tiled=True)
     grad_keys = grad_keys.reshape(ns, own, 2, key_part).transpose(1, 2, 0, 3)
@@ -1254,14 +1450,14 @@
     own_in = jnp.concatenate(
         [
             grad_keys.reshape(own, 2 * key_cols),
-            grad_mixer_own[:, 2 * qcols : 2 * qcols + value_width],
+            grad_qfv_own[:, 2 * qcols :],
             join_columns(grad_gate),
             join_columns(grad_up),
         ],
         axis=1,
     ).astype(f32)
     own_out = jnp.concatenate(
-        [grad_mixer_own[:, 2 * qcols + value_width :], join_columns(grad_down)],
+        [grad_o_own, join_columns(grad_down)],
         axis=1,
     ).astype(f32)
 
@@ -1286,8 +1482,7 @@
     grad_norm = jnp.sqrt(squares_all)
     scale = jnp.minimum(1.0, CLIP_NORM / (grad_norm + 1e-06))
     occupied = occupied_here.astype(f32)
-    wide_occ = occupied[None, :, None, None]
-    new_in = adam_update(
+    new_in = adam_blocks(
         in_weight,
         in_first,
         in_second,
@@ -1296,9 +1491,9 @@
         scale,
         LEARN_RATE,
         WEIGHT_DECAY,
-        wide_occ,
-    )
-    new_out = adam_update(
+        occupied,
+    )
+    new_out = adam_blocks(
         out_weight,
         out_first,
         out_second,
@@ -1307,9 +1502,9 @@
         scale,
         LEARN_RATE,
         WEIGHT_DECAY,
-        wide_occ,
-    )
-    new_table = adam_update(
+        occupied,
+    )
+    new_table = adam_blocks(
         table_weight,
         table_first,
         table_second,
@@ -1318,7 +1513,7 @@
         scale,
         LEARN_RATE,
         WEIGHT_DECAY,
-        wide_occ,
+        occupied,
     )
     new_gain = adam_update(
         gain_weight,

time: 1470 us -> 1280 us (0.87)
  other arithmetic: 144 us -> 60.7 us
  waiting for transfers between devices: 127 us -> 53.9 us
  blocking collectives: 37 us -> 0 us
    pallas_call x0 -> x4, Pallas kernels: none -> 162 us  [the longest x1 95.2 us: rows_back(): pl.pallas_call(functools.partial(rows_back_kernel, nd, ns, width), out_sh...]
    pallas_call x1, Pallas kernels: 288 us -> 191 us  [slots_back(): pl.pallas_call(functools.partial(slots_back_kernel, nd, ns, width, units)...]
    pallas_call x1, Pallas kernels: 290 us -> 202 us  [front(): pl.pallas_call(functools.partial(front_kernel, nd, ns, vocab), out_shape=...]
    unnamed x4 -> x2, waiting for transfers between devices: 75.6 us -> 0.03 us
    all_to_all x0 -> x2, waiting for transfers between devices: none -> 53.2 us  [swap_dp(): return lax.all_to_all(values, 'dp', split_axis=0, concat_axis=0, tiled=True)]
    reduce_scatter x1 -> x2, waiting for transfers between devices: 50.8 us -> 0.69 us  [the longest x1 0.69 us: on_device(): lax.psum_scatter(times_left(grad_one, gated).astype(bf16), 'dp', scatter_...]
    mul x4 -> x1, other arithmetic: 48.9 us -> 0.07 us  [adam_update(): average_new * occupied]
    all_to_all x1 -> x0, blocking collectives: 37 us -> none  [swap_dp(): return lax.all_to_all(values, 'dp', split_axis=0, concat_axis=0, tiled=True)]
  transfers between devices with their start and end apart: 4 -> 5, of which waited for: 3 -> 2; matrix products, arithmetic and copies ran while one was open for 9% -> 21% of each run, Pallas kernels for 2% -> 23%
where the time goes in v3:
time: 1280 us; the launch traced here: 1270 us
  Pallas kernels  782 us (61%)
  matrix products  188 us (15%)
  local copies, waits for them, and re-layouts  153 us (12%)
  other arithmetic  60.7 us (5%)
  waiting for transfers between devices  53.9 us (4%)
  between operations  21.2 us (2%)
  starting transfers between devices  14.3 us (1%)
    pallas_call x1, Pallas kernels, front(): pl.pallas_call(functools.partial(front_kernel, nd, ns, vocab), out_shape=...  202 us
    pallas_call x1, Pallas kernels, slots_back(): pl.pallas_call(functools.partial(slots_back_kernel, nd, ns, width, units)...  191 us
    pallas_call x2, Pallas kernels, gather_all(): pl.pallas_call(functools.partial(gather_all_kernel, nd, ns), out_shape=ja...  107 us
    pallas_call x1, Pallas kernels, rows_back(): pl.pallas_call(functools.partial(rows_back_kernel, nd, ns, width), out_sh...  95.2 us
    dot_general x6, matrix products, times_right(): lax.dot_general(left, right, (((1,), (1,)), ((), ())), preferred_element_...  91.8 us
    pallas_call x3, Pallas kernels, adam_blocks(): pl.pallas_call(functools.partial(adam_kernel, rate, decay), grid=(capacit...  66.8 us
    pallas_call x3, Pallas kernels, small_gather(): pl.pallas_call(functools.partial(small_gather_kernel, nd, ns, everyone, l...  62 us
    all_to_all x2, waiting for transfers between devices, swap_dp(): return lax.all_to_all(values, 'dp', split_axis=0, concat_axis=0, tiled=True)  53.2 us
  transfers between devices with their start and end apart: 5, of which 2 were waited for; matrix products, arithmetic and copies ran while one was open for 21% of the time, Pallas kernels for 23%

profile of v3, /device:TPU:0, one launch (start us, length us, event | category | flops | bytes accessed | tf_op | source)
XLA Modules:
  0.0 1273.4 jit_solution(15431925901308847802)
XLA Ops:
  44.1 7.8 concatenate.62
  51.9 202.5 %shard_map.348 = (s32[8,16,128]{2,1,0:T(8,128)S(1)}, bf16[8,16,128]{2,1,0:T(8,128)(2,1)S(1)}, bf16[2560,1024]{1,0:T(8,128)(2,1)}, bf16[4,8,320,256]{3,2,1,0:T(8,...) custom-call(s32[16,128]{1,0:T(8,128)S(1)} %pad_bitcast_fusion.small_ref, ...), custom_call_target="tpu_custom_call" | custom-call | flops 42949672960 | bytes 6553600 | tf_op jit(solution)/shard_map/pallas_call | solution.py:793
  306.1 8.4 fusion.58
  328.1 11.3 shard_map.349
  343.8 69.6 %shard_map.350 = bf16[2,2,2,4,32,2560]{5,4,3,2,1,0:T(8,128)(2,1)S(1)} custom-call(bf16[32,2560]{1,0:T(8,128)(2,1)S(1)} %multiply_convert_fusion.3.in_ref), custom_call_target="tpu_custom_call" | custom-call | tf_op jit(solution)/shard_map/pallas_call | solution.py:359
  419.9 46.7 %shard_map.351 = f32[32,2560]{1,0:T(8,128)S(1)} custom-call(bf16[2,2,2,4,32,2560]{5,4,3,2,1,0:T(8,128)(2,1)S(1)} %bitcast.262), custom_call_target="tpu_custom_call" | custom-call | tf_op jit(solution)/shard_map/pallas_call | solution.py:506
  469.0 37.3 %shard_map.352 = bf16[2,2,2,4,32,2560]{5,4,3,2,1,0:T(8,128)(2,1)S(1)} custom-call(bf16[32,2560]{1,0:T(8,128)(2,1)S(1)} %multiply_convert_fusion.2.in_ref), custom_call_target="tpu_custom_call" | custom-call | tf_op jit(solution)/shard_map/pallas_call | solution.py:359
  513.9 9.6 select_reduce_fusion.2
  528.1 16.1 %shard_map.353 = f32[32,24,128]{2,1,0:T(8,128)} custom-call(f32[24,128]{1,0:T(8,128)} %reshape.626.refs_0_), custom_call_target="tpu_custom_call" | custom-call | tf_op jit(solution)/shard_map/pallas_call | solution.py:264
  549.6 11.7 convolution_convert_fusion.2
  561.3 11.3 convolution_convert_fusion.3
  572.6 190.9 %shard_map.354 = (bf16[4,32,2560]{2,1,0:T(8,128)(2,1)}, bf16[8,320,1024]{2,1,0:T(8,128)(2,1)}, bf16[2560,640]{1,0:T(8,128)(2,1)}, f32[2,2560]{1,0:T(2,128)}) custom-call(bf16[2,2,2,4,32,2560]{5,4,3,2,1,0:T(8,128)(2,1)} %bitcast.344, bf16[8,320,1024]{2,1,0:T(8,128)(2,1)} %bitcast.343, f32[32,2560]{1,0:T(8,128)} %copy-done.45, f32[32,2560]{1,0:T(8,128)} %copy-done.39, ...), custom_call_target="tpu_custom_call" | custom-call | flops 13421772800 | bytes 262144000 | tf_op jit(solution)/shard_map/pallas_call | solution.py:980
  781.9 7.6 select_reduce_fusion
  812.8 53.2 %all-to-all-done.1 = bf16[8,320,640]{2,1,0:T(8,128)(2,1)} async-done(((bf16[8,320,640]{2,1,0:T(8,128)(2,1)}), bf16[8,320,640]{2,1,0:T(8,128)(2,1)}, u32[]{:S(2)}, u32[]{:S(2)}) %all-to-all-start.1) | async-done | bytes 3276832 | tf_op jit(solution)/shard_map/all_to_all | solution.py:170
  866.0 13.0 %convolution_convert_fusion = bf16[2560,1536]{1,0:T(8,128)(2,1)} fusion(bf16[1024,1536]{1,0:T(8,128)(2,1)S(1)} %pad_maximum_fusion, bf16[2560,1024]{1,0:T(8,128)(2,1)} %get-tuple-element.50, f32[2560]{0:T(1024)S(1)} %copy-done.74, f32[1024]{0:T(1024)S(1)} %copy-done.80), kind=kOutput, calls=%fused_computation.11 | convolution fusion | flops 8067481600 | bytes 16267264 | tf_op jit(solution)/shard_map/dot_general | solution.py:137
  917.5 12.9 %fusion.16.in_ref = bf16[2560,1024]{1,0:T(8,128)(2,1)} fusion(bf16[1024,1536]{1,0:T(8,128)(2,1)} %copy-done.38, bf16[2560,512]{1,0:T(8,128)(2,1)S(1)} %copy-done.42, bf16[2560,512]{1,0:T(8,128)(2,1)} %copy-done.43, bf16[2560,512]{1,0:T(8,128)(2,1)} %get-tuple-element.221), kind=kOutput, calls=%fused_computation.27 | convolution fusion | flops 8079278080 | bytes 16252928 | tf_op jit(solution)/shard_map/dot_general | solution.py:141
  930.4 95.2 %shard_map.355 = (bf16[320,8192]{1,0:T(8,128)(2,1)}, f32[2560,1]{1,0:T(8,128)S(1)}) custom-call(bf16[2560,1024]{1,0:T(8,128)(2,1)} %fusion.16.in_ref, bf16[2560,256]{1,0:T(8,128)(2,1)S(1)} %constant_dynamic-slice_fusion.stream_ref, f32[2560,1]{1,0:T(8,128)S(1)} %broadcast_in_dim_squeeze.3.gain_ref, f32[2560,256]{1,0:T(8,128)} %fusion.103.more_ref), custom_call_target="tpu_custom_call" | custom-call | bytes 157286400 | tf_op jit(solution)/shard_map/pallas_call | solution.py:1122
  1026.7 30.1 %shard_map.357 = bf16[32,80,128]{2,1,0:T(8,128)(2,1)} custom-call(bf16[80,128]{1,0:T(8,128)(2,1)} %fusion.117.refs_0_), custom_call_target="tpu_custom_call" | custom-call | tf_op jit(solution)/shard_map/pallas_call | solution.py:264
  1072.9 58.2 %fusion = f32[320,8000]{1,0:T(8,128)} fusion(bf16[320,8192]{1,0:T(8,128)(2,1)} %get-tuple-element.60, s32[8192]{0:T(1024)S(1)} %bitcast.330), kind=kOutput, calls=%fused_computation.3 | convolution fusion | flops 42008576000 | bytes 15515648 | tf_op jit(solution)/shard_map/dot_general | solution.py:141
  1140.1 12.5 multiply_reduce_fusion
  1161.9 15.9 %shard_map.356 = f32[32,8,128]{2,1,0:T(8,128)} custom-call(f32[8,128]{1,0:T(8,128)} %broadcast_in_dim.226.refs_0_), custom_call_target="tpu_custom_call" | custom-call | tf_op jit(solution)/shard_map/pallas_call | solution.py:264
  1187.8 35.9 %shard_map.360 = (f32[1,5,64,8000]{3,2,1,0:T(8,128)}, f32[1,5,64,8000]{3,2,1,0:T(8,128)}, f32[1,5,64,8000]{3,2,1,0:T(8,128)}, f32[1,5,64,8000]{3,2,1,0:T(8,128)}) custom-call(f32[1]{0:T(128)} %bitcast.80.scale_ref, f32[5]{0:T(128)S(1)} %fusion.155.held_ref, f32[1,5,64,8000]{3,2,1,0:T(8,128)S(1)} %copy-done, f32[1,5,64,8000]{3,2,1,0:T(8,128)} %first.5, ...), custom_call_target="tpu_custom_call" | custom-call | tf_op jit(solution)/shard_map/pallas_call | solution.py:126
  1228.8 9.3 shard_map.359
  1243.4 21.6 %shard_map.358 = (f32[1,5,64,4352]{3,2,1,0:T(8,128)}, f32[1,5,64,4352]{3,2,1,0:T(8,128)}, f32[1,5,64,4352]{3,2,1,0:T(8,128)}, f32[1,5,64,4352]{3,2,1,0:T(8,128)}) custom-call(f32[1]{0:T(128)} %bitcast.80.scale_ref, f32[5]{0:T(128)S(1)} %fusion.155.held_ref, f32[1,5,64,4352]{3,2,1,0:T(8,128)S(1)} %bitcast.264, f32[1,5,64,4352]{3,2,1,0:T(8,128)S(1)} %copy-done.4, ...), custom_call_target="tpu_custom_call" | custom-call | tf_op jit(solution)/shard_map/pallas_call | solution.py:126
  (392 shorter events, 263.7 us)
Async XLA Ops:
  9.4 309.7 %copy-start.81 = (s32[32]{0:T(128)}, s32[32]{0:T(128)S(1)}, u32[]{:S(2)}) copy-start(s32[32]{0:T(128)S(1)} %get-tuple-element.206) | copy-start | bytes 388
  51.9 202.5 %slice-start.6 = ((s8[5242880]{0:T(1024)(128)(4,1)}), s8[4194304]{0:T(1024)(128)(4,1)S(1)}, s32[]{:S(2)}) async-start(s8[5242880]{0:T(1024)(128)(4,1)} %bitcast.277), calls=%async_computation.13 | async-start | bytes 8388608
  51.9 202.5 %slice-start.7 = ((s8[5242880]{0:T(1024)(128)(4,1)}), s8[1048576]{0:T(1024)(128)(4,1)S(1)}, s32[]{:S(2)}) async-start(s8[5242880]{0:T(1024)(128)(4,1)} %bitcast.277), calls=%async_computation.14 | async-start | bytes 2097152
  257.6 256.4 %all-to-all-start = ((bf16[8,320,1024]{2,1,0:T(8,128)(2,1)}), bf16[8,320,1024]{2,1,0:T(8,128)(2,1)}, u32[]{:S(2)}, u32[]{:S(2)}) async-start(bf16[8,320,1024]{2,1,0:T(8,128)(2,1)} %bitcast.276), calls=%async_computation | async-start | bytes 10485760 | tf_op jit(solution)/shard_map/all_to_all | solution.py:170
  343.7 123.6 %copy-start.39 = (f32[32,2560]{1,0:T(8,128)}, f32[32,2560]{1,0:T(8,128)S(1)}, u32[]{:S(2)}) copy-start(f32[32,2560]{1,0:T(8,128)S(1)} %get-tuple-element.215.one_ref) | copy-start | bytes 983044
  343.8 69.6 %copy-start.25 = (bf16[8,320,640]{2,1,0:T(8,128)(2,1)S(1)}, bf16[8,320,640]{2,1,0:T(8,128)(2,1)}, u32[]{:S(2)}) copy-start(bf16[8,320,640]{2,1,0:T(8,128)(2,1)} %get-tuple-element.54) | copy-start | bytes 9830404
  572.6 191.0 %copy-start.21 = (bf16[512,2560]{1,0:T(8,128)(2,1)S(1)}, bf16[512,2560]{1,0:T(8,128)(2,1)}, u32[]{:S(2)}) copy-start(bf16[512,2560]{1,0:T(8,128)(2,1)} %copy.234) | copy-start | bytes 7864324
  572.6 191.0 %copy-start.70 = (f32[128,4]{0,1:T(4,128)S(1)}, f32[128,4]{0,1:T(4,128)}, u32[]{:S(2)}) copy-start(f32[128,4]{0,1:T(4,128)} %copy-done.69) | copy-start | bytes 6148
  765.6 100.4 %all-to-all-start.1 = ((bf16[8,320,640]{2,1,0:T(8,128)(2,1)}), bf16[8,320,640]{2,1,0:T(8,128)(2,1)}, u32[]{:S(2)}, u32[]{:S(2)}) async-start(bf16[8,320,640]{2,1,0:T(8,128)(2,1)} %bitcast.311), calls=%async_computation.1 | async-start | bytes 6553600 | tf_op jit(solution)/shard_map/all_to_all | solution.py:170
  770.1 123.2 %reduce-scatter.5.cloned.1.call-start = ((), (), s32[]{:S(2)}) async-start(), calls=%async_computation.6 | async-start | bytes 2949120 | tf_op jit(solution)/shard_map/reduce_scatter | solution.py:1411
  779.7 351.4 %reduce-scatter.3.cloned.1.call-start = ((), (), s32[]{:S(2)}) async-start(), calls=%async_computation.5 | async-start | bytes 8847360 | tf_op jit(solution)/shard_map/reduce_scatter | solution.py:1436
  812.5 53.5 %copy-start.74 = (f32[2560]{0:T(1024)S(1)}, f32[2560]{0:T(1024)}, u32[]{:S(2)}) copy-start(f32[2560]{0:T(1024)} %copy-done.73) | copy-start | bytes 30724
  812.5 53.5 %copy-start.80 = (f32[1024]{0:T(1024)S(1)}, f32[1024]{0:T(1024)}, u32[]{:S(2)}) copy-start(f32[1024]{0:T(1024)} %copy-done.79) | copy-start | bytes 12292
  812.8 66.2 %copy-start.38 = (bf16[1024,1536]{1,0:T(8,128)(2,1)}, bf16[1024,1536]{1,0:T(8,128)(2,1)S(1)}, u32[]{:S(2)}) copy-start(bf16[1024,1536]{1,0:T(8,128)(2,1)S(1)} %pad_maximum_fusion) | copy-start | bytes 9437188
  1025.6 36.1 %copy-start.28 = (bf16[320,8,176]{2,1,0:T(8,128)(2,1)S(1)}, bf16[320,8,176]{2,1,0:T(8,128)(2,1)}, u32[]{:S(2)}) copy-start(bf16[320,8,176]{2,1,0:T(8,128)(2,1)} %copy.257) | copy-start | bytes 2703364
  1026.0 37.2 %copy-start.29 = (bf16[320,8,176]{2,1,0:T(8,128)(2,1)S(1)}, bf16[320,8,176]{2,1,0:T(8,128)(2,1)}, u32[]{:S(2)}) copy-start(bf16[320,8,176]{2,1,0:T(8,128)(2,1)} %copy.255) | copy-start | bytes 2703364
  1135.4 17.2 %all-to-all-start.2 = ((bf16[4,320,256]{2,1,0:T(8,128)(2,1)}), bf16[4,320,256]{2,1,0:T(8,128)(2,1)S(1)}, u32[]{:S(2)}, u32[]{:S(2)}) async-start(bf16[4,320,256]{2,1,0:T(8,128)(2,1)} %reshape.638), calls=%async_computation.3 | async-start | bytes 1310720 | tf_op jit(solution)/shard_map/all_to_all | solution.py:1445
  1153.6 27.2 %copy-start.57 = (f32[40,1,64]{2,0,1:T(8,128)S(1)}, f32[40,1,64]{2,0,1:T(8,128)}, u32[]{:S(2)}) copy-start(f32[40,1,64]{2,0,1:T(8,128)} %slice.214) | copy-start | bytes 30724
  1153.6 27.1 %copy-start.58 = (f32[40,1,64]{2,0,1:T(8,128)S(1)}, f32[40,1,64]{2,0,1:T(8,128)}, u32[]{:S(2)}) copy-start(f32[40,1,64]{2,0,1:T(8,128)} %slice.217) | copy-start | bytes 30724
  1153.7 87.1 %slice-start = ((s8[5570560]{0:T(1024)(128)(4,1)}), s8[1376256]{0:T(1024)(128)(4,1)S(1)}, s32[]{:S(2)}) async-start(s8[5570560]{0:T(1024)(128)(4,1)} %bitcast.263), calls=%async_computation.7 | async-start | bytes 2752512
  1155.4 28.0 %copy-start.44 = (bf16[320,2,4,128]{3,2,1,0:T(4,128)(2,1)S(1)}, bf16[320,2,4,128]{3,2,1,0:T(4,128)(2,1)}, u32[]{:S(2)}) copy-start(bf16[320,2,4,128]{3,2,1,0:T(4,128)(2,1)} %copy.245) | copy-start | bytes 1966084
  1187.8 36.0 %copy-start.1 = (f32[1,5,64,1920]{3,2,1,0:T(8,128)S(1)}, f32[1,5,64,1920]{3,2,1,0:T(8,128)}, u32[]{:S(2)}) copy-start(f32[1,5,64,1920]{3,2,1,0:T(8,128)} %maximum_convert_fusion.1.grad) | copy-start | bytes 7372804
  1187.8 36.0 %copy-start.3 = (f32[1,5,64,1920]{3,2,1,0:T(8,128)S(1)}, f32[1,5,64,1920]{3,2,1,0:T(8,128)}, u32[]{:S(2)}) copy-start(f32[1,5,64,1920]{3,2,1,0:T(8,128)} %weight.4) | copy-start | bytes 7372804
  1187.8 53.0 %slice-start.1 = ((s8[5570560]{0:T(1024)(128)(4,1)}), s8[4194304]{0:T(1024)(128)(4,1)S(1)}, s32[]{:S(2)}) async-start(s8[5570560]{0:T(1024)(128)(4,1)} %bitcast.263), calls=%async_computation.8 | async-start | bytes 8388608
  (78 other events, 526.1 us)
Sparse Core Ops, SparseCore 0:
  779.8 113.4 reduce-scatter.4
  897.5 162.5 reduce-scatter.2

commit v4 on v3

--- a/solution.py
+++ b/solution.py
@@ -108,7 +108,7 @@
         first[...],
         second[...],
         average[...],
-        grad[...],
+        grad[...].astype(jnp.float32),
         scale_ref[0],
         rate,
         decay,
@@ -120,7 +120,7 @@
 
 def adam_blocks(weight, first, second, average, grad, scale, rate, decay, occupied):
     capacity, block_rows, cols = weight.shape[1:]
-    rows = 16
+    rows = 32
     block = pl.BlockSpec((1, 1, rows, cols), lambda i, j: (0, i, j, 0))
     scalar = pl.BlockSpec(memory_space=pltpu.SMEM)
     return pl.pallas_call(
@@ -129,7 +129,7 @@
         out_shape=[jax.ShapeDtypeStruct(weight.shape, weight.dtype)] * 4,
         in_specs=[scalar, scalar] + [block] * 5,
         out_specs=[block] * 4,
-        compiler_params=pltpu.CompilerParams(vmem_limit_bytes=40 * 2**20),
+        compiler_params=pltpu.CompilerParams(vmem_limit_bytes=48 * 2**20),
     )(scale.reshape(1), occupied, weight, first, second, average, grad)
 
 
@@ -236,39 +236,62 @@
     return peers
 
 
-def small_gather_kernel(nd, ns, everyone, count, *refs):
-    sources, outs, (sends, recvs) = refs[:count], refs[count : 2 * count], refs[2 * count :]
-    dp, st = lax.axis_index("dp"), lax.axis_index("state")
-    peers = []
-    for a in range(nd):
-        for b in range(ns if everyone else 1):
+def add_up(parts):
+    found = parts[0]
+    for part in parts[1:]:
+        found = found + part
+    return found
+
+
+def add_exponentials(parts):
+    top = parts[0][0]
+    for part in parts[1:]:
+        top = jnp.maximum(top, part[0])
+    total = add_up([part[1] * jnp.exp(part[0] - top) for part in parts])
+    return jnp.stack([top, total, add_up([part[2] for part in parts])])
+
+
+def combine_kernel(nd, ns, combine, in_ref, out_ref, near, far, sends, recvs):
+    dp, st, z, y, x, c = places(nd, ns)
+    deep = nd // 2
+    plane = []
+    for a in range(2):
+        for b in range(ns):
             if a or b:
-                peers.append((lax.rem(dp + a, nd), lax.rem(st + b, ns)))
-    greet(peers)
-    me = dp * ns + st if everyone else dp
+                plane.append((z * 2 + lax.rem(y + a, 2), lax.rem(st + b, ns)))
+    line = [(lax.rem(z + k, deep) * 2 + y, st) for k in range(1, deep)]
+    greet(plane + line)
     links = Links(sends, recvs)
-    for source, out in zip(sources, outs):
-        out[me] = source[...]
-        for there, far in peers:
-            links.copy(source, out.at[me], there, far)
-    for made in links.open:
-        made.wait_recv()
+    me = y * ns + st
+    near[me] = in_ref[...]
+    made = [links.copy(in_ref, near.at[me], *peer) for peer in plane]
+    for copy in made:
+        copy.wait_recv()
+    far[z] = combine([near[i] for i in range(2 * ns)])
+    made = [links.copy(far.at[z], far.at[z], *peer) for peer in line]
+    for copy in made:
+        copy.wait_recv()
+    out_ref[...] = combine([far[i] for i in range(deep)])
     links.finish()
 
 
-def small_gather(arrays, everyone, number):
+def combine_all(values, combine, number):
     nd, ns = lax.axis_size("dp"), lax.axis_size("state")
-    members = nd * ns if everyone else nd
-    copies = (members - 1) * len(arrays)
+    copies = 2 * ns - 1 + nd // 2 - 1
     vmem = pl.BlockSpec(memory_space=pltpu.VMEM)
     return pl.pallas_call(
-        functools.partial(small_gather_kernel, nd, ns, everyone, len(arrays)),
-        out_shape=[jax.ShapeDtypeStruct((members,) + a.shape, a.dtype) for a in arrays],
-        in_specs=[vmem] * len(arrays),
-        out_specs=[vmem] * len(arrays),
-        scratch_shapes=[pltpu.SemaphoreType.DMA((copies,)), pltpu.SemaphoreType.DMA((copies,))],
+        functools.partial(combine_kernel, nd, ns, combine),
+        out_shape=jax.ShapeDtypeStruct(values.shape, values.dtype),
+        in_specs=[vmem],
+        out_specs=vmem,
+        scratch_shapes=[
+            pltpu.VMEM((2 * ns,) + values.shape, values.dtype),
+            pltpu.VMEM((nd // 2,) + values.shape, values.dtype),
+            pltpu.SemaphoreType.DMA((copies,)),
+            pltpu.SemaphoreType.DMA((copies,)),
+        ],
         compiler_params=pltpu.CompilerParams(collective_id=number, has_side_effects=True),
-    )(*arrays)
+    )(values)
 
 
 def gather_all_kernel(nd, ns, in_ref, out_ref, sends, recvs):
@@ -940,12 +963,12 @@
             dffn[cols, :inner_cols] = lax.dot_general(
                 rows_ref[:, cols], dgu[...], (((0,), (0,)), ((), ())),
                 preferred_element_type=jnp.float32,
-            ).astype(dffn.dtype)
+            ).astype(dgu.dtype)
             dffn[cols, inner_cols:] = lax.dot_general(
                 flat_down[:, :, :, :, :, cols].reshape(every, span), hidden_ref[...],
                 (((0,), (0,)), ((), ())),
                 preferred_element_type=jnp.float32,
-            ).astype(dffn.dtype)
+            ).astype(dgu.dtype)
 
         home = pltpu.make_async_copy(dffn, ffn_out, local.at[1])
         home.start()
@@ -1239,7 +1262,6 @@
 
     in_own = lowered(in_weight)
     out_own = lowered(out_weight)
-    table_own = lowered(table_weight)
 
     def in_rows(flat):
         flat = jnp.pad(flat, (0, -flat.shape[0] % (16 * LANES)))
@@ -1251,7 +1273,9 @@
     rest_sent = jnp.concatenate(
         [in_own[:, 2 * key_cols : mixer_cols], out_own[:, :value_width]], axis=1
     )
-    table_padded = jnp.pad(table_own, ((0, 0), (0, nd * vocab_part - vocab_share)))
+    table_padded = lowered(
+        jnp.pad(table_weight, ((0, 0), (0, 0), (0, 0), (0, nd * vocab_part - vocab_share)))
+    )
 
     def by_part(columns, parts):
         return columns.reshape(own, nd, parts)
@@ -1379,12 +1403,11 @@
     top_here = jnp.max(logits, axis=1)
     sum_here = jnp.sum(jnp.exp(logits - top_here[:, None]), axis=1)
     picked_here = jnp.sum(jnp.where(target_hit, logits, 0.0), axis=1)
-    shares = small_gather(
-        [jnp.stack([top_here, sum_here, picked_here]).reshape(-1, LANES)], True, 6
-    )[0].reshape(nd * ns, 3, -1)
-    top = jnp.max(shares[:, 0], axis=0)
-    lse = top + jnp.log(jnp.sum(shares[:, 1] * jnp.exp(shares[:, 0] - top[None]), axis=0))
-    loss_sum = jnp.sum((lse - jnp.sum(shares[:, 2], axis=0)) * live)
+    shares = combine_all(
+        jnp.stack([top_here, sum_here, picked_here]).reshape(3, -1, LANES), add_exponentials, 6
+    ).reshape(3, -1)
+    lse = shares[0] + jnp.log(shares[1])
+    loss_sum = jnp.sum((lse - shares[2]) * live)
     probs = jnp.exp(logits - lse[:, None])
     dlogits = ((probs - target_hit.astype(f32)) * (live / count)[:, None]).astype(bf16)
     grad_table_part = times_left(rows_three, dlogits).astype(bf16)
@@ -1404,13 +1427,10 @@
         7,
     )
     grad_gain_three, grad_gain_four = gain_pair
-    grad_table_own = join_columns(grad_table_back)[:, :vocab_share].astype(f32)
-    grad_ffn = swap_dp(grad_ffn.reshape(nd, own, gu_cols + down_cols))
 
     grad_gated = times_plain(grad_one, w_o)
-    grad_o_own = lax.psum_scatter(
-        times_left(grad_one, gated).astype(bf16), "dp", scatter_dimension=0, tiled=True
-    )
+    grad_o_part = times_left(grad_one, gated).astype(bf16)
+    grad_gated, grad_o_part = lax.optimization_barrier((grad_gated, grad_o_part))
     grad_mixed, grad_gain_two = back_head(grad_gated)
     grad_query, grad_key, grad_forget, grad_value = back_mix(
         grad_mixed.astype(bf16).astype(f32)
@@ -1419,69 +1439,98 @@
     grad_query_pre = times_left(pick, grad_query_pre)
     (grad_forget_pre,) = back_gates((grad_key, grad_forget))
     grad_qfv = jnp.concatenate([grad_query_pre, grad_forget_pre, grad_value], axis=1).astype(bf16)
-    grad_qfv, grad_ffn = lax.optimization_barrier((grad_qfv, grad_ffn))
     pick_mine = lax.dynamic_slice_in_dim(pick_low, me_state * quarter, quarter, axis=1)
+    grad_rows = times_right(w_qfv, grad_qfv).astype(bf16)
+    grad_w_qfv = times_plain(normed_one, grad_qfv).astype(bf16)
+    grad_rows, grad_w_qfv = lax.optimization_barrier((grad_rows, grad_w_qfv))
     embed, grad_gain_one = rows_back(
-        times_right(w_qfv, grad_qfv).astype(bf16),
+        grad_rows,
         stream_mine,
         gains[0][:, None],
         times_left(grad_one, pick_mine),
         width,
         8,
     )
+    embed, grad_ffn, grad_table_back = lax.optimization_barrier(
+        (embed, grad_ffn, grad_table_back)
+    )
+    grad_ffn = swap_dp(grad_ffn.reshape(nd, own, gu_cols + down_cols))
     grad_gain_one = grad_gain_one[:, 0]
-    grad_w_qfv = times_plain(normed_one, grad_qfv).astype(bf16)
 
     def sum_dp(values):
         return lax.psum_scatter(values, "dp", scatter_dimension=0, tiled=True)
 
+    def square_sum(values):
+        values = values.astype(f32)
+        return jnp.sum(values * values)
+
     grad_qfv_own = sum_dp(grad_w_qfv)
-    grad_lookup = times_right(embed, hit.astype(bf16))
-    grad_qfv_own, grad_lookup = lax.optimization_barrier((grad_qfv_own, grad_lookup))
-    own_table = grad_table_own + grad_lookup
+    grad_o_own = sum_dp(grad_o_part)
+    own_table = times_right(embed, hit.astype(bf16)) + join_columns(grad_table_back)[
+        :, :vocab_share
+    ].astype(f32)
+    squares = square_sum(own_table)
+    grad_ffn, squares = lax.optimization_barrier((grad_ffn, squares))
+    squares = squares + square_sum(grad_ffn)
+    grad_gate = join_columns(grad_ffn[:, :, :unit_part])
+    grad_up = join_columns(grad_ffn[:, :, unit_part : 2 * unit_part])
+    grad_down = join_columns(grad_ffn[:, :, gu_cols : gu_cols + unit_part])
+    grad_qfv_own, grad_o_own, squares, grad_gate, grad_up, grad_down = lax.optimization_barrier(
+        (grad_qfv_own, grad_o_own, squares, grad_gate, grad_up, grad_down)
+    )
+    squares = squares + square_sum(grad_qfv_own) + square_sum(grad_o_own)
 
     grad_keys = grad_qfv_own[:, : 2 * qcols].reshape(own, 2, ns, key_part)
     grad_keys = grad_keys.transpose(2, 0, 1, 3).reshape(ns, own, 2 * key_part)
     grad_keys = lax.all_to_all(grad_keys, "state", split_axis=0, concat_axis=0, tiled=True)
+
+    head_full = lax.dynamic_update_slice_in_dim(
+        jnp.zeros((width,), f32), grad_gain_two, me_state * value_width, 0
+    )
+    gain_parts = jnp.concatenate([grad_gain_one, grad_gain_three, grad_gain_four, head_full])
+    sums = jnp.concatenate([gain_parts, squares[None]])
+    sums = jnp.pad(sums, (0, -sums.shape[0] % (8 * LANES))).reshape(-1, LANES)
+    sums = combine_all(sums, add_up, 10).reshape(-1)
+    gain_sums = sums[: 3 * wide + width]
+    head_slots = (
+        jnp.zeros((nd * capacity, block_rows), f32)
+        .at[index]
+        .set(gain_sums[3 * wide :].reshape(block_count, block_rows))
+    )
+    gain_slots = gain_sums[: 3 * wide].reshape(3, nd * capacity, block_rows)
+    gain_slots = jnp.stack([gain_slots[0], head_slots, gain_slots[1], gain_slots[2]], axis=1)
+    own_gain = lax.dynamic_slice_in_dim(gain_slots, me_dp * capacity, capacity)
+
+    squares_all = sums[3 * wide + width] + jnp.sum(gain_sums * gain_sums)
+    grad_norm = jnp.sqrt(squares_all)
+    scale = jnp.minimum(1.0, CLIP_NORM / (grad_norm + 1e-06))
+    occupied = occupied_here.astype(f32)
+    new_table = adam_blocks(
+        table_weight,
+        table_first,
+        table_second,
+        table_average,
+        own_table.reshape(table_weight.shape),
+        scale,
+        LEARN_RATE,
+        WEIGHT_DECAY,
+        occupied,
+    )
+    grad_keys, grad_gate, _ = lax.optimization_barrier(
+        (grad_keys, grad_gate, new_table[0][0, 0, :8, :LANES])
+    )
     grad_keys = grad_keys.reshape(ns, own, 2, key_part).transpose(1, 2, 0, 3)
-    grad_gate = grad_ffn[:, :, :unit_part]
-    grad_up = grad_ffn[:, :, unit_part : 2 * unit_part]
-    grad_down = grad_ffn[:, :, gu_cols : gu_cols + unit_part]
     own_in = jnp.concatenate(
         [
             grad_keys.reshape(own, 2 * key_cols),
             grad_qfv_own[:, 2 * qcols :],
-            join_columns(grad_gate),
-            join_columns(grad_up),
+            grad_gate,
+            grad_up,
         ],
         axis=1,
-    ).astype(f32)
-    own_out = jnp.concatenate(
-        [grad_o_own, join_columns(grad_down)],
-        axis=1,
-    ).astype(f32)
-
-    head_full = lax.dynamic_update_slice_in_dim(
-        jnp.zeros((width,), f32), grad_gain_two, me_state * value_width, 0
-    )
-    gain_parts = jnp.concatenate([grad_gain_one, grad_gain_three, grad_gain_four, head_full])
-    gain_parts = small_gather([in_rows(gain_parts.astype(bf16))], True, 11)[0]
-    gain_sums = jnp.sum(gain_parts.reshape(nd * ns, -1)[:, : 3 * wide + width].astype(f32), axis=0)
-    head_slots = (
-        jnp.zeros((nd * capacity, block_rows), f32)
-        .at[index]
-        .set(gain_sums[3 * wide :].reshape(block_count, block_rows))
-    )
-    gain_slots = gain_sums[: 3 * wide].reshape(3, nd * capacity, block_rows)
-    gain_slots = jnp.stack([gain_slots[0], head_slots, gain_slots[1], gain_slots[2]], axis=1)
-    own_gain = lax.dynamic_slice_in_dim(gain_slots, me_dp * capacity, capacity)
-
-    squares = jnp.sum(own_in * own_in) + jnp.sum(own_out * own_out) + jnp.sum(own_table * own_table)
-    squares = small_gather([jnp.full((8, LANES), squares)], True, 10)[0][:, 0, 0]
-    squares_all = jnp.sum(squares) + jnp.sum(gain_sums * gain_sums)
-    grad_norm = jnp.sqrt(squares_all)
-    scale = jnp.minimum(1.0, CLIP_NORM / (grad_norm + 1e-06))
-    occupied = occupied_here.astype(f32)
+    )
+    own_out = jnp.concatenate([grad_o_own, grad_down], axis=1)
+
     new_in = adam_blocks(
         in_weight,
         in_first,
@@ -1499,17 +1548,6 @@
         out_second,
         out_average,
         own_out.reshape(out_weight.shape),
-        scale,
-        LEARN_RATE,
-        WEIGHT_DECAY,
-        occupied,
-    )
-    new_table = adam_blocks(
-        table_weight,
-        table_first,
-        table_second,
-        table_average,
-        own_table.reshape(table_weight.shape),
         scale,
         LEARN_RATE,
         WEIGHT_DECAY,

time: 1280 us -> 1200 us (0.938)
  local copies, waits for them, and re-layouts: 153 us -> 99.5 us
  starting transfers between devices: 14.3 us -> 39.9 us
  Pallas kernels: 782 us -> 758 us
  waiting for transfers between devices: 53.9 us -> 32.2 us
  other arithmetic: 60.7 us -> 44.7 us
    pallas_call x3 -> x2, Pallas kernels: 62 us -> 27.8 us  [combine_all(): pl.pallas_call(functools.partial(combine_kernel, nd, ns, combine), out_sh...]
    all_to_all x2, starting transfers between devices: 10.5 us -> 36.1 us  [swap_dp(): return lax.all_to_all(values, 'dp', split_axis=0, concat_axis=0, tiled=True)]
    all_to_all x2, waiting for transfers between devices: 53.2 us -> 32.1 us  [swap_dp(): return lax.all_to_all(values, 'dp', split_axis=0, concat_axis=0, tiled=True)]
    unnamed x197 -> x180, local copies, waits for them, and re-layouts: 37.7 us -> 18.1 us
    pallas_call x1, Pallas kernels: 95.2 us -> 110 us  [rows_back(): pl.pallas_call(functools.partial(rows_back_kernel, nd, ns, width), out_sh...]
    reduce_sum x9 -> x6, other arithmetic: 23.9 us -> 10.4 us  [the longest x3 8.38 us: square_sum(): return jnp.sum(values * values)]
  transfers between devices with their start and end apart: 5 -> 5, of which waited for: 2 -> 1; matrix products, arithmetic and copies ran while one was open for 21% -> 16% of each run, Pallas kernels for 23% -> 27%
where the time goes in v4:
time: 1200 us; the launch traced here: 1190 us
  Pallas kernels  758 us (63%)
  matrix products  191 us (16%)
  local copies, waits for them, and re-layouts  99.5 us (8%)
  other arithmetic  44.7 us (4%)
  starting transfers between devices  39.9 us (3%)
  waiting for transfers between devices  32.2 us (3%)
  between operations  22 us (2%)
    pallas_call x1, Pallas kernels, front(): pl.pallas_call(functools.partial(front_kernel, nd, ns, vocab), out_shape=...  202 us
    pallas_call x1, Pallas kernels, slots_back(): pl.pallas_call(functools.partial(slots_back_kernel, nd, ns, width, units)...  186 us
    pallas_call x2, Pallas kernels, gather_all(): pl.pallas_call(functools.partial(gather_all_kernel, nd, ns), out_shape=ja...  112 us
    pallas_call x1, Pallas kernels, rows_back(): pl.pallas_call(functools.partial(rows_back_kernel, nd, ns, width), out_sh...  110 us
    dot_general x6, matrix products, times_right(): lax.dot_general(left, right, (((1,), (1,)), ((), ())), preferred_element_...  93 us
    pallas_call x3, Pallas kernels, adam_blocks(): pl.pallas_call(functools.partial(adam_kernel, rate, decay), grid=(capacit...  62.6 us
    pallas_call x1, Pallas kernels, scatter_all(): pl.pallas_call(functools.partial(scatter_all_kernel, nd, ns), out_shape=j...  46.5 us
    all_to_all x2, starting transfers between devices, swap_dp(): return lax.all_to_all(values, 'dp', split_axis=0, concat_axis=0, tiled=True)  36.1 us
  transfers between devices with their start and end apart: 5, of which 1 were waited for; matrix products, arithmetic and copies ran while one was open for 16% of the time, Pallas kernels for 27%

profile of v4, /device:TPU:0, one launch (start us, length us, event | category | flops | bytes accessed | tf_op | source)
XLA Modules:
  0.0 1187.7 jit_solution(13743436595959941671)
XLA Ops:
  40.1 7.8 concatenate.41
  47.9 202.4 %shard_map.348 = (s32[8,16,128]{2,1,0:T(8,128)S(1)}, bf16[8,16,128]{2,1,0:T(8,128)(2,1)S(1)}, bf16[2560,1024]{1,0:T(8,128)(2,1)}, bf16[4,8,320,256]{3,2,1,0:T(8,...) custom-call(s32[16,128]{1,0:T(8,128)S(1)} %pad_bitcast_fusion.1.small_ref, ...), custom_call_target="tpu_custom_call" | custom-call | flops 42949672960 | bytes 6553600 | tf_op jit(solution)/shard_map/pallas_call | solution.py:816
  298.0 8.4 fusion.61
  318.8 11.1 shard_map.349
  334.4 75.3 %shard_map.350 = bf16[2,2,2,4,32,2560]{5,4,3,2,1,0:T(8,128)(2,1)S(1)} custom-call(bf16[32,2560]{1,0:T(8,128)(2,1)S(1)} %multiply_convert_fusion.3.in_ref), custom_call_target="tpu_custom_call" | custom-call | tf_op jit(solution)/shard_map/pallas_call | solution.py:382
  416.3 46.5 %shard_map.351 = f32[32,2560]{1,0:T(8,128)S(1)} custom-call(bf16[2,2,2,4,32,2560]{5,4,3,2,1,0:T(8,128)(2,1)S(1)} %bitcast.229), custom_call_target="tpu_custom_call" | custom-call | tf_op jit(solution)/shard_map/pallas_call | solution.py:529
  463.2 36.7 %shard_map.352 = bf16[2,2,2,4,32,2560]{5,4,3,2,1,0:T(8,128)(2,1)S(1)} custom-call(bf16[32,2560]{1,0:T(8,128)(2,1)S(1)} %multiply_convert_fusion.2.in_ref), custom_call_target="tpu_custom_call" | custom-call | tf_op jit(solution)/shard_map/pallas_call | solution.py:382
  503.2 9.4 select_reduce_fusion.2
  517.1 14.2 %shard_map.353 = f32[3,8,128]{2,1,0:T(8,128)} custom-call(f32[3,8,128]{2,1,0:T(8,128)} %pad_maximum_fusion.6.in_ref), custom_call_target="tpu_custom_call" | custom-call | tf_op jit(solution)/shard_map/pallas_call | solution.py:282
  533.4 11.8 convolution_convert_fusion.2
  545.2 11.1 convolution_convert_fusion.3
  556.4 185.9 %shard_map.354 = (bf16[4,32,2560]{2,1,0:T(8,128)(2,1)}, bf16[8,320,1024]{2,1,0:T(8,128)(2,1)}, bf16[2560,640]{1,0:T(8,128)(2,1)}, f32[2,2560]{1,0:T(2,128)}) custom-call(bf16[2,2,2,4,32,2560]{5,4,3,2,1,0:T(8,128)(2,1)} %bitcast.317, bf16[8,320,1024]{2,1,0:T(8,128)(2,1)} %bitcast.316, f32[32,2560]{1,0:T(8,128)} %copy-done.33, f32[32,2560]{1,0:T(8,128)} %copy-done.23, ...), custom_call_target="tpu_custom_call" | custom-call | flops 13421772800 | bytes 262144000 | tf_op jit(solution)/shard_map/pallas_call | solution.py:1003
  757.4 7.8 select_reduce_fusion
  768.9 6.9 fusion.2
  790.7 11.1 convolution_convert_fusion
  801.7 12.9 %fusion.17.in_ref = bf16[2560,1024]{1,0:T(8,128)(2,1)} fusion(bf16[2560,512]{1,0:T(8,128)(2,1)S(1)} %copy-done.26, bf16[2560,512]{1,0:T(8,128)(2,1)} %bitcast.278, bf16[2560,512]{1,0:T(8,128)(2,1)} %bitcast.279, bf16[1024,512]{1,0:T(8,128)(2,1)} %copy.236, bf16[1024,512]{1,0:T(8,128)(2,1)} %copy-done.34, bf16[1024,512]{1,0:T(8,128)(2,1)} %copy-done.76), kind=kOutput, calls=%fused_computation.27 | convolution fusion | flops 8088715264 | bytes 16252928 | tf_op jit(solution)/shard_map/dot_general | solution.py:141
  821.1 110.0 %shard_map.355 = (bf16[320,8192]{1,0:T(8,128)(2,1)}, f32[2560,1]{1,0:T(8,128)S(1)}) custom-call(bf16[2560,1024]{1,0:T(8,128)(2,1)} %fusion.17.in_ref, bf16[2560,256]{1,0:T(8,128)(2,1)S(1)} %constant_dynamic-slice_fusion.stream_ref, f32[2560,1]{1,0:T(8,128)S(1)} %broadcast_in_dim_squeeze.3.gain_ref, f32[2560,256]{1,0:T(8,128)} %fusion.104.more_ref), custom_call_target="tpu_custom_call" | custom-call | bytes 157286400 | tf_op jit(solution)/shard_map/pallas_call | solution.py:1145
  934.3 30.3 %all-to-all-start.1 = ((bf16[8,320,640]{2,1,0:T(8,128)(2,1)}), bf16[8,320,640]{2,1,0:T(8,128)(2,1)}, u32[]{:S(2)}, u32[]{:S(2)}) async-start(bf16[8,320,640]{2,1,0:T(8,128)(2,1)} %bitcast.275), calls=%async_computation.3 | async-start | bytes 6553600 | tf_op jit(solution)/shard_map/all_to_all | solution.py:170
  965.3 59.6 %multiply_reduce_fusion = (f32[]{:T(128)}, f32[320,8000]{1,0:T(8,128)}) fusion(bf16[320,8192]{1,0:T(8,128)(2,1)} %bitcast.263, bf16[320,8192]{1,0:T(8,128)(2,1)} %get-tuple-element.81, s32[8192]{0:T(1024)S(1)} %bitcast.303), kind=kOutput, calls=%fused_computation.18 | convolution fusion | flops 42018816000 | bytes 20635652 | tf_op jit(solution)/shard_map/dot_general | solution.py:141
  1024.8 32.1 %all-to-all-done.1 = bf16[8,320,640]{2,1,0:T(8,128)(2,1)} async-done(((bf16[8,320,640]{2,1,0:T(8,128)(2,1)}), bf16[8,320,640]{2,1,0:T(8,128)(2,1)}, u32[]{:S(2)}, u32[]{:S(2)}) %all-to-all-start.1) | async-done | bytes 3276832 | tf_op jit(solution)/shard_map/all_to_all | solution.py:170
  1080.4 13.6 %shard_map.356 = f32[80,128]{1,0:T(8,128)} custom-call(f32[80,128]{1,0:T(8,128)} %pad_bitcast_fusion.in_ref), custom_call_target="tpu_custom_call" | custom-call | tf_op jit(solution)/shard_map/pallas_call | solution.py:282
  1108.5 32.9 %shard_map.359 = (f32[1,5,64,8000]{3,2,1,0:T(8,128)}, f32[1,5,64,8000]{3,2,1,0:T(8,128)}, f32[1,5,64,8000]{3,2,1,0:T(8,128)}, f32[1,5,64,8000]{3,2,1,0:T(8,128)}) custom-call(f32[1]{0:T(128)} %bitcast.76.scale_ref, f32[5]{0:T(128)S(1)} %get-tuple-element.163.held_ref, f32[1,5,64,8000]{3,2,1,0:T(8,128)} %weight.5, f32[1,5,64,8000]{3,2,1,0:T(8,128)} %first.5, ...), custom_call_target="tpu_custom_call" | custom-call | tf_op jit(solution)/shard_map/pallas_call | solution.py:126
  1141.4 10.4 shard_map.358
  1160.0 19.3 %shard_map.357 = (f32[1,5,64,4352]{3,2,1,0:T(8,128)}, f32[1,5,64,4352]{3,2,1,0:T(8,128)}, f32[1,5,64,4352]{3,2,1,0:T(8,128)}, f32[1,5,64,4352]{3,2,1,0:T(8,128)}) custom-call(f32[1]{0:T(128)} %bitcast.76.scale_ref, f32[5]{0:T(128)S(1)} %get-tuple-element.163.held_ref, f32[1,5,64,4352]{3,2,1,0:T(8,128)} %weight.3, f32[1,5,64,4352]{3,2,1,0:T(8,128)} %first.3, ...), custom_call_target="tpu_custom_call" | custom-call | tf_op jit(solution)/shard_map/pallas_call | solution.py:126
  (365 shorter events, 198.1 us)
Async XLA Ops:
  9.4 300.8 %copy-start.72 = (s32[32]{0:T(128)}, s32[32]{0:T(128)S(1)}, u32[]{:S(2)}) copy-start(s32[32]{0:T(128)S(1)} %get-tuple-element.146) | copy-start | bytes 388
  47.9 202.4 %slice-start.4 = ((s8[5242880]{0:T(1024)(128)(4,1)}), s8[4194304]{0:T(1024)(128)(4,1)S(1)}, s32[]{:S(2)}) async-start(s8[5242880]{0:T(1024)(128)(4,1)} %bitcast.242), calls=%async_computation.11 | async-start | bytes 8388608
  47.9 202.4 %slice-start.5 = ((s8[5242880]{0:T(1024)(128)(4,1)}), s8[1048576]{0:T(1024)(128)(4,1)S(1)}, s32[]{:S(2)}) async-start(s8[5242880]{0:T(1024)(128)(4,1)} %bitcast.242), calls=%async_computation.12 | async-start | bytes 2097152
  253.5 249.7 %all-to-all-start = ((bf16[8,320,1024]{2,1,0:T(8,128)(2,1)}), bf16[8,320,1024]{2,1,0:T(8,128)(2,1)}, u32[]{:S(2)}, u32[]{:S(2)}) async-start(bf16[8,320,1024]{2,1,0:T(8,128)(2,1)} %bitcast.241), calls=%async_computation | async-start | bytes 10485760 | tf_op jit(solution)/shard_map/all_to_all | solution.py:170
  259.4 813.0 %reduce-scatter.5.cloned.1.call-start = ((), (), s32[]{:S(2)}) async-start(), calls=%async_computation.6 | async-start | bytes 2949120 | tf_op jit(solution)/shard_map/reduce_scatter | solution.py:1461
  267.7 19.7 %copy-start.70 = (f32[1024]{0:T(1024)}, f32[1024]{0:T(1024)S(1)}, u32[]{:S(2)}) copy-start(f32[1024]{0:T(1024)S(1)} %add_rsqrt_fusion) | copy-start | bytes 12292
  267.8 19.6 %copy-start.63 = (f32[2560]{0:T(1024)}, f32[2560]{0:T(1024)S(1)}, u32[]{:S(2)}) copy-start(f32[2560]{0:T(1024)S(1)} %mul.384) | copy-start | bytes 30724
  311.7 439.2 %copy-start.32 = (pred[128,1024]{1,0:T(8,128)(4,1)}, pred[128,1024]{1,0:T(8,128)(4,1)S(1)}, u32[]{:S(2)}) copy-start(pred[128,1024]{1,0:T(8,128)(4,1)S(1)} %get-tuple-element.145) | copy-start | bytes 393220
  315.1 19.1 %copy-start.39 = (bf16[128,4,128]{0,2,1:T(8,128)(2,1)}, bf16[128,4,128]{0,2,1:T(8,128)(2,1)S(1)}, u32[]{:S(2)}) copy-start(bf16[128,4,128]{0,2,1:T(8,128)(2,1)S(1)} %multiply_convert_fusion.4) | copy-start | bytes 393220
  334.3 128.6 %copy-start.23 = (f32[32,2560]{1,0:T(8,128)}, f32[32,2560]{1,0:T(8,128)S(1)}, u32[]{:S(2)}) copy-start(f32[32,2560]{1,0:T(8,128)S(1)} %get-tuple-element.155.one_ref) | copy-start | bytes 983044
  334.4 75.4 %copy-start.17 = (bf16[8,320,640]{2,1,0:T(8,128)(2,1)S(1)}, bf16[8,320,640]{2,1,0:T(8,128)(2,1)}, u32[]{:S(2)}) copy-start(bf16[8,320,640]{2,1,0:T(8,128)(2,1)} %get-tuple-element.67) | copy-start | bytes 9830404
  463.1 36.9 %copy-start.33 = (f32[32,2560]{1,0:T(8,128)}, f32[32,2560]{1,0:T(8,128)S(1)}, u32[]{:S(2)}) copy-start(f32[32,2560]{1,0:T(8,128)S(1)} %get-tuple-element.125.two_ref) | copy-start | bytes 983044
  463.2 39.3 %copy-start.44 = (f32[2,40,64]{2,0,1:T(2,128)S(1)}, f32[2,40,64]{2,0,1:T(2,128)}, u32[]{:S(2)}) copy-start(f32[2,40,64]{2,0,1:T(2,128)} %slice.210) | copy-start | bytes 61444
  556.4 185.9 %copy-start.40 = (bf16[128,4,128]{0,2,1:T(8,128)(2,1)S(1)}, bf16[128,4,128]{0,2,1:T(8,128)(2,1)}, u32[]{:S(2)}) copy-start(bf16[128,4,128]{0,2,1:T(8,128)(2,1)} %copy-done.39) | copy-start | bytes 393220
  782.0 290.4 %reduce-scatter.3.cloned.1.call-start = ((), (), s32[]{:S(2)}) async-start(), calls=%async_computation.5 | async-start | bytes 8847360 | tf_op jit(solution)/shard_map/reduce_scatter | solution.py:1461
  818.1 112.9 %slice-start.8 = ((s8[5242880]{0:T(1024)(128)(4,1)}), s8[4194304]{0:T(1024)(128)(4,1)S(1)}, s32[]{:S(2)}) async-start(s8[5242880]{0:T(1024)(128)(4,1)} %bitcast.259), calls=%async_computation.15 | async-start | bytes 8388608
  821.1 110.0 %slice-start.9 = ((s8[5242880]{0:T(1024)(128)(4,1)}), s8[1048576]{0:T(1024)(128)(4,1)S(1)}, s32[]{:S(2)}) async-start(s8[5242880]{0:T(1024)(128)(4,1)} %bitcast.259), calls=%async_computation.16 | async-start | bytes 2097152
  934.3 30.7 %copy-start.58 = (f32[2,2560]{1,0:T(2,128)S(1)}, f32[2,2560]{1,0:T(2,128)}, u32[]{:S(2)}) copy-start(f32[2,2560]{1,0:T(2,128)} %get-tuple-element.74) | copy-start | bytes 61444
  934.3 30.9 %copy-start.66 = (f32[4,128]{1,0:T(4,128)S(1)}, f32[4,128]{1,0:T(4,128)}, u32[]{:S(2)}) copy-start(f32[4,128]{1,0:T(4,128)} %get-tuple-element.110) | copy-start | bytes 6148
  934.3 122.7 %all-to-all-start.1 = ((bf16[8,320,640]{2,1,0:T(8,128)(2,1)}), bf16[8,320,640]{2,1,0:T(8,128)(2,1)}, u32[]{:S(2)}, u32[]{:S(2)}) async-start(bf16[8,320,640]{2,1,0:T(8,128)(2,1)} %bitcast.275), calls=%async_computation.3 | async-start | bytes 6553600 | tf_op jit(solution)/shard_map/all_to_all | solution.py:170
  1072.4 22.4 %slice-start.12 = ((bf16[320,1536]{1,0:T(8,128)(2,1)}), bf16[320,1024]{1,0:T(8,128)(2,1)S(1)}, s32[]{:S(2)}) async-start(bf16[320,1536]{1,0:T(8,128)(2,1)} %reduce-scatter.3.cloned.1.call-done), calls=%async_computation.19 | async-start | bytes 1310720 | tf_op jit(solution)/shard_map/slice | solution.py:1483
  1097.1 56.1 %all-to-all-start.2 = ((bf16[4,320,256]{2,1,0:T(8,128)(2,1)}), bf16[4,320,256]{2,1,0:T(8,128)(2,1)S(1)}, u32[]{:S(2)}, u32[]{:S(2)}) async-start(bf16[4,320,256]{2,1,0:T(8,128)(2,1)} %reshape.546), calls=%async_computation.4 | async-start | bytes 1310720 | tf_op jit(solution)/shard_map/all_to_all | solution.py:1485
  1108.4 32.9 %copy-start.1 = (f32[1,5,64,1920]{3,2,1,0:T(8,128)S(1)}, f32[1,5,64,1920]{3,2,1,0:T(8,128)}, u32[]{:S(2)}) copy-start(f32[1,5,64,1920]{3,2,1,0:T(8,128)} %weight.4) | copy-start | bytes 7372804
  1108.5 32.9 %copy-start.4 = (f32[1,5,64,1920]{3,2,1,0:T(8,128)S(1)}, f32[1,5,64,1920]{3,2,1,0:T(8,128)}, u32[]{:S(2)}) copy-start(f32[1,5,64,1920]{3,2,1,0:T(8,128)} %first.4) | copy-start | bytes 7372804
  (72 other events, 392.7 us)
Sparse Core Ops, SparseCore 0:
  782.1 72.9 reduce-scatter.4
  859.3 212.5 reduce-scatter.2

commit v5 on v4

--- a/solution.py
+++ b/solution.py
@@ -392,11 +392,29 @@
     return out.reshape(nd * ns * rows, wide)
 
 
-def scatter_all_kernel(nd, ns, in_ref, out_ref, *scratch):
+def scatter_all_kernel(nd, ns, in_ref, cargo_ref, out_ref, cargo_out, local, *scratch):
     sends, recvs = scratch[-2:]
-    greet(near_peers(nd, ns))
+    dp, st, z, y, x, c = places(nd, ns)
+    dp_peers = [(lax.rem(dp + k, nd), st) for k in range(1, nd)]
+    x_peers = [(dp, lax.rem(x + k, ns // 2) * 2 + c) for k in range(1, ns // 2)]
+    greet(dp_peers + x_peers + [(dp, st + 1 - 2 * c)])
     links = Links(sends, recvs)
-    scatter_body(nd, ns, links, in_ref, out_ref, scratch[:-2])
+    own_copy = pltpu.make_async_copy(cargo_ref.at[dp], cargo_out.at[dp], local.at[0])
+    own_copy.start()
+    chunk = cargo_ref.shape[1] // CHUNKS
+    queue = [(peer, i) for i in range(CHUNKS) for peer in dp_peers]
+    third = -(-len(queue) // 3)
+    pieces = []
+
+    def feed(place):
+        for peer, i in queue[place * third : (place + 1) * third]:
+            rows = pl.ds(i * chunk, chunk)
+            pieces.append(links.copy(cargo_ref.at[peer[0], rows], cargo_out.at[dp, rows], *peer))
+
+    scatter_body(nd, ns, links, in_ref, out_ref, scratch[:-2], feed)
+    for made in pieces:
+        made.wait_recv()
+    own_copy.wait()
     links.finish()
 
 
@@ -519,24 +537,29 @@
     ]
 
 
-def scatter_all(values, number):
+def scatter_all(values, cargo, number):
     nd, ns = lax.axis_size("dp"), lax.axis_size("state")
     deep, across = nd // 2, ns // 2
     rows, wide = values.shape[0] // (nd * ns), values.shape[1]
-    copies = scatter_copies(nd, ns)
+    copies = scatter_copies(nd, ns) + (nd - 1) * CHUNKS
     vmem = pl.BlockSpec(memory_space=pltpu.VMEM)
+    hbm = pl.BlockSpec(memory_space=pl.ANY)
     kind = values.dtype
     return pl.pallas_call(
         functools.partial(scatter_all_kernel, nd, ns),
-        out_shape=jax.ShapeDtypeStruct((rows, wide), jnp.float32),
-        in_specs=[vmem],
-        out_specs=vmem,
-        scratch_shapes=scatter_scratch(nd, ns, rows, wide, kind)
+        out_shape=[
+            jax.ShapeDtypeStruct((rows, wide), jnp.float32),
+            jax.ShapeDtypeStruct(cargo.shape, cargo.dtype),
+        ],
+        in_specs=[vmem, hbm],
+        out_specs=[vmem, hbm],
+        scratch_shapes=[pltpu.SemaphoreType.DMA((1,))]
+        + scatter_scratch(nd, ns, rows, wide, kind)
         + [pltpu.SemaphoreType.DMA((copies,)), pltpu.SemaphoreType.DMA((copies,))],
         compiler_params=pltpu.CompilerParams(
             collective_id=number, has_side_effects=True, vmem_limit_bytes=40 * 2**20
         ),
-    )(values.reshape(2, across, 2, deep, rows, wide))
+    )(values.reshape(2, across, 2, deep, rows, wide), cargo)
 
 
 def front_kernel(
@@ -1337,7 +1360,10 @@
     w_gu = parts_all[:, :gu_cols]
     w_d = parts_all[:, gu_cols:]
     table_padded, stream = lax.optimization_barrier((table_padded, stream))
-    table = swap_dp(spread_columns(table_padded, nd)).reshape(wide, vocab_part)
+    table_parts = spread_columns(table_padded, nd)
+    late_cols = max(LANES, vocab_part // (4 * LANES) * LANES)
+    early_cols = vocab_part - late_cols
+    table_early = swap_dp(table_parts[:, :, :early_cols])
 
     positions = loss_positions[0]
     pick_hit = positions[:, None] == jnp.arange(tokens)[None, :]
@@ -1390,7 +1416,11 @@
     rows_two = gather_all(normed_two.astype(bf16), 3)
     gate_up = times_plain(rows_two, w_gu)
     hidden = swiglu(gate_up, unit_part, down_cols).astype(bf16)
-    stream_two = stream_one + scatter_all(times_right(hidden, w_d).astype(bf16), 4)
+    ffn_sum, table_late = scatter_all(
+        times_right(hidden, w_d).astype(bf16), table_parts[:, :, early_cols:], 4
+    )
+    stream_two = stream_one + ffn_sum
+    table = jnp.concatenate([table_early, table_late], axis=2).reshape(wide, vocab_part)
     normed_three = wide_norm(stream_two, gains[3])
     rows_three = gather_all(normed_three.astype(bf16), 5)
 

time: 1200 us -> 1190 us (level)
  Pallas kernels: 758 us -> 736 us
  local copies, waits for them, and re-layouts: 99.5 us -> 113 us
    pallas_call x2, Pallas kernels: 112 us -> 83.4 us  [gather_all(): pl.pallas_call(functools.partial(gather_all_kernel, nd, ns), out_shape=ja...]
  transfers between devices with their start and end apart: 5 -> 5, of which waited for: 1 -> 2; matrix products, arithmetic and copies ran while one was open for 16% -> 18% of each run, Pallas kernels for 27% -> 26%
where the time goes in v5:
time: 1190 us; the launch traced here: 1180 us
  Pallas kernels  736 us (62%)
  matrix products  188 us (16%)
  local copies, waits for them, and re-layouts  113 us (9%)
  other arithmetic  50.1 us (4%)
  starting transfers between devices  39.9 us (3%)
  waiting for transfers between devices  31.4 us (3%)
  between operations  21.8 us (2%)
    pallas_call x1, Pallas kernels, front(): pl.pallas_call(functools.partial(front_kernel, nd, ns, vocab), out_shape=...  202 us
    pallas_call x1, Pallas kernels, slots_back(): pl.pallas_call(functools.partial(slots_back_kernel, nd, ns, width, units)...  185 us
    pallas_call x1, Pallas kernels, rows_back(): pl.pallas_call(functools.partial(rows_back_kernel, nd, ns, width), out_sh...  109 us
    dot_general x6, matrix products, times_right(): lax.dot_general(left, right, (((1,), (1,)), ((), ())), preferred_element_...  92.6 us
    pallas_call x2, Pallas kernels, gather_all(): pl.pallas_call(functools.partial(gather_all_kernel, nd, ns), out_shape=ja...  83.4 us
    pallas_call x3, Pallas kernels, adam_blocks(): pl.pallas_call(functools.partial(adam_kernel, rate, decay), grid=(capacit...  62.6 us
    pallas_call x1, Pallas kernels, scatter_all(): pl.pallas_call(functools.partial(scatter_all_kernel, nd, ns), out_shape=[...  56.5 us
    all_to_all x2, starting transfers between devices, swap_dp(): return lax.all_to_all(values, 'dp', split_axis=0, concat_axis=0, tiled=True)  36.2 us
  transfers between devices with their start and end apart: 5, of which 2 were waited for; matrix products, arithmetic and copies ran while one was open for 18% of the time, Pallas kernels for 26%

profile of v5, /device:TPU:0, one launch (start us, length us, event | category | flops | bytes accessed | tf_op | source)
XLA Modules:
  0.0 1180.4 jit_solution(167591104625967693)
XLA Ops:
  40.6 7.8 concatenate.44
  48.4 202.4 %shard_map.348 = (s32[8,16,128]{2,1,0:T(8,128)S(1)}, bf16[8,16,128]{2,1,0:T(8,128)(2,1)S(1)}, bf16[2560,1024]{1,0:T(8,128)(2,1)}, bf16[4,8,320,256]{3,2,1,0:T(8,...) custom-call(s32[16,128]{1,0:T(8,128)S(1)} %pad_bitcast_fusion.1.small_ref, ...), custom_call_target="tpu_custom_call" | custom-call | flops 42949672960 | bytes 6553600 | tf_op jit(solution)/shard_map/pallas_call | solution.py:839
  285.8 6.6 fusion.101
  303.4 8.4 fusion.61
  333.7 11.2 shard_map.349
  350.1 42.6 %shard_map.350 = bf16[2,2,2,4,32,2560]{5,4,3,2,1,0:T(8,128)(2,1)S(1)} custom-call(bf16[32,2560]{1,0:T(8,128)(2,1)S(1)} %multiply_convert_fusion.3.in_ref), custom_call_target="tpu_custom_call" | custom-call | tf_op jit(solution)/shard_map/pallas_call | solution.py:382
  405.5 56.5 %shard_map.351 = (f32[32,2560]{1,0:T(8,128)S(1)}, bf16[8,320,256]{2,1,0:T(8,128)(2,1)S(1)}) custom-call(bf16[2,2,2,4,32,2560]{5,4,3,2,1,0:T(8,128)(2,1)S(1)} %bitcast.229, bf16[8,320,256]{2,1,0:T(8,128)(2,1)S(1)} %slice.216.cargo_ref), custom_call_target="tpu_custom_call" | custom-call | tf_op jit(solution)/shard_map/pallas_call | solution.py:548
  462.2 40.8 %shard_map.352 = bf16[2,2,2,4,32,2560]{5,4,3,2,1,0:T(8,128)(2,1)S(1)} custom-call(bf16[32,2560]{1,0:T(8,128)(2,1)S(1)} %multiply_convert_fusion.2.in_ref), custom_call_target="tpu_custom_call" | custom-call | tf_op jit(solution)/shard_map/pallas_call | solution.py:382
  520.3 11.9 %shard_map.353 = f32[3,8,128]{2,1,0:T(8,128)} custom-call(f32[3,8,128]{2,1,0:T(8,128)} %pad_maximum_fusion.7.in_ref), custom_call_target="tpu_custom_call" | custom-call | tf_op jit(solution)/shard_map/pallas_call | solution.py:282
  534.4 11.8 convolution_convert_fusion.2
  546.2 9.2 convolution_convert_fusion.3
  555.4 185.3 %shard_map.354 = (bf16[4,32,2560]{2,1,0:T(8,128)(2,1)}, bf16[8,320,1024]{2,1,0:T(8,128)(2,1)}, bf16[2560,640]{1,0:T(8,128)(2,1)}, f32[2,2560]{1,0:T(2,128)}) custom-call(bf16[2,2,2,4,32,2560]{5,4,3,2,1,0:T(8,128)(2,1)} %bitcast.324, bf16[8,320,1024]{2,1,0:T(8,128)(2,1)} %bitcast.323, f32[32,2560]{1,0:T(8,128)} %copy-done.40, f32[32,2560]{1,0:T(8,128)} %copy-done.29, ...), custom_call_target="tpu_custom_call" | custom-call | flops 13421772800 | bytes 262144000 | tf_op jit(solution)/shard_map/pallas_call | solution.py:1026
  752.9 7.6 select_reduce_fusion
  764.1 6.9 fusion.2
  784.8 11.1 convolution_convert_fusion
  795.9 12.9 %fusion.17.in_ref = bf16[2560,1024]{1,0:T(8,128)(2,1)} fusion(bf16[2560,512]{1,0:T(8,128)(2,1)S(1)} %copy-done.32, bf16[2560,512]{1,0:T(8,128)(2,1)} %bitcast.285, bf16[2560,512]{1,0:T(8,128)(2,1)} %bitcast.286, bf16[1024,512]{1,0:T(8,128)(2,1)} %copy.236, bf16[1024,512]{1,0:T(8,128)(2,1)} %copy-done.41, bf16[1024,512]{1,0:T(8,128)(2,1)} %copy-done.74), kind=kOutput, calls=%fused_computation.27 | convolution fusion | flops 8088715264 | bytes 16252928 | tf_op jit(solution)/shard_map/dot_general | solution.py:141
  815.2 109.4 %shard_map.355 = (bf16[320,8192]{1,0:T(8,128)(2,1)}, f32[2560,1]{1,0:T(8,128)S(1)}) custom-call(bf16[2560,1024]{1,0:T(8,128)(2,1)} %fusion.17.in_ref, bf16[2560,256]{1,0:T(8,128)(2,1)S(1)} %constant_dynamic-slice_fusion.stream_ref, f32[2560,1]{1,0:T(8,128)S(1)} %broadcast_in_dim_squeeze.3.gain_ref, f32[2560,256]{1,0:T(8,128)} %fusion.104.more_ref), custom_call_target="tpu_custom_call" | custom-call | bytes 157286400 | tf_op jit(solution)/shard_map/pallas_call | solution.py:1168
  927.8 30.6 %all-to-all-start.1 = ((bf16[8,320,640]{2,1,0:T(8,128)(2,1)}), bf16[8,320,640]{2,1,0:T(8,128)(2,1)}, u32[]{:S(2)}, u32[]{:S(2)}) async-start(bf16[8,320,640]{2,1,0:T(8,128)(2,1)} %bitcast.282), calls=%async_computation.3 | async-start | bytes 6553600 | tf_op jit(solution)/shard_map/all_to_all | solution.py:170
  959.1 59.8 %multiply_reduce_fusion = (f32[]{:T(128)}, f32[320,8000]{1,0:T(8,128)}) fusion(bf16[320,8192]{1,0:T(8,128)(2,1)} %bitcast.266, bf16[320,8192]{1,0:T(8,128)(2,1)} %get-tuple-element.85, s32[8192]{0:T(1024)S(1)} %bitcast.310), kind=kOutput, calls=%fused_computation.18 | convolution fusion | flops 42018816000 | bytes 20635652 | tf_op jit(solution)/shard_map/dot_general | solution.py:141
  1018.9 29.1 %all-to-all-done.1 = bf16[8,320,640]{2,1,0:T(8,128)(2,1)} async-done(((bf16[8,320,640]{2,1,0:T(8,128)(2,1)}), bf16[8,320,640]{2,1,0:T(8,128)(2,1)}, u32[]{:S(2)}, u32[]{:S(2)}) %all-to-all-start.1) | async-done | bytes 3276832 | tf_op jit(solution)/shard_map/all_to_all | solution.py:170
  1073.6 13.4 %shard_map.356 = f32[80,128]{1,0:T(8,128)} custom-call(f32[80,128]{1,0:T(8,128)} %pad_bitcast_fusion.in_ref), custom_call_target="tpu_custom_call" | custom-call | tf_op jit(solution)/shard_map/pallas_call | solution.py:282
  1101.4 32.9 %shard_map.359 = (f32[1,5,64,8000]{3,2,1,0:T(8,128)}, f32[1,5,64,8000]{3,2,1,0:T(8,128)}, f32[1,5,64,8000]{3,2,1,0:T(8,128)}, f32[1,5,64,8000]{3,2,1,0:T(8,128)}) custom-call(f32[1]{0:T(128)} %bitcast.76.scale_ref, f32[5]{0:T(128)S(1)} %get-tuple-element.167.held_ref, f32[1,5,64,8000]{3,2,1,0:T(8,128)} %weight.5, f32[1,5,64,8000]{3,2,1,0:T(8,128)} %first.5, ...), custom_call_target="tpu_custom_call" | custom-call | tf_op jit(solution)/shard_map/pallas_call | solution.py:126
  1134.4 10.4 shard_map.358
  1152.9 19.3 %shard_map.357 = (f32[1,5,64,4352]{3,2,1,0:T(8,128)}, f32[1,5,64,4352]{3,2,1,0:T(8,128)}, f32[1,5,64,4352]{3,2,1,0:T(8,128)}, f32[1,5,64,4352]{3,2,1,0:T(8,128)}) custom-call(f32[1]{0:T(128)} %bitcast.76.scale_ref, f32[5]{0:T(128)S(1)} %get-tuple-element.167.held_ref, f32[1,5,64,4352]{3,2,1,0:T(8,128)} %weight.3, f32[1,5,64,4352]{3,2,1,0:T(8,128)} %first.3, ...), custom_call_target="tpu_custom_call" | custom-call | tf_op jit(solution)/shard_map/pallas_call | solution.py:126
  (376 shorter events, 220.7 us)
Async XLA Ops:
  48.4 202.5 %slice-start.6 = ((s8[5242880]{0:T(1024)(128)(4,1)}), s8[4194304]{0:T(1024)(128)(4,1)S(1)}, s32[]{:S(2)}) async-start(s8[5242880]{0:T(1024)(128)(4,1)} %bitcast.245), calls=%async_computation.13 | async-start | bytes 8388608
  48.4 202.5 %slice-start.7 = ((s8[5242880]{0:T(1024)(128)(4,1)}), s8[1048576]{0:T(1024)(128)(4,1)S(1)}, s32[]{:S(2)}) async-start(s8[5242880]{0:T(1024)(128)(4,1)} %bitcast.245), calls=%async_computation.14 | async-start | bytes 2097152
  256.4 249.9 %all-to-all-start = ((bf16[8,320,768]{2,1,0:T(8,128)(2,1)}), bf16[8,320,768]{2,1,0:T(8,128)(2,1)}, u32[]{:S(2)}, u32[]{:S(2)}) async-start(bf16[8,320,768]{2,1,0:T(8,128)(2,1)} %slice.218), calls=%async_computation | async-start | bytes 7864320 | tf_op jit(solution)/shard_map/all_to_all | solution.py:170
  262.1 801.3 %reduce-scatter.5.cloned.1.call-start = ((), (), s32[]{:S(2)}) async-start(), calls=%async_computation.6 | async-start | bytes 2949120 | tf_op jit(solution)/shard_map/reduce_scatter | solution.py:1491
  266.0 19.8 %copy-start.70 = (f32[1024]{0:T(1024)}, f32[1024]{0:T(1024)S(1)}, u32[]{:S(2)}) copy-start(f32[1024]{0:T(1024)S(1)} %add_rsqrt_fusion) | copy-start | bytes 12292
  267.8 18.0 %copy-start.64 = (f32[2560]{0:T(1024)}, f32[2560]{0:T(1024)S(1)}, u32[]{:S(2)}) copy-start(f32[2560]{0:T(1024)S(1)} %mul.384) | copy-start | bytes 30724
  315.7 13.8 %copy-start.12 = (f32[4,128,1024]{2,1,0:T(8,128)}, f32[4,128,1024]{2,1,0:T(8,128)S(1)}, u32[]{:S(2)}) copy-start(f32[4,128,1024]{2,1,0:T(8,128)S(1)} %copy.194) | copy-start | bytes 6291460
  349.9 112.0 %copy-start.29 = (f32[32,2560]{1,0:T(8,128)}, f32[32,2560]{1,0:T(8,128)S(1)}, u32[]{:S(2)}) copy-start(f32[32,2560]{1,0:T(8,128)S(1)} %get-tuple-element.159.one_ref) | copy-start | bytes 983044
  462.1 40.9 %copy-start.40 = (f32[32,2560]{1,0:T(8,128)}, f32[32,2560]{1,0:T(8,128)S(1)}, u32[]{:S(2)}) copy-start(f32[32,2560]{1,0:T(8,128)S(1)} %get-tuple-element.129.two_ref) | copy-start | bytes 983044
  517.8 28.3 %slice-start.12 = ((s8[5242880]{0:T(1024)(128)(4,1)}), s8[1048576]{0:T(1024)(128)(4,1)S(1)}, s32[]{:S(2)}) async-start(s8[5242880]{0:T(1024)(128)(4,1)} %bitcast.268), calls=%async_computation.19 | async-start | bytes 2097152
  534.4 11.8 %slice-start.13 = ((s8[5242880]{0:T(1024)(128)(4,1)}), s8[4194304]{0:T(1024)(128)(4,1)S(1)}, s32[]{:S(2)}) async-start(s8[5242880]{0:T(1024)(128)(4,1)} %bitcast.268), calls=%async_computation.20 | async-start | bytes 8388608
  534.4 11.8 copy-start.28
  555.4 185.4 %copy-start.47 = (bf16[128,4,128]{0,2,1:T(8,128)(2,1)S(1)}, bf16[128,4,128]{0,2,1:T(8,128)(2,1)}, u32[]{:S(2)}) copy-start(bf16[128,4,128]{0,2,1:T(8,128)(2,1)} %copy-done.46) | copy-start | bytes 393220
  777.2 288.5 %reduce-scatter.3.cloned.1.call-start = ((), (), s32[]{:S(2)}) async-start(), calls=%async_computation.5 | async-start | bytes 8847360 | tf_op jit(solution)/shard_map/reduce_scatter | solution.py:1491
  784.8 11.1 copy-start.32
  812.3 112.3 %slice-start.10 = ((s8[5242880]{0:T(1024)(128)(4,1)}), s8[4194304]{0:T(1024)(128)(4,1)S(1)}, s32[]{:S(2)}) async-start(s8[5242880]{0:T(1024)(128)(4,1)} %bitcast.262), calls=%async_computation.17 | async-start | bytes 8388608
  815.2 109.4 %slice-start.11 = ((s8[5242880]{0:T(1024)(128)(4,1)}), s8[1048576]{0:T(1024)(128)(4,1)S(1)}, s32[]{:S(2)}) async-start(s8[5242880]{0:T(1024)(128)(4,1)} %bitcast.262), calls=%async_computation.18 | async-start | bytes 2097152
  927.8 31.0 %copy-start.59 = (f32[2,2560]{1,0:T(2,128)S(1)}, f32[2,2560]{1,0:T(2,128)}, u32[]{:S(2)}) copy-start(f32[2,2560]{1,0:T(2,128)} %get-tuple-element.78) | copy-start | bytes 61444
  927.8 120.2 %all-to-all-start.1 = ((bf16[8,320,640]{2,1,0:T(8,128)(2,1)}), bf16[8,320,640]{2,1,0:T(8,128)(2,1)}, u32[]{:S(2)}, u32[]{:S(2)}) async-start(bf16[8,320,640]{2,1,0:T(8,128)(2,1)} %bitcast.282), calls=%async_computation.3 | async-start | bytes 6553600 | tf_op jit(solution)/shard_map/all_to_all | solution.py:170
  1065.6 22.2 %slice-start.16 = ((bf16[320,1536]{1,0:T(8,128)(2,1)}), bf16[320,1024]{1,0:T(8,128)(2,1)S(1)}, s32[]{:S(2)}) async-start(bf16[320,1536]{1,0:T(8,128)(2,1)} %reduce-scatter.3.cloned.1.call-done), calls=%async_computation.23 | async-start | bytes 1310720 | tf_op jit(solution)/shard_map/slice | solution.py:1513
  1090.0 56.1 %all-to-all-start.2 = ((bf16[4,320,256]{2,1,0:T(8,128)(2,1)}), bf16[4,320,256]{2,1,0:T(8,128)(2,1)S(1)}, u32[]{:S(2)}, u32[]{:S(2)}) async-start(bf16[4,320,256]{2,1,0:T(8,128)(2,1)} %reshape.546), calls=%async_computation.4 | async-start | bytes 1310720 | tf_op jit(solution)/shard_map/all_to_all | solution.py:1515
  1101.4 32.9 %copy-start.1 = (f32[1,5,64,1920]{3,2,1,0:T(8,128)S(1)}, f32[1,5,64,1920]{3,2,1,0:T(8,128)}, u32[]{:S(2)}) copy-start(f32[1,5,64,1920]{3,2,1,0:T(8,128)} %weight.4) | copy-start | bytes 7372804
  1101.4 32.9 %copy-start.4 = (f32[1,5,64,1920]{3,2,1,0:T(8,128)S(1)}, f32[1,5,64,1920]{3,2,1,0:T(8,128)}, u32[]{:S(2)}) copy-start(f32[1,5,64,1920]{3,2,1,0:T(8,128)} %first.4) | copy-start | bytes 7372804
  1134.3 10.4 copy-start.51
  (75 other events, 330.5 us)
Sparse Core Ops, SparseCore 0:
  777.3 73.9 reduce-scatter.4
  855.4 210.1 reduce-scatter.2

commit v6 on v5

--- a/solution.py
+++ b/solution.py
@@ -63,10 +63,10 @@
     column = jnp.arange(heads * KEY_DIM)
     of_head = (column % key_part) // (key_part // heads) == jnp.arange(heads)[:, None]
     grown = jnp.where(of_head[:, None, None], grown[None], 0.0)
-    scores = jnp.einsum("hbnk,bgk->hnbg", grown, key_decay, precision=FULL_PRECISION)
+    scores = jnp.einsum("hbnk,bgk->hnbg", grown, key_decay, precision=lax.Precision.HIGH)
     scores = jnp.where(allowed[None], scores.reshape(heads, slots, tokens), 0.0)
     mixed = jnp.einsum(
-        "hns,shv->nhv", scores, values.reshape(tokens, heads, VAL_DIM), precision=FULL_PRECISION
+        "hns,shv->nhv", scores, values.reshape(tokens, heads, VAL_DIM), precision=lax.Precision.HIGH
     )
     return mixed.reshape(slots, -1)
 

time: 1190 us -> 1190 us (level)
  transfers between devices with their start and end apart: 5 -> 5, of which waited for: 2 -> 1; matrix products, arithmetic and copies ran while one was open for 18% -> 18% of each run, Pallas kernels for 26% -> 25%
where the time goes in v6:
time: 1190 us; the launch traced here: 1180 us
  Pallas kernels  737 us (62%)
  matrix products  187 us (16%)
  local copies, waits for them, and re-layouts  113 us (9%)
  other arithmetic  50 us (4%)
  starting transfers between devices  40.2 us (3%)
  waiting for transfers between devices  35 us (3%)
  between operations  21.9 us (2%)
    pallas_call x1, Pallas kernels, front(): pl.pallas_call(functools.partial(front_kernel, nd, ns, vocab), out_shape=...  202 us
    pallas_call x1, Pallas kernels, slots_back(): pl.pallas_call(functools.partial(slots_back_kernel, nd, ns, width, units)...  186 us
    pallas_call x1, Pallas kernels, rows_back(): pl.pallas_call(functools.partial(rows_back_kernel, nd, ns, width), out_sh...  107 us
    dot_general x6, matrix products, times_right(): lax.dot_general(left, right, (((1,), (1,)), ((), ())), preferred_element_...  92.1 us
    pallas_call x2, Pallas kernels, gather_all(): pl.pallas_call(functools.partial(gather_all_kernel, nd, ns), out_shape=ja...  83 us
    pallas_call x3, Pallas kernels, adam_blocks(): pl.pallas_call(functools.partial(adam_kernel, rate, decay), grid=(capacit...  62.6 us
    pallas_call x1, Pallas kernels, scatter_all(): pl.pallas_call(functools.partial(scatter_all_kernel, nd, ns), out_shape=[...  55.4 us
    dot_general x5, matrix products, times_plain(): return jnp.dot(left, right, preferred_element_type=jnp.float32)  41.5 us
  transfers between devices with their start and end apart: 5, of which 1 were waited for; matrix products, arithmetic and copies ran while one was open for 18% of the time, Pallas kernels for 25%

profile of v6, /device:TPU:0, one launch (start us, length us, event | category | flops | bytes accessed | tf_op | source)
XLA Modules:
  0.0 1184.3 jit_solution(5338291935600789336)
XLA Ops:
  40.6 7.8 concatenate.44
  48.4 202.4 %shard_map.348 = (s32[8,16,128]{2,1,0:T(8,128)S(1)}, bf16[8,16,128]{2,1,0:T(8,128)(2,1)S(1)}, bf16[2560,1024]{1,0:T(8,128)(2,1)}, bf16[4,8,320,256]{3,2,1,0:T(8,...) custom-call(s32[16,128]{1,0:T(8,128)S(1)} %pad_bitcast_fusion.1.small_ref, ...), custom_call_target="tpu_custom_call" | custom-call | flops 42949672960 | bytes 6553600 | tf_op jit(solution)/shard_map/pallas_call | solution.py:839
  256.4 5.7 all-to-all-start
  275.9 6.1 fusion.21
  286.0 16.5 %fusion.101 = (f32[128,512]{1,0:T(8,128)S(1)}, f32[128,512]{1,0:T(8,128)}) fusion(bf16[4,320,8,128]{3,2,1,0:T(8,128)(2,1)} %get-tuple-element.130, s32[128]{0:T(128)S(1)} %bitcast.317, bf16[2560,1024]{1,0:T(8,128)(2,1)} %get-tuple-element.67, f32[2560]{0:T(1024)S(1)} %mul.384, f32[1024]{0:T(1024)S(1)} %add_rsqrt_fusion), kind=kOutput, calls=%fused_computation.168 | convolution fusion | flops 1017970688 | bytes 8403456 | tf_op jit(solution)/shard_map/dot_general | solution.py:137
  338.7 11.2 shard_map.349
  355.1 43.4 %shard_map.350 = bf16[2,2,2,4,32,2560]{5,4,3,2,1,0:T(8,128)(2,1)S(1)} custom-call(bf16[32,2560]{1,0:T(8,128)(2,1)S(1)} %multiply_convert_fusion.3.in_ref), custom_call_target="tpu_custom_call" | custom-call | tf_op jit(solution)/shard_map/pallas_call | solution.py:382
  411.2 55.4 %shard_map.351 = (f32[32,2560]{1,0:T(8,128)S(1)}, bf16[8,320,256]{2,1,0:T(8,128)(2,1)S(1)}) custom-call(bf16[2,2,2,4,32,2560]{5,4,3,2,1,0:T(8,128)(2,1)S(1)} %bitcast.229, bf16[8,320,256]{2,1,0:T(8,128)(2,1)S(1)} %slice.216.cargo_ref), custom_call_target="tpu_custom_call" | custom-call | tf_op jit(solution)/shard_map/pallas_call | solution.py:548
  467.0 39.7 %shard_map.352 = bf16[2,2,2,4,32,2560]{5,4,3,2,1,0:T(8,128)(2,1)S(1)} custom-call(bf16[32,2560]{1,0:T(8,128)(2,1)S(1)} %multiply_convert_fusion.2.in_ref), custom_call_target="tpu_custom_call" | custom-call | tf_op jit(solution)/shard_map/pallas_call | solution.py:382
  513.4 6.0 select_reduce_fusion.2
  524.0 13.2 %shard_map.353 = f32[3,8,128]{2,1,0:T(8,128)} custom-call(f32[3,8,128]{2,1,0:T(8,128)} %pad_maximum_fusion.7.in_ref), custom_call_target="tpu_custom_call" | custom-call | tf_op jit(solution)/shard_map/pallas_call | solution.py:282
  539.3 11.8 convolution_convert_fusion.2
  551.1 9.0 convolution_convert_fusion.3
  560.1 185.9 %shard_map.354 = (bf16[4,32,2560]{2,1,0:T(8,128)(2,1)}, bf16[8,320,1024]{2,1,0:T(8,128)(2,1)}, bf16[2560,640]{1,0:T(8,128)(2,1)}, f32[2,2560]{1,0:T(2,128)}) custom-call(bf16[2,2,2,4,32,2560]{5,4,3,2,1,0:T(8,128)(2,1)} %bitcast.324, bf16[8,320,1024]{2,1,0:T(8,128)(2,1)} %bitcast.323, f32[32,2560]{1,0:T(8,128)} %copy-done.40, f32[32,2560]{1,0:T(8,128)} %copy-done.29, ...), custom_call_target="tpu_custom_call" | custom-call | flops 13421772800 | bytes 262144000 | tf_op jit(solution)/shard_map/pallas_call | solution.py:1026
  784.2 11.3 convolution_convert_fusion
  795.6 12.9 %fusion.17.in_ref = bf16[2560,1024]{1,0:T(8,128)(2,1)} fusion(bf16[2560,512]{1,0:T(8,128)(2,1)S(1)} %copy-done.32, bf16[2560,512]{1,0:T(8,128)(2,1)} %bitcast.285, bf16[2560,512]{1,0:T(8,128)(2,1)} %bitcast.286, bf16[1024,512]{1,0:T(8,128)(2,1)} %copy.236, bf16[1024,512]{1,0:T(8,128)(2,1)} %copy-done.41, bf16[1024,512]{1,0:T(8,128)(2,1)} %copy-done.74), kind=kOutput, calls=%fused_computation.27 | convolution fusion | flops 8088715264 | bytes 16252928 | tf_op jit(solution)/shard_map/dot_general | solution.py:141
  814.9 107.0 %shard_map.355 = (bf16[320,8192]{1,0:T(8,128)(2,1)}, f32[2560,1]{1,0:T(8,128)S(1)}) custom-call(bf16[2560,1024]{1,0:T(8,128)(2,1)} %fusion.17.in_ref, bf16[2560,256]{1,0:T(8,128)(2,1)S(1)} %constant_dynamic-slice_fusion.stream_ref, f32[2560,1]{1,0:T(8,128)S(1)} %broadcast_in_dim_squeeze.3.gain_ref, f32[2560,256]{1,0:T(8,128)} %fusion.104.more_ref), custom_call_target="tpu_custom_call" | custom-call | bytes 157286400 | tf_op jit(solution)/shard_map/pallas_call | solution.py:1168
  925.1 30.7 %all-to-all-start.1 = ((bf16[8,320,640]{2,1,0:T(8,128)(2,1)}), bf16[8,320,640]{2,1,0:T(8,128)(2,1)}, u32[]{:S(2)}, u32[]{:S(2)}) async-start(bf16[8,320,640]{2,1,0:T(8,128)(2,1)} %bitcast.282), calls=%async_computation.3 | async-start | bytes 6553600 | tf_op jit(solution)/shard_map/all_to_all | solution.py:170
  956.5 59.6 %multiply_reduce_fusion = (f32[]{:T(128)}, f32[320,8000]{1,0:T(8,128)}) fusion(bf16[320,8192]{1,0:T(8,128)(2,1)} %bitcast.266, bf16[320,8192]{1,0:T(8,128)(2,1)} %get-tuple-element.85, s32[8192]{0:T(1024)S(1)} %bitcast.310), kind=kOutput, calls=%fused_computation.18 | convolution fusion | flops 42018816000 | bytes 20635652 | tf_op jit(solution)/shard_map/dot_general | solution.py:141
  1016.0 34.9 %all-to-all-done.1 = bf16[8,320,640]{2,1,0:T(8,128)(2,1)} async-done(((bf16[8,320,640]{2,1,0:T(8,128)(2,1)}), bf16[8,320,640]{2,1,0:T(8,128)(2,1)}, u32[]{:S(2)}, u32[]{:S(2)}) %all-to-all-start.1) | async-done | bytes 3276832 | tf_op jit(solution)/shard_map/all_to_all | solution.py:170
  1074.3 16.5 %shard_map.356 = f32[80,128]{1,0:T(8,128)} custom-call(f32[80,128]{1,0:T(8,128)} %pad_bitcast_fusion.in_ref), custom_call_target="tpu_custom_call" | custom-call | tf_op jit(solution)/shard_map/pallas_call | solution.py:282
  1105.2 32.9 %shard_map.359 = (f32[1,5,64,8000]{3,2,1,0:T(8,128)}, f32[1,5,64,8000]{3,2,1,0:T(8,128)}, f32[1,5,64,8000]{3,2,1,0:T(8,128)}, f32[1,5,64,8000]{3,2,1,0:T(8,128)}) custom-call(f32[1]{0:T(128)} %bitcast.76.scale_ref, f32[5]{0:T(128)S(1)} %get-tuple-element.167.held_ref, f32[1,5,64,8000]{3,2,1,0:T(8,128)} %weight.5, f32[1,5,64,8000]{3,2,1,0:T(8,128)} %first.5, ...), custom_call_target="tpu_custom_call" | custom-call | tf_op jit(solution)/shard_map/pallas_call | solution.py:126
  1138.2 10.4 shard_map.358
  1156.7 19.3 %shard_map.357 = (f32[1,5,64,4352]{3,2,1,0:T(8,128)}, f32[1,5,64,4352]{3,2,1,0:T(8,128)}, f32[1,5,64,4352]{3,2,1,0:T(8,128)}, f32[1,5,64,4352]{3,2,1,0:T(8,128)}) custom-call(f32[1]{0:T(128)} %bitcast.76.scale_ref, f32[5]{0:T(128)S(1)} %get-tuple-element.167.held_ref, f32[1,5,64,4352]{3,2,1,0:T(8,128)} %weight.3, f32[1,5,64,4352]{3,2,1,0:T(8,128)} %first.3, ...), custom_call_target="tpu_custom_call" | custom-call | tf_op jit(solution)/shard_map/pallas_call | solution.py:126
  (376 shorter events, 212.8 us)
Async XLA Ops:
  48.4 202.5 %slice-start.6 = ((s8[5242880]{0:T(1024)(128)(4,1)}), s8[4194304]{0:T(1024)(128)(4,1)S(1)}, s32[]{:S(2)}) async-start(s8[5242880]{0:T(1024)(128)(4,1)} %bitcast.245), calls=%async_computation.13 | async-start | bytes 8388608
  48.4 202.5 %slice-start.7 = ((s8[5242880]{0:T(1024)(128)(4,1)}), s8[1048576]{0:T(1024)(128)(4,1)S(1)}, s32[]{:S(2)}) async-start(s8[5242880]{0:T(1024)(128)(4,1)} %bitcast.245), calls=%async_computation.14 | async-start | bytes 2097152
  256.4 253.5 %all-to-all-start = ((bf16[8,320,768]{2,1,0:T(8,128)(2,1)}), bf16[8,320,768]{2,1,0:T(8,128)(2,1)}, u32[]{:S(2)}, u32[]{:S(2)}) async-start(bf16[8,320,768]{2,1,0:T(8,128)(2,1)} %slice.218), calls=%async_computation | async-start | bytes 7864320 | tf_op jit(solution)/shard_map/all_to_all | solution.py:170
  262.1 804.2 %reduce-scatter.5.cloned.1.call-start = ((), (), s32[]{:S(2)}) async-start(), calls=%async_computation.6 | async-start | bytes 2949120 | tf_op jit(solution)/shard_map/reduce_scatter | solution.py:1491
  266.2 19.8 %copy-start.70 = (f32[1024]{0:T(1024)}, f32[1024]{0:T(1024)S(1)}, u32[]{:S(2)}) copy-start(f32[1024]{0:T(1024)S(1)} %add_rsqrt_fusion) | copy-start | bytes 12292
  267.9 18.0 %copy-start.64 = (f32[2560]{0:T(1024)}, f32[2560]{0:T(1024)S(1)}, u32[]{:S(2)}) copy-start(f32[2560]{0:T(1024)S(1)} %mul.384) | copy-start | bytes 30724
  284.8 17.7 %copy-start.5 = (f32[8,128,512]{2,1,0:T(8,128)}, f32[8,128,512]{2,1,0:T(8,128)S(1)}, u32[]{:S(2)}) copy-start(f32[8,128,512]{2,1,0:T(8,128)S(1)} %get-tuple-element.138) | copy-start | bytes 6291460
  285.9 18.9 %copy-start.36 = (f32[128,512]{1,0:T(8,128)}, f32[128,512]{1,0:T(8,128)S(1)}, u32[]{:S(2)}) copy-start(f32[128,512]{1,0:T(8,128)S(1)} %fusion.82) | copy-start | bytes 786436
  321.2 13.3 %copy-start.12 = (f32[4,128,1024]{2,1,0:T(8,128)}, f32[4,128,1024]{2,1,0:T(8,128)S(1)}, u32[]{:S(2)}) copy-start(f32[4,128,1024]{2,1,0:T(8,128)S(1)} %copy.194) | copy-start | bytes 6291460
  354.9 111.7 %copy-start.29 = (f32[32,2560]{1,0:T(8,128)}, f32[32,2560]{1,0:T(8,128)S(1)}, u32[]{:S(2)}) copy-start(f32[32,2560]{1,0:T(8,128)S(1)} %get-tuple-element.159.one_ref) | copy-start | bytes 983044
  466.8 39.8 %copy-start.40 = (f32[32,2560]{1,0:T(8,128)}, f32[32,2560]{1,0:T(8,128)S(1)}, u32[]{:S(2)}) copy-start(f32[32,2560]{1,0:T(8,128)S(1)} %get-tuple-element.129.two_ref) | copy-start | bytes 983044
  521.5 29.6 %slice-start.12 = ((s8[5242880]{0:T(1024)(128)(4,1)}), s8[1048576]{0:T(1024)(128)(4,1)S(1)}, s32[]{:S(2)}) async-start(s8[5242880]{0:T(1024)(128)(4,1)} %bitcast.268), calls=%async_computation.19 | async-start | bytes 2097152
  539.3 11.8 slice-start.13
  539.3 11.8 copy-start.28
  560.1 185.9 %copy-start.47 = (bf16[128,4,128]{0,2,1:T(8,128)(2,1)S(1)}, bf16[128,4,128]{0,2,1:T(8,128)(2,1)}, u32[]{:S(2)}) copy-start(bf16[128,4,128]{0,2,1:T(8,128)(2,1)} %copy-done.46) | copy-start | bytes 393220
  776.6 289.7 %reduce-scatter.3.cloned.1.call-start = ((), (), s32[]{:S(2)}) async-start(), calls=%async_computation.5 | async-start | bytes 8847360 | tf_op jit(solution)/shard_map/reduce_scatter | solution.py:1491
  811.9 110.0 %slice-start.10 = ((s8[5242880]{0:T(1024)(128)(4,1)}), s8[4194304]{0:T(1024)(128)(4,1)S(1)}, s32[]{:S(2)}) async-start(s8[5242880]{0:T(1024)(128)(4,1)} %bitcast.262), calls=%async_computation.17 | async-start | bytes 8388608
  814.9 107.1 %slice-start.11 = ((s8[5242880]{0:T(1024)(128)(4,1)}), s8[1048576]{0:T(1024)(128)(4,1)S(1)}, s32[]{:S(2)}) async-start(s8[5242880]{0:T(1024)(128)(4,1)} %bitcast.262), calls=%async_computation.18 | async-start | bytes 2097152
  925.1 31.1 %copy-start.59 = (f32[2,2560]{1,0:T(2,128)S(1)}, f32[2,2560]{1,0:T(2,128)}, u32[]{:S(2)}) copy-start(f32[2,2560]{1,0:T(2,128)} %get-tuple-element.78) | copy-start | bytes 61444
  925.1 125.8 %all-to-all-start.1 = ((bf16[8,320,640]{2,1,0:T(8,128)(2,1)}), bf16[8,320,640]{2,1,0:T(8,128)(2,1)}, u32[]{:S(2)}, u32[]{:S(2)}) async-start(bf16[8,320,640]{2,1,0:T(8,128)(2,1)} %bitcast.282), calls=%async_computation.3 | async-start | bytes 6553600 | tf_op jit(solution)/shard_map/all_to_all | solution.py:170
  1066.3 25.3 %slice-start.16 = ((bf16[320,1536]{1,0:T(8,128)(2,1)}), bf16[320,1024]{1,0:T(8,128)(2,1)S(1)}, s32[]{:S(2)}) async-start(bf16[320,1536]{1,0:T(8,128)(2,1)} %reduce-scatter.3.cloned.1.call-done), calls=%async_computation.23 | async-start | bytes 1310720 | tf_op jit(solution)/shard_map/slice | solution.py:1513
  1093.9 56.1 %all-to-all-start.2 = ((bf16[4,320,256]{2,1,0:T(8,128)(2,1)}), bf16[4,320,256]{2,1,0:T(8,128)(2,1)S(1)}, u32[]{:S(2)}, u32[]{:S(2)}) async-start(bf16[4,320,256]{2,1,0:T(8,128)(2,1)} %reshape.546), calls=%async_computation.4 | async-start | bytes 1310720 | tf_op jit(solution)/shard_map/all_to_all | solution.py:1515
  1105.2 32.9 %copy-start.1 = (f32[1,5,64,1920]{3,2,1,0:T(8,128)S(1)}, f32[1,5,64,1920]{3,2,1,0:T(8,128)}, u32[]{:S(2)}) copy-start(f32[1,5,64,1920]{3,2,1,0:T(8,128)} %weight.4) | copy-start | bytes 7372804
  1105.2 32.9 %copy-start.4 = (f32[1,5,64,1920]{3,2,1,0:T(8,128)S(1)}, f32[1,5,64,1920]{3,2,1,0:T(8,128)}, u32[]{:S(2)}) copy-start(f32[1,5,64,1920]{3,2,1,0:T(8,128)} %first.4) | copy-start | bytes 7372804
  (75 other events, 319.9 us)
Sparse Core Ops, SparseCore 0:
  776.7 72.3 reduce-scatter.4
  853.3 209.7 reduce-scatter.2
